TPU v7x, 512 devices: a whole 4x4x16 slice. The times are simulated.
512 devices in a mesh: fe: 64 (over z, y), band: 8 (over x, core).
Axes of the slice: x: 4, y: 4, z: 16, core: 2. Of those that a mesh axis runs over, the one named last changes fastest.
Arguments:
- wavefunctions: float32 [128, 65536], P('band', 'fe'), may hold values from -11 to 11
- potential: float32 [65536], P('fe'), may hold values from -0.3 to 0.6
- element_matrix: float32 [512, 512], replicated, may hold values from -0.1 to 0.6, as said below
- projectors: float32 [256, 18, 512], P('fe'), may hold values from -0.078125 to 0.078125
- coupling: float32 [512, 18], replicated, may hold values from 0.1 to 0.8
- connectivity: int32 [256, 512], P('fe'), may hold values from 0 to 1279, as said below
- send_list: int32 [16384], P('fe'), may hold values from 0 to 1023, as said below
- atom_of_cell: int32 [256], P('fe'), may hold values from 0 to 15, as said below
Outputs:
- filtered: float32 [128, 65536], P('band', 'fe')
- projected: float32 [128, 128], P(None, 'band')
- correlation: float32 [128, 128], P(None, 'band')
Inputs may be any that keep to these rules, and one draw needn't show every extreme that they name: `connectivity`: entries below 1024 name owned nodes, the others ghost slots; only the last cell of each fe index names ghost slots; each ghost slot appears exactly once among one fe index's cells, each owned node once or twice. `send_list`: the 256 entries of one fe index are distinct. `atom_of_cell`: the last cell of each fe index names slots of 8 or more. `element_matrix`: Symmetric.
All inputs are finite; a program needn't handle non-finite values.
Results may differ from a plain program's by a relative error of at most 0.00016.
Values sent between devices are 32-bit elements; how exact they have to be, the bound alone decides.
No kernel may reach another device: no remote copies, remote signals or barrier semaphores. Data moves between devices by JAX's collectives and lax.ppermute only.
A program may use at most 64 MiB of HBM per device.

v0:
```python
import jax
import jax.numpy as jnp
from jax import lax
from jax.sharding import PartitionSpec as P

NPROJ = 18
DEGREE = 6
ATOM_DEV = 8


PRECISE = lax.Precision.HIGHEST
CENTER = 0.9
HALF_WIDTH = 1.1


def shifted(block, axis, distance):
    devices = range(lax.axis_size(axis))
    route = [((i - distance) % len(devices), i) for i in devices]
    return lax.ppermute(block, axis, route)


def extended_2(shard, sides, width):
    for axis, dim in sides:
        size, length = (lax.axis_size(axis), shard.shape[dim])
        up = [(i, (i + 1) % size) for i in range(size)]
        down = [(j, i) for i, j in up]
        last = lax.slice_in_dim(shard, length - width, length, axis=dim)
        initial = lax.slice_in_dim(shard, 0, width, axis=dim)
        before = lax.ppermute(last, axis, up)
        after = lax.ppermute(initial, axis, down)
        shard = jnp.concatenate([before, shard, after], axis=dim)
    return shard


def cell_products(cell_rows, proj_block, element_matrix):
    stiffness = jnp.einsum("wcn,nm->wcm", cell_rows, element_matrix, precision=PRECISE)
    partial_value = jnp.einsum("wcn,cpn->wcp", cell_rows, proj_block, precision=PRECISE)
    return (stiffness, partial_value)


def on_device(
    wavefunctions,
    potential,
    element_matrix,
    projectors,
    coupling,
    connectivity,
    send_list,
    atom_of_cell,
):
    band_rows, node_count = wavefunctions.shape
    ghost_count = send_list.shape[0]
    fe_count = lax.axis_size("fe")
    fe_index = lax.axis_index("fe")
    lower_index = (fe_index + fe_count - 1) % fe_count
    own_coupling = lax.dynamic_slice_in_dim(coupling, fe_index * ATOM_DEV, ATOM_DEV, 0)
    lower_coupling = lax.dynamic_slice_in_dim(coupling, lower_index * ATOM_DEV, ATOM_DEV, 0)
    pair_coupling = jnp.concatenate([lower_coupling, own_coupling], axis=0)
    slot_range = jnp.arange(2 * ATOM_DEV, dtype=jnp.int32)
    onehot = (atom_of_cell[:, None] == slot_range[None, :]).astype(jnp.float32)

    def hamiltonian(vectors):
        outgoing = vectors[:, send_list]
        ghosts = shifted(outgoing, "fe", -1)
        extended = jnp.concatenate([vectors, ghosts], axis=1)
        stiffness, partial_value = cell_products(
            extended[:, connectivity], projectors, element_matrix
        )
        slot_sums = jnp.einsum("wcp,ca->wap", partial_value, onehot, precision=PRECISE)
        beside_all = extended_2(slot_sums, (("fe", 1),), ATOM_DEV)
        grouped = beside_all.reshape(band_rows, 2, 2, ATOM_DEV, NPROJ)
        totals = (grouped[:, :, 0] + grouped[:, :, 1]).reshape(band_rows, 2 * ATOM_DEV, NPROJ)
        weights = totals * pair_coupling[None, :, :]
        coefficients = jnp.einsum("wap,ca->wcp", weights, onehot, precision=PRECISE)
        nonlocal_part = jnp.einsum("wcp,cpn->wcn", coefficients, projectors, precision=PRECISE)
        assembled = jnp.zeros((band_rows, node_count + ghost_count), jnp.float32)
        assembled = assembled.at[:, connectivity].add(stiffness + nonlocal_part)
        incoming = shifted(assembled[:, node_count:], "fe", 1)
        owned_sum = assembled[:, :node_count].at[:, send_list].add(incoming)
        return owned_sum + potential[None, :] * vectors

    previous = wavefunctions
    current = (hamiltonian(wavefunctions) - CENTER * wavefunctions) / HALF_WIDTH
    for degree_step in range(DEGREE - 1):
        following = 2.0 * (hamiltonian(current) - CENTER * current) / HALF_WIDTH - previous
        previous, current = (current, following)
    applied = hamiltonian(current)
    node_total = node_count * fe_count
    stacked = jnp.concatenate([applied, current], axis=0)
    panels = lax.dot_general(
        lax.all_gather(current, "band", axis=0, tiled=True),
        stacked,
        (((1,), (1,)), ((), ())),
        precision=PRECISE,
        preferred_element_type=jnp.float32,
    )
    summed = lax.psum(panels, "fe")
    projected = summed[:, :band_rows] / node_total
    correlation = summed[:, band_rows:] / node_total
    return (current, projected, correlation)


def solution(mesh):
    in_specs = (
        P("band", "fe"),
        P("fe"),
        P(),
        P("fe", None, None),
        P(),
        P("fe", None),
        P("fe"),
        P("fe"),
    )
    out_specs = (P("band", "fe"), P(None, "band"), P(None, "band"))
    return jax.shard_map(
        on_device, mesh=mesh, in_specs=in_specs, out_specs=out_specs, check_vma=False
    )
```

profile of v0, /device:TPU:2, one launch (start us, length us, event | category | flops | bytes accessed | tf_op | source)
XLA Modules:
  0.0 703.3 jit_solution(11491815225038246941)
XLA Ops:
  3.2 14.0 %collective-permute-start = (f32[16,256]{0,1:T(8,128)S(1)}, f32[16,256]{0,1:T(8,128)S(1)}, u32[]{:S(2)}, u32[]{:S(2)}) collective-permute-start(f32[16,256]{0,1:T(8,128)S(1)} %bitcast.281), channel_id=1, source_target_pairs={{8,0},{16,8},{24,16},{32,24},{40,32},{48,40},{56,48},{64,56},{72,6... | collective-permute-start | bytes 49160 | tf_op jit(solution)/shard_map/ppermute | solution.py:19
  20.3 7.6 %gather_fusion.1 = f32[2048,16]{1,0:T(8,128)} fusion(f32[16,1280]{0,1:T(8,128)S(1)} %pad_maximum_fusion, s32[2048]{0:T(1024)S(1)} %broadcast_clamp_fusion), kind=kCustom, calls=%fused_computation.1 | custom fusion | bytes 270336 | tf_op jit(solution)/shard_map/gather | solution.py:67
  32.3 7.4 %collective-permute-start.2 = (f32[16,8,18]{2,1,0:T(8,128)S(1)}, f32[16,8,18]{2,1,0:T(8,128)S(1)}, u32[]{:S(2)}, u32[]{:S(2)}) collective-permute-start(f32[16,8,18]{2,1,0:T(8,128)S(1)} %get-tuple-element.30), channel_id=1, source_target_pairs={{8,0},{16,8},{24,16},{32,24},{40,32},{48,40},{56,48},{64,56},{72,6... | collective-permute-start | bytes 27656 | tf_op jit(solution)/shard_map/ppermute | solution.py:30
  43.5 12.0 %scatter_custom_fusion = f32[16,1280]{0,1:T(8,128)S(1)} fusion(s32[2048]{0:T(1024)S(1)} %bitcast.274, f32[2048,16]{1,0:T(8,128)} %bitcast.260, f32[]{:T(128)} %constant.43.clone.1), kind=kCustom, calls=%fused_computation.129 | custom fusion | flops 32768 | bytes 82432 | tf_op jit(solution)/shard_map/scatter-add | solution.py:77
  58.3 7.8 %collective-permute-done.3 = f32[16,256]{0,1:T(8,128)S(1)} collective-permute-done((f32[16,256]{0,1:T(8,128)S(1)}, f32[16,256]{0,1:T(8,128)S(1)}, u32[]{:S(2)}, u32[]{:S(2)}) %collective-permute-start.3) | collective-permute-done | bytes 16416 | tf_op jit(solution)/shard_map/ppermute | solution.py:19
  66.1 3.6 scatter_custom_fusion.1
  71.5 3.9 collective-permute-start.4
  75.4 2.9 collective-permute-done.4
  78.4 7.6 %gather_fusion.3 = f32[2048,16]{1,0:T(8,128)} fusion(f32[16,1280]{0,1:T(8,128)S(1)} %pad_maximum_fusion.1, s32[2048]{0:T(1024)S(1)} %broadcast_clamp_fusion), kind=kCustom, calls=%fused_computation.3 | custom fusion | bytes 270336 | tf_op jit(solution)/shard_map/gather | solution.py:67
  90.1 7.2 %collective-permute-start.6 = (f32[16,8,18]{2,1,0:T(8,128)S(1)}, f32[16,8,18]{2,1,0:T(8,128)S(1)}, u32[]{:S(2)}, u32[]{:S(2)}) collective-permute-start(f32[16,8,18]{2,1,0:T(8,128)S(1)} %get-tuple-element.28), channel_id=1, source_target_pairs={{8,0},{16,8},{24,16},{32,24},{40,32},{48,40},{56,48},{64,56},{72,6... | collective-permute-start | bytes 27656 | tf_op jit(solution)/shard_map/ppermute | solution.py:30
  101.1 12.0 %scatter_custom_fusion.2 = f32[16,1280]{0,1:T(8,128)S(1)} fusion(s32[2048]{0:T(1024)S(1)} %bitcast.275, f32[2048,16]{1,0:T(8,128)} %bitcast.261, f32[]{:T(128)} %constant.43.clone.1), kind=kCustom, calls=%fused_computation.127 | custom fusion | flops 32768 | bytes 82432 | tf_op jit(solution)/shard_map/scatter-add | solution.py:77
  116.0 7.6 %collective-permute-done.7 = f32[16,256]{0,1:T(8,128)S(1)} collective-permute-done((f32[16,256]{0,1:T(8,128)S(1)}, f32[16,256]{0,1:T(8,128)S(1)}, u32[]{:S(2)}, u32[]{:S(2)}) %collective-permute-start.7) | collective-permute-done | bytes 16416 | tf_op jit(solution)/shard_map/ppermute | solution.py:19
  123.6 3.6 scatter_custom_fusion.3
  129.1 4.1 collective-permute-start.8
  133.2 2.8 collective-permute-done.8
  136.0 7.6 %gather_fusion.5 = f32[2048,16]{1,0:T(8,128)} fusion(f32[16,1280]{0,1:T(8,128)S(1)} %pad_maximum_fusion.2, s32[2048]{0:T(1024)S(1)} %broadcast_clamp_fusion), kind=kCustom, calls=%fused_computation.5 | custom fusion | bytes 270336 | tf_op jit(solution)/shard_map/gather | solution.py:67
  145.8 7.2 %collective-permute-start.10 = (f32[16,8,18]{2,1,0:T(8,128)S(1)}, f32[16,8,18]{2,1,0:T(8,128)S(1)}, u32[]{:S(2)}, u32[]{:S(2)}) collective-permute-start(f32[16,8,18]{2,1,0:T(8,128)S(1)} %get-tuple-element.26), channel_id=1, source_target_pairs={{8,0},{16,8},{24,16},{32,24},{40,32},{48,40},{56,48},{64,56},{72,6... | collective-permute-start | bytes 27656 | tf_op jit(solution)/shard_map/ppermute | solution.py:30
  155.7 6.8 collective-permute-done.9
  164.4 12.0 %scatter_custom_fusion.4 = f32[16,1280]{0,1:T(8,128)S(1)} fusion(s32[2048]{0:T(1024)S(1)} %bitcast.276, f32[2048,16]{1,0:T(8,128)} %bitcast.262, f32[]{:T(128)} %constant.43.clone.1), kind=kCustom, calls=%fused_computation.125 | custom fusion | flops 32768 | bytes 82432 | tf_op jit(solution)/shard_map/scatter-add | solution.py:77
  179.3 7.3 %collective-permute-done.11 = f32[16,256]{0,1:T(8,128)S(1)} collective-permute-done((f32[16,256]{0,1:T(8,128)S(1)}, f32[16,256]{0,1:T(8,128)S(1)}, u32[]{:S(2)}, u32[]{:S(2)}) %collective-permute-start.11) | collective-permute-done | bytes 16416 | tf_op jit(solution)/shard_map/ppermute | solution.py:19
  186.6 3.6 scatter_custom_fusion.5
  194.0 4.9 collective-permute-done.12
  199.0 7.6 %gather_fusion.7 = f32[2048,16]{1,0:T(8,128)} fusion(f32[16,1280]{0,1:T(8,128)S(1)} %pad_maximum_fusion.3, s32[2048]{0:T(1024)S(1)} %broadcast_clamp_fusion), kind=kCustom, calls=%fused_computation.7 | custom fusion | bytes 270336 | tf_op jit(solution)/shard_map/gather | solution.py:67
  210.7 7.2 %collective-permute-start.14 = (f32[16,8,18]{2,1,0:T(8,128)S(1)}, f32[16,8,18]{2,1,0:T(8,128)S(1)}, u32[]{:S(2)}, u32[]{:S(2)}) collective-permute-start(f32[16,8,18]{2,1,0:T(8,128)S(1)} %get-tuple-element.24), channel_id=1, source_target_pairs={{8,0},{16,8},{24,16},{32,24},{40,32},{48,40},{56,48},{64,56},{72,6... | collective-permute-start | bytes 27656 | tf_op jit(solution)/shard_map/ppermute | solution.py:30
  221.7 12.0 %scatter_custom_fusion.6 = f32[16,1280]{0,1:T(8,128)S(1)} fusion(s32[2048]{0:T(1024)S(1)} %bitcast.277, f32[2048,16]{1,0:T(8,128)} %bitcast.263, f32[]{:T(128)} %constant.43.clone.1), kind=kCustom, calls=%fused_computation.123 | custom fusion | flops 32768 | bytes 82432 | tf_op jit(solution)/shard_map/scatter-add | solution.py:77
  235.8 8.5 %collective-permute-done.15 = f32[16,256]{0,1:T(8,128)} collective-permute-done((f32[16,256]{0,1:T(8,128)S(1)}, f32[16,256]{0,1:T(8,128)}, u32[]{:S(2)}, u32[]{:S(2)}) %collective-permute-start.15) | collective-permute-done | bytes 16416 | tf_op jit(solution)/shard_map/ppermute | solution.py:19
  244.3 2.5 scatter_custom_fusion.7
  247.7 3.9 collective-permute-start.16
  251.6 2.9 collective-permute-done.16
  254.6 7.6 %gather_fusion.9 = f32[2048,16]{1,0:T(8,128)} fusion(f32[16,1280]{0,1:T(8,128)S(1)} %pad_maximum_fusion.4, s32[2048]{0:T(1024)S(1)} %broadcast_clamp_fusion), kind=kCustom, calls=%fused_computation.9 | custom fusion | bytes 270336 | tf_op jit(solution)/shard_map/gather | solution.py:67
  266.3 7.5 %collective-permute-start.18 = (f32[16,8,18]{2,1,0:T(8,128)S(1)}, f32[16,8,18]{2,1,0:T(8,128)S(1)}, u32[]{:S(2)}, u32[]{:S(2)}) collective-permute-start(f32[16,8,18]{2,1,0:T(8,128)S(1)} %get-tuple-element.22), channel_id=1, source_target_pairs={{8,0},{16,8},{24,16},{32,24},{40,32},{48,40},{56,48},{64,56},{72,6... | collective-permute-start | bytes 27656 | tf_op jit(solution)/shard_map/ppermute | solution.py:30
  277.3 12.0 %scatter_custom_fusion.8 = f32[16,1280]{0,1:T(8,128)S(1)} fusion(s32[2048]{0:T(1024)S(1)} %bitcast.278, f32[2048,16]{1,0:T(8,128)} %bitcast.264, f32[]{:T(128)} %constant.43.clone.1), kind=kCustom, calls=%fused_computation.121 | custom fusion | flops 32768 | bytes 82432 | tf_op jit(solution)/shard_map/scatter-add | solution.py:77
  291.4 8.5 %collective-permute-done.19 = f32[16,256]{0,1:T(8,128)} collective-permute-done((f32[16,256]{0,1:T(8,128)S(1)}, f32[16,256]{0,1:T(8,128)}, u32[]{:S(2)}, u32[]{:S(2)}) %collective-permute-start.19) | collective-permute-done | bytes 16416 | tf_op jit(solution)/shard_map/ppermute | solution.py:19
  299.9 2.5 scatter_custom_fusion.9
  303.3 3.9 collective-permute-start.20
  307.2 2.9 collective-permute-done.20
  310.2 7.6 %gather_fusion.11 = f32[2048,16]{1,0:T(8,128)} fusion(f32[16,1280]{0,1:T(8,128)S(1)} %pad_maximum_fusion.5, s32[2048]{0:T(1024)S(1)} %broadcast_clamp_fusion), kind=kCustom, calls=%fused_computation.11 | custom fusion | bytes 270336 | tf_op jit(solution)/shard_map/gather | solution.py:67
  321.9 7.2 %collective-permute-start.22 = (f32[16,8,18]{2,1,0:T(8,128)S(1)}, f32[16,8,18]{2,1,0:T(8,128)S(1)}, u32[]{:S(2)}, u32[]{:S(2)}) collective-permute-start(f32[16,8,18]{2,1,0:T(8,128)S(1)} %get-tuple-element.20), channel_id=1, source_target_pairs={{8,0},{16,8},{24,16},{32,24},{40,32},{48,40},{56,48},{64,56},{72,6... | collective-permute-start | bytes 27656 | tf_op jit(solution)/shard_map/ppermute | solution.py:30
  332.9 12.0 %scatter_custom_fusion.10 = f32[16,1280]{0,1:T(8,128)S(1)} fusion(s32[2048]{0:T(1024)S(1)} %bitcast.279, f32[2048,16]{1,0:T(8,128)} %bitcast.265, f32[]{:T(128)} %constant.43.clone.1), kind=kCustom, calls=%fused_computation.119 | custom fusion | flops 32768 | bytes 82432 | tf_op jit(solution)/shard_map/scatter-add | solution.py:77
  347.8 7.6 %collective-permute-done.23 = f32[16,256]{0,1:T(8,128)S(1)} collective-permute-done((f32[16,256]{0,1:T(8,128)S(1)}, f32[16,256]{0,1:T(8,128)S(1)}, u32[]{:S(2)}, u32[]{:S(2)}) %collective-permute-start.23) | collective-permute-done | bytes 16416 | tf_op jit(solution)/shard_map/ppermute | solution.py:19
  355.4 3.6 scatter_custom_fusion.11
  361.0 3.9 collective-permute-start.24
  365.0 13.2 %all_gather.3 = f32[128,1024]{1,0:T(8,128)S(1)} all-gather(f32[16,1024]{1,0:T(8,128)S(1)} %copy.211), channel_id=1, replica_groups=mesh['fe'=64,'band'=8] {'band'}, dimensions={0}, use_global_device_ids=true | all-gather | bytes 589824 | tf_op jit(solution)/shard_map/all_gather | solution.py:91
  378.2 7.6 %gather_fusion.13 = f32[2048,16]{1,0:T(8,128)} fusion(f32[16,1280]{0,1:T(8,128)S(1)} %pad_maximum_fusion.6, s32[2048]{0:T(1024)S(1)} %broadcast_clamp_fusion), kind=kCustom, calls=%fused_computation.13 | custom fusion | bytes 270336 | tf_op jit(solution)/shard_map/gather | solution.py:67
  389.9 7.5 %collective-permute-start.26 = (f32[16,8,18]{2,1,0:T(8,128)S(1)}, f32[16,8,18]{2,1,0:T(8,128)S(1)}, u32[]{:S(2)}, u32[]{:S(2)}) collective-permute-start(f32[16,8,18]{2,1,0:T(8,128)S(1)} %get-tuple-element.18), channel_id=1, source_target_pairs={{8,0},{16,8},{24,16},{32,24},{40,32},{48,40},{56,48},{64,56},{72,6... | collective-permute-start | bytes 27656 | tf_op jit(solution)/shard_map/ppermute | solution.py:30
  400.9 12.0 %scatter_custom_fusion.12 = f32[16,1280]{0,1:T(8,128)S(1)} fusion(s32[2048]{0:T(1024)S(1)} %bitcast.280, f32[2048,16]{1,0:T(8,128)} %bitcast.259, f32[]{:T(128)} %constant.43.clone.1), kind=kCustom, calls=%fused_computation.117 | custom fusion | flops 32768 | bytes 82432 | tf_op jit(solution)/shard_map/scatter-add | solution.py:77
  415.0 8.4 %collective-permute-done.27 = f32[16,256]{0,1:T(8,128)S(1)} collective-permute-done((f32[16,256]{0,1:T(8,128)S(1)}, f32[16,256]{0,1:T(8,128)S(1)}, u32[]{:S(2)}, u32[]{:S(2)}) %collective-permute-start.27) | collective-permute-done | bytes 16416 | tf_op jit(solution)/shard_map/ppermute | solution.py:19
  426.3 275.9 %psum.7 = f32[128,32]{0,1:T(8,128)S(1)} all-reduce(f32[128,32]{0,1:T(8,128)S(1)} %fusion.84), channel_id=1, replica_groups=mesh['fe'=64,'band'=8] {'fe'}, use_global_device_ids=true, to_apply=%region_14.15 | all-reduce | flops 4096 | bytes 32768 | tf_op jit(solution)/shard_map/psum | solution.py:97
  (163 shorter events, 92.0 us)
Async XLA Ops:
  0.6 39.2 %copy-start = (f32[512,512]{1,0:T(8,128)S(1)}, f32[512,512]{1,0:T(8,128)}, u32[]{:S(2)}) copy-start(f32[512,512]{1,0:T(8,128)} %param.10) | copy-start | bytes 3145732
  2.5 14.8 %copy-start.8 = (s32[4,512]{1,0:T(4,128)S(1)}, s32[4,512]{1,0:T(4,128)}, u32[]{:S(2)}) copy-start(s32[4,512]{1,0:T(4,128)} %param.13) | copy-start | bytes 24580
  3.2 14.1 %copy-start.4 = (f32[16,1024]{1,0:T(8,128)S(1)}, f32[16,1024]{1,0:T(8,128)}, u32[]{:S(2)}) copy-start(f32[16,1024]{1,0:T(8,128)} %param.8) | copy-start | bytes 196612
  3.2 17.0 %collective-permute-start = (f32[16,256]{0,1:T(8,128)S(1)}, f32[16,256]{0,1:T(8,128)S(1)}, u32[]{:S(2)}, u32[]{:S(2)}) collective-permute-start(f32[16,256]{0,1:T(8,128)S(1)} %bitcast.281), channel_id=1, source_target_pairs={{8,0},{16,8},{24,16},{32,24},{40,32},{48,40},{56,48},{64,56},{72,6... | collective-permute-start | bytes 49160 | tf_op jit(solution)/shard_map/ppermute | solution.py:19
  17.3 0.7 copy-start.5
  17.9 0.8 copy-start.7
  27.8 1.6 copy-start.1
  29.4 0.7 copy-start.6
  30.4 10.1 %collective-permute-start.1 = (f32[16,8,18]{2,1,0:T(8,128)S(1)}, f32[16,8,18]{2,1,0:T(8,128)S(1)}, u32[]{:S(2)}, u32[]{:S(2)}) collective-permute-start(f32[16,8,18]{2,1,0:T(8,128)S(1)} %get-tuple-element.29), channel_id=1, source_target_pairs={{0,8},{8,16},{16,24},{24,32},{32,40},{40,48},{48,56},{56,64},{64,7... | collective-permute-start | bytes 27656 | tf_op jit(solution)/shard_map/ppermute | solution.py:29
  32.3 9.3 %collective-permute-start.2 = (f32[16,8,18]{2,1,0:T(8,128)S(1)}, f32[16,8,18]{2,1,0:T(8,128)S(1)}, u32[]{:S(2)}, u32[]{:S(2)}) collective-permute-start(f32[16,8,18]{2,1,0:T(8,128)S(1)} %get-tuple-element.30), channel_id=1, source_target_pairs={{8,0},{16,8},{24,16},{32,24},{40,32},{48,40},{56,48},{64,56},{72,6... | collective-permute-start | bytes 27656 | tf_op jit(solution)/shard_map/ppermute | solution.py:30
  55.5 10.5 %collective-permute-start.3 = (f32[16,256]{0,1:T(8,128)S(1)}, f32[16,256]{0,1:T(8,128)S(1)}, u32[]{:S(2)}, u32[]{:S(2)}) collective-permute-start(f32[16,256]{0,1:T(8,128)S(1)} %slice.209), channel_id=1, source_target_pairs={{504,0},{0,8},{8,16},{16,24},{24,32},{32,40},{40,48},{48,56},{56,6... | collective-permute-start | bytes 49160 | tf_op jit(solution)/shard_map/ppermute | solution.py:19
  58.3 11.4 %copy-start.2 = (f32[16,1024]{0,1:T(8,128)S(1)}, f32[16,1024]{0,1:T(8,128)}, u32[]{:S(2)}) copy-start(f32[16,1024]{0,1:T(8,128)} %copy.164) | copy-start | bytes 196612
  71.5 6.9 collective-permute-start.4
  88.2 9.9 %collective-permute-start.5 = (f32[16,8,18]{2,1,0:T(8,128)S(1)}, f32[16,8,18]{2,1,0:T(8,128)S(1)}, u32[]{:S(2)}, u32[]{:S(2)}) collective-permute-start(f32[16,8,18]{2,1,0:T(8,128)S(1)} %get-tuple-element.27), channel_id=1, source_target_pairs={{0,8},{8,16},{16,24},{24,32},{32,40},{40,48},{48,56},{56,64},{64,7... | collective-permute-start | bytes 27656 | tf_op jit(solution)/shard_map/ppermute | solution.py:29
  90.1 9.1 %collective-permute-start.6 = (f32[16,8,18]{2,1,0:T(8,128)S(1)}, f32[16,8,18]{2,1,0:T(8,128)S(1)}, u32[]{:S(2)}, u32[]{:S(2)}) collective-permute-start(f32[16,8,18]{2,1,0:T(8,128)S(1)} %get-tuple-element.28), channel_id=1, source_target_pairs={{8,0},{16,8},{24,16},{32,24},{40,32},{48,40},{56,48},{64,56},{72,6... | collective-permute-start | bytes 27656 | tf_op jit(solution)/shard_map/ppermute | solution.py:30
  113.1 10.5 %collective-permute-start.7 = (f32[16,256]{0,1:T(8,128)S(1)}, f32[16,256]{0,1:T(8,128)S(1)}, u32[]{:S(2)}, u32[]{:S(2)}) collective-permute-start(f32[16,256]{0,1:T(8,128)S(1)} %slice.215), channel_id=1, source_target_pairs={{504,0},{0,8},{8,16},{16,24},{24,32},{32,40},{40,48},{48,56},{56,6... | collective-permute-start | bytes 49160 | tf_op jit(solution)/shard_map/ppermute | solution.py:19
  129.1 6.9 collective-permute-start.8
  145.8 9.9 %collective-permute-start.10 = (f32[16,8,18]{2,1,0:T(8,128)S(1)}, f32[16,8,18]{2,1,0:T(8,128)S(1)}, u32[]{:S(2)}, u32[]{:S(2)}) collective-permute-start(f32[16,8,18]{2,1,0:T(8,128)S(1)} %get-tuple-element.26), channel_id=1, source_target_pairs={{8,0},{16,8},{24,16},{32,24},{40,32},{48,40},{56,48},{64,56},{72,6... | collective-permute-start | bytes 27656 | tf_op jit(solution)/shard_map/ppermute | solution.py:30
  153.0 9.5 %collective-permute-start.9 = (f32[16,8,18]{2,1,0:T(8,128)S(1)}, f32[16,8,18]{2,1,0:T(8,128)S(1)}, u32[]{:S(2)}, u32[]{:S(2)}) collective-permute-start(f32[16,8,18]{2,1,0:T(8,128)S(1)} %get-tuple-element.25), channel_id=1, source_target_pairs={{0,8},{8,16},{16,24},{24,32},{32,40},{40,48},{48,56},{56,64},{64,7... | collective-permute-start | bytes 27656 | tf_op jit(solution)/shard_map/ppermute | solution.py:29
  176.4 10.2 %collective-permute-start.11 = (f32[16,256]{0,1:T(8,128)S(1)}, f32[16,256]{0,1:T(8,128)S(1)}, u32[]{:S(2)}, u32[]{:S(2)}) collective-permute-start(f32[16,256]{0,1:T(8,128)S(1)} %slice.221), channel_id=1, source_target_pairs={{504,0},{0,8},{8,16},{16,24},{24,32},{32,40},{40,48},{48,56},{56,6... | collective-permute-start | bytes 49160 | tf_op jit(solution)/shard_map/ppermute | solution.py:19
  192.1 6.9 collective-permute-start.12
  208.7 9.9 %collective-permute-start.13 = (f32[16,8,18]{2,1,0:T(8,128)S(1)}, f32[16,8,18]{2,1,0:T(8,128)S(1)}, u32[]{:S(2)}, u32[]{:S(2)}) collective-permute-start(f32[16,8,18]{2,1,0:T(8,128)S(1)} %get-tuple-element.23), channel_id=1, source_target_pairs={{0,8},{8,16},{16,24},{24,32},{32,40},{40,48},{48,56},{56,64},{64,7... | collective-permute-start | bytes 27656 | tf_op jit(solution)/shard_map/ppermute | solution.py:29
  210.7 9.1 %collective-permute-start.14 = (f32[16,8,18]{2,1,0:T(8,128)S(1)}, f32[16,8,18]{2,1,0:T(8,128)S(1)}, u32[]{:S(2)}, u32[]{:S(2)}) collective-permute-start(f32[16,8,18]{2,1,0:T(8,128)S(1)} %get-tuple-element.24), channel_id=1, source_target_pairs={{8,0},{16,8},{24,16},{32,24},{40,32},{48,40},{56,48},{64,56},{72,6... | collective-permute-start | bytes 27656 | tf_op jit(solution)/shard_map/ppermute | solution.py:30
  233.7 10.6 %collective-permute-start.15 = (f32[16,256]{0,1:T(8,128)S(1)}, f32[16,256]{0,1:T(8,128)}, u32[]{:S(2)}, u32[]{:S(2)}) collective-permute-start(f32[16,256]{0,1:T(8,128)S(1)} %slice.227), channel_id=1, source_target_pairs={{504,0},{0,8},{8,16},{16,24},{24,32},{32,40},{40,48},{48,56},{56,6... | collective-permute-start | bytes 49160 | tf_op jit(solution)/shard_map/ppermute | solution.py:19
  247.7 6.9 collective-permute-start.16
  264.3 10.1 %collective-permute-start.17 = (f32[16,8,18]{2,1,0:T(8,128)S(1)}, f32[16,8,18]{2,1,0:T(8,128)S(1)}, u32[]{:S(2)}, u32[]{:S(2)}) collective-permute-start(f32[16,8,18]{2,1,0:T(8,128)S(1)} %get-tuple-element.21), channel_id=1, source_target_pairs={{0,8},{8,16},{16,24},{24,32},{32,40},{40,48},{48,56},{56,64},{64,7... | collective-permute-start | bytes 27656 | tf_op jit(solution)/shard_map/ppermute | solution.py:29
  266.3 9.1 %collective-permute-start.18 = (f32[16,8,18]{2,1,0:T(8,128)S(1)}, f32[16,8,18]{2,1,0:T(8,128)S(1)}, u32[]{:S(2)}, u32[]{:S(2)}) collective-permute-start(f32[16,8,18]{2,1,0:T(8,128)S(1)} %get-tuple-element.22), channel_id=1, source_target_pairs={{8,0},{16,8},{24,16},{32,24},{40,32},{48,40},{56,48},{64,56},{72,6... | collective-permute-start | bytes 27656 | tf_op jit(solution)/shard_map/ppermute | solution.py:30
  289.3 10.6 %collective-permute-start.19 = (f32[16,256]{0,1:T(8,128)S(1)}, f32[16,256]{0,1:T(8,128)}, u32[]{:S(2)}, u32[]{:S(2)}) collective-permute-start(f32[16,256]{0,1:T(8,128)S(1)} %slice.233), channel_id=1, source_target_pairs={{504,0},{0,8},{8,16},{16,24},{24,32},{32,40},{40,48},{48,56},{56,6... | collective-permute-start | bytes 49160 | tf_op jit(solution)/shard_map/ppermute | solution.py:19
  303.3 6.9 collective-permute-start.20
  319.9 9.9 %collective-permute-start.21 = (f32[16,8,18]{2,1,0:T(8,128)S(1)}, f32[16,8,18]{2,1,0:T(8,128)S(1)}, u32[]{:S(2)}, u32[]{:S(2)}) collective-permute-start(f32[16,8,18]{2,1,0:T(8,128)S(1)} %get-tuple-element.19), channel_id=1, source_target_pairs={{0,8},{8,16},{16,24},{24,32},{32,40},{40,48},{48,56},{56,64},{64,7... | collective-permute-start | bytes 27656 | tf_op jit(solution)/shard_map/ppermute | solution.py:29
  321.9 9.1 %collective-permute-start.22 = (f32[16,8,18]{2,1,0:T(8,128)S(1)}, f32[16,8,18]{2,1,0:T(8,128)S(1)}, u32[]{:S(2)}, u32[]{:S(2)}) collective-permute-start(f32[16,8,18]{2,1,0:T(8,128)S(1)} %get-tuple-element.20), channel_id=1, source_target_pairs={{8,0},{16,8},{24,16},{32,24},{40,32},{48,40},{56,48},{64,56},{72,6... | collective-permute-start | bytes 27656 | tf_op jit(solution)/shard_map/ppermute | solution.py:30
  344.9 10.5 %collective-permute-start.23 = (f32[16,256]{0,1:T(8,128)S(1)}, f32[16,256]{0,1:T(8,128)S(1)}, u32[]{:S(2)}, u32[]{:S(2)}) collective-permute-start(f32[16,256]{0,1:T(8,128)S(1)} %slice.239), channel_id=1, source_target_pairs={{504,0},{0,8},{8,16},{16,24},{24,32},{32,40},{40,48},{48,56},{56,6... | collective-permute-start | bytes 49160 | tf_op jit(solution)/shard_map/ppermute | solution.py:19
  361.0 64.7 %copy-start.3 = (f32[16,1024]{1,0:T(8,128)}, f32[16,1024]{1,0:T(8,128)S(1)}, u32[]{:S(2)}) copy-start(f32[16,1024]{1,0:T(8,128)S(1)} %copy.211) | copy-start | bytes 196612
  361.0 17.1 %collective-permute-start.24 = (f32[16,256]{0,1:T(8,128)S(1)}, f32[16,256]{0,1:T(8,128)S(1)}, u32[]{:S(2)}, u32[]{:S(2)}) collective-permute-start(f32[16,256]{0,1:T(8,128)S(1)} %bitcast.282), channel_id=1, source_target_pairs={{8,0},{16,8},{24,16},{32,24},{40,32},{48,40},{56,48},{64,56},{72,6... | collective-permute-start | bytes 49160 | tf_op jit(solution)/shard_map/ppermute | solution.py:19
  388.0 10.2 %collective-permute-start.25 = (f32[16,8,18]{2,1,0:T(8,128)S(1)}, f32[16,8,18]{2,1,0:T(8,128)S(1)}, u32[]{:S(2)}, u32[]{:S(2)}) collective-permute-start(f32[16,8,18]{2,1,0:T(8,128)S(1)} %get-tuple-element.17), channel_id=1, source_target_pairs={{0,8},{8,16},{16,24},{24,32},{32,40},{40,48},{48,56},{56,64},{64,7... | collective-permute-start | bytes 27656 | tf_op jit(solution)/shard_map/ppermute | solution.py:29
  389.9 9.1 %collective-permute-start.26 = (f32[16,8,18]{2,1,0:T(8,128)S(1)}, f32[16,8,18]{2,1,0:T(8,128)S(1)}, u32[]{:S(2)}, u32[]{:S(2)}) collective-permute-start(f32[16,8,18]{2,1,0:T(8,128)S(1)} %get-tuple-element.18), channel_id=1, source_target_pairs={{8,0},{16,8},{24,16},{32,24},{40,32},{48,40},{56,48},{64,56},{72,6... | collective-permute-start | bytes 27656 | tf_op jit(solution)/shard_map/ppermute | solution.py:30
  412.9 10.5 %collective-permute-start.27 = (f32[16,256]{0,1:T(8,128)S(1)}, f32[16,256]{0,1:T(8,128)S(1)}, u32[]{:S(2)}, u32[]{:S(2)}) collective-permute-start(f32[16,256]{0,1:T(8,128)S(1)} %slice.245), channel_id=1, source_target_pairs={{504,0},{0,8},{8,16},{16,24},{24,32},{32,40},{40,48},{48,56},{56,6... | collective-permute-start | bytes 49160 | tf_op jit(solution)/shard_map/ppermute | solution.py:19
where the time goes:
time: 713 us; the launch traced here: 703 us
  blocking collectives  289 us (41%)
  other arithmetic  117 us (16%)
  starting transfers between devices  114 us (16%)
  waiting for transfers between devices  85.2 us (12%)
  local copies, waits for them, and re-layouts  82.6 us (12%)
  matrix products  14.1 us (2%)
    psum x1, blocking collectives, on_device(): summed = lax.psum(panels, 'fe')  276 us
    scatter-add x7, other arithmetic, hamiltonian(): assembled = assembled.at[:, connectivity].add(stiffness + nonlocal_part)  83.9 us
    ppermute x14, waiting for transfers between devices, shifted(): return lax.ppermute(block, axis, route)  72.1 us
    gather x14, local copies, waits for them, and re-layouts, hamiltonian(): extended[:, connectivity]  63.6 us
    ppermute x7, starting transfers between devices, extended_2(): after = lax.ppermute(initial, axis, down)  51.4 us
    ppermute x14, starting transfers between devices, shifted(): return lax.ppermute(block, axis, route)  49.1 us
    scatter-add x7, other arithmetic, hamiltonian(): owned_sum = assembled[:, :node_count].at[:, send_list].add(incoming)  21.5 us
  transfers between devices with their start and end apart: 28, of which 19 were waited for; matrix products, arithmetic and copies ran while one was open for 2% of the time, Pallas kernels for 0%

commit v1 on v0

v1 whole, which is shorter than its diff:
```python
import functools

import jax
import jax.numpy as jnp
from jax import lax
from jax.experimental import pallas as pl
from jax.experimental.pallas import tpu as pltpu
from jax.sharding import PartitionSpec as P

NPROJ = 18
ATOM_DEV = 8
DEGREE = 6
CENTER = 0.9
HALF_WIDTH = 1.1
BANDS = 16
NODES = 1024
NPC = 512
GHOST = 256
LANES = 128
SLOT = 32
F32 = jnp.float32
BF16 = jnp.bfloat16


def dot(a, b):
    return lax.dot_general(a, b, (((1,), (0,)), ((), ())), preferred_element_type=F32)


def dot_nt(a, b):
    return lax.dot_general(a, b, (((1,), (1,)), ((), ())), preferred_element_type=F32)


def split2(x):
    high = x.astype(BF16)
    return high, (x - high.astype(F32)).astype(BF16)


def split3(x):
    high = x.astype(BF16)
    rest = x - high.astype(F32)
    mid = rest.astype(BF16)
    return high, mid, (rest - mid.astype(F32)).astype(BF16)


def product(x_high, x_low, w_high, w_low):
    rows = x_high.shape[0]
    both = dot(jnp.concatenate([x_high, x_low], axis=0), w_high)
    return both[:rows] + both[rows:] + dot(x_high, w_low)


def blocks_of(x):
    return [x[:, i : i + LANES] for i in range(0, x.shape[1], LANES)]


def pick(sources, index, first=0):
    rows = sources[0].shape[0]
    index = jnp.broadcast_to(index, (rows, LANES))
    lane = index & (LANES - 1)
    block = index >> 7
    total = jnp.zeros((rows, LANES), F32)
    for k, source in enumerate(sources):
        value = jnp.take_along_axis(source, lane, axis=1, mode="promise_in_bounds")
        total = jnp.where(block == first + k, value, total)
    return total


def pick_row(sources, index, first=0):
    return jnp.concatenate([pick(sources, i, first) for i in blocks_of(index)], axis=1)


def column(row):
    return jnp.broadcast_to(row, (LANES, row.shape[1])).T


def lane_iota(rows, lanes):
    return lax.broadcasted_iota(jnp.int32, (rows, lanes), 1)


def row_iota(rows, lanes):
    return lax.broadcasted_iota(jnp.int32, (rows, lanes), 0)


def gathered(vectors, conn_ref, send_ref):
    sources = blocks_of(vectors)
    cells = [pick_row(sources, conn_ref[c : c + 1, :]) for c in range(4)]
    return cells, pick_row(sources, send_ref[...])


def padded_projectors(cell):
    return jnp.concatenate([cell, jnp.zeros((SLOT - NPROJ, NPC), F32)], axis=0)


def inner_partials(cells, inner_t_high, inner_t_low):
    x_high, x_low = split2(jnp.concatenate(cells[:3], axis=0))
    wide = product(x_high, x_low, inner_t_high, inner_t_low)
    which = lane_iota(BANDS, LANES) >> 5
    total = jnp.zeros((BANDS, LANES), F32)
    for c in range(3):
        total = jnp.where(which == c, wide[c * BANDS : (c + 1) * BANDS], total)
    return total


def first_kernel(v_ref, conn_ref, send_ref, atom_ref, proj_ref, x_ref, g_ref, up_ref, down_ref, inner_ref):
    cells, ghosts = gathered(v_ref[...], conn_ref, send_ref)
    for c in range(4):
        x_ref[c * BANDS : (c + 1) * BANDS, :] = cells[c]
    g_ref[...] = ghosts
    stacked = jnp.concatenate([padded_projectors(proj_ref[c]) for c in range(3)] + [jnp.zeros((SLOT, NPC), F32)], axis=0)
    inner_high, inner_low = split2(stacked.T)
    inner_ref[0] = inner_high
    inner_ref[1] = inner_low
    partials = inner_partials(cells, inner_high, inner_low)
    which = lane_iota(1, LANES) >> 5
    atoms = jnp.zeros((1, LANES), F32)
    for c in range(4):
        atoms = jnp.where(which == c, atom_ref[c].astype(F32), atoms)
    edge = conn_ref[3:4, :]
    names = column(edge.astype(F32))
    position = row_iota(NPC, LANES).astype(F32)
    inverse = []
    for k in range(GHOST // LANES):
        slot = (lane_iota(NPC, LANES) + (NODES + k * LANES)).astype(F32)
        inverse.append(jnp.max(jnp.where(names == slot, position, -1.0), axis=0, keepdims=True))
    up_ref[...] = jnp.zeros_like(up_ref)
    up_ref[0:BANDS, 0:NPC] = cells[3]
    up_ref[0:BANDS, NPC:] = partials
    up_ref[16 : 16 + NPROJ, 0:NPC] = proj_ref[3]
    up_ref[40:41, 0:NPC] = edge.astype(F32)
    up_ref[41:42, 0:GHOST] = jnp.concatenate(inverse, axis=1)
    up_ref[42:43, 0:LANES] = atoms
    down_ref[...] = jnp.zeros_like(down_ref)
    down_ref[0:BANDS, 0:GHOST] = ghosts
    down_ref[0:BANDS, GHOST:] = partials
    down_ref[16:17, 0:LANES] = atoms


def local_kernel(conn_ref, send_ref, element_ref, e_ref, maps_ref):
    high, low = split2(element_ref[...])
    e_ref[0] = high
    e_ref[1] = low
    least = [jnp.full((1, LANES), 4.0 * NPC, F32)] * (NODES // LANES)
    most = [jnp.full((1, LANES), -1.0, F32)] * (NODES // LANES)
    position = row_iota(NPC, LANES).astype(F32)
    node = lane_iota(NPC, LANES).astype(F32)
    for c in range(4):
        names = column(conn_ref[c : c + 1, :].astype(F32))
        place = position + float(c * NPC)
        for k in range(NODES // LANES):
            same = names == node + float(k * LANES)
            least[k] = jnp.minimum(least[k], jnp.min(jnp.where(same, place, 4.0 * NPC), axis=0, keepdims=True))
            most[k] = jnp.maximum(most[k], jnp.max(jnp.where(same, place, -1.0), axis=0, keepdims=True))
    names = column(send_ref[...].astype(F32))
    maps_ref[...] = jnp.zeros_like(maps_ref)
    for k in range(NODES // LANES):
        here = slice(k * LANES, (k + 1) * LANES)
        maps_ref[0:1, here] = least[k].astype(jnp.int32)
        maps_ref[1:2, here] = jnp.where(most[k] > least[k], most[k], -1.0).astype(jnp.int32)
        same = names == node[:GHOST] + float(k * LANES)
        maps_ref[2:3, here] = jnp.max(jnp.where(same, position[:GHOST], -1.0), axis=0, keepdims=True).astype(jnp.int32)


def joined_kernel(up_ref, down_ref, maps_ref, atom_ref, place_ref, proj_ref, coupling_ref, p_ref, pt_ref, k_ref, coup_ref, index_ref):
    low_atoms, high_atoms = up_ref[42:43, 0:LANES], down_ref[16:17, 0:LANES]
    lane = lane_iota(1, LANES)
    which = lane >> 5
    own = jnp.full((1, LANES), -100.0, F32)
    for c in range(4):
        own = jnp.where(which == c, atom_ref[c].astype(F32), own)
    edge_low = low_atoms[:, 96:97] - float(ATOM_DEV)
    fifth = jnp.where(which == 0, jnp.broadcast_to(edge_low, (1, LANES)), -200.0)
    from_upper = jnp.where(which < 3, high_atoms + float(ATOM_DEV), -300.0)
    from_lower = jnp.where(which < 3, low_atoms - float(ATOM_DEV), -400.0)
    source = jnp.concatenate([own, fifth, from_upper, from_lower], axis=1)
    inside = (lane_iota(SLOT, 4 * LANES) & (SLOT - 1)) == row_iota(SLOT, 4 * LANES)
    rows = []
    for c in range(8):
        if c < 4:
            same = source == atom_ref[c].astype(F32)
        elif c == 4:
            same = source == jnp.broadcast_to(edge_low, source.shape)
        else:
            same = source == 1000.0
        rows.append(jnp.where(inside & jnp.broadcast_to(same, inside.shape), 1.0, 0.0))
    k_ref[...] = jnp.concatenate(rows, axis=0).T.astype(BF16)
    lower = coupling_ref[pl.ds(pl.multiple_of(place_ref[0] * ATOM_DEV, ATOM_DEV), ATOM_DEV), :]
    mine = coupling_ref[pl.ds(pl.multiple_of(place_ref[1] * ATOM_DEV, ATOM_DEV), ATOM_DEV), :]
    pair = jnp.concatenate([lower, mine], axis=0)
    pair = jnp.concatenate([pair, jnp.zeros((2 * ATOM_DEV, SLOT - NPROJ), F32)], axis=1)
    wide = jnp.concatenate([pair] * 8, axis=1)
    target = source[:, : 2 * LANES]
    slot = row_iota(2 * ATOM_DEV, 2 * LANES).astype(F32)
    chosen = jnp.where(jnp.broadcast_to(target, slot.shape) == slot, wide, 0.0)
    coup_ref[...] = jnp.broadcast_to(jnp.sum(chosen, axis=0, keepdims=True), coup_ref.shape)
    parts = [padded_projectors(proj_ref[c]) for c in range(4)]
    parts.append(padded_projectors(up_ref[16 : 16 + NPROJ, 0:NPC]))
    parts.append(jnp.zeros((3 * SLOT, NPC), F32))
    stacked = jnp.concatenate(parts, axis=0)
    p_ref[0], p_ref[1] = split2(stacked)
    pt_ref[0], pt_ref[1] = split2(stacked.T)
    inverse = up_ref[41:42, 0:GHOST]
    index_ref[...] = jnp.zeros_like(index_ref)
    index_ref[0:2, :] = maps_ref[0:2, :]
    sent = maps_ref[2:3, :]
    rows8 = [jnp.broadcast_to(b, (8, LANES)) for b in blocks_of(inverse)]
    third = pick_row(rows8, sent)
    third = jnp.where(jnp.broadcast_to(sent, third.shape) >= 0, third, -1.0)
    index_ref[2:3, :] = third[0:1].astype(jnp.int32)
    index_ref[3:4, 0:NPC] = up_ref[40:41, 0:NPC].astype(jnp.int32) - NODES


def apply(v, x_ref, g_ref, up_ref, down_ref, conn_ref, index_ref, pot_ref, e_ref, p_ref, pt_ref, k_ref, coup_ref):
    edge = x_ref[48:64, :] + pick_row(blocks_of(down_ref[0:BANDS, 0:GHOST]), conn_ref[3:4, :] - NODES)
    low = up_ref[0:BANDS, 0:NPC] + pick_row(blocks_of(g_ref[...]), index_ref[3:4, 0:NPC])
    x_high, x_low = split2(jnp.concatenate([x_ref[0:48, :], edge, low], axis=0))
    wide = product(x_high, x_low, pt_ref[0], pt_ref[1])
    which = lane_iota(BANDS, 2 * LANES) >> 5
    own = jnp.zeros((BANDS, 2 * LANES), F32)
    for c in range(5):
        own = jnp.where(which == c, wide[c * BANDS : (c + 1) * BANDS], own)
    partials = jnp.concatenate([own, down_ref[0:BANDS, GHOST:], up_ref[0:BANDS, NPC:]], axis=1)
    sums = dot(jnp.concatenate(split3(partials), axis=0), k_ref[...])
    weights = (sums[0:16] + sums[16:32] + sums[32:48]) * coup_ref[0:1, :]
    spread = jnp.concatenate([jnp.where(which == c, weights, 0.0) for c in range(5)], axis=0)
    c_high, c_low = split2(spread)
    y = product(x_high, x_low, e_ref[0], e_ref[1]) + product(c_high, c_low, p_ref[0], p_ref[1])
    cells = []
    for c in range(5):
        cells += blocks_of(y[c * BANDS : (c + 1) * BANDS])
    out = []
    for k in range(NODES // LANES):
        here = slice(k * LANES, (k + 1) * LANES)
        total = pick(cells[:16], index_ref[0:1, here]) + pick(cells[:16], index_ref[1:2, here])
        out.append(total + pick(cells[16:], index_ref[2:3, here]))
    return jnp.concatenate(out, axis=1) + pot_ref[...] * v


def step_kernel(first, v_ref, prev_ref, x_ref, g_ref, up_ref, down_ref, conn_ref, send_ref, index_ref, pot_ref, e_ref, p_ref, pt_ref,
                k_ref, coup_ref, inner_ref, new_ref, xo_ref, go_ref, upo_ref, downo_ref):
    v = v_ref[...]
    h = apply(v, x_ref, g_ref, up_ref, down_ref, conn_ref, index_ref, pot_ref, e_ref, p_ref, pt_ref, k_ref, coup_ref)
    if first:
        new = (h - CENTER * v) * (1.0 / HALF_WIDTH)
    else:
        new = (h - CENTER * v) * (2.0 / HALF_WIDTH) - prev_ref[...]
    new_ref[...] = new
    cells, ghosts = gathered(new, conn_ref, send_ref)
    for c in range(4):
        xo_ref[c * BANDS : (c + 1) * BANDS, :] = cells[c]
    go_ref[...] = ghosts
    partials = inner_partials(cells, inner_ref[0], inner_ref[1])
    upo_ref[:, 0:NPC] = cells[3]
    upo_ref[:, NPC:] = partials
    downo_ref[:, 0:GHOST] = ghosts
    downo_ref[:, GHOST:] = partials


def gram_kernel(v_ref, all_ref, x_ref, g_ref, up_ref, down_ref, conn_ref, index_ref, pot_ref, e_ref, p_ref, pt_ref, k_ref, coup_ref,
                out_ref):
    v = v_ref[...]
    h = apply(v, x_ref, g_ref, up_ref, down_ref, conn_ref, index_ref, pot_ref, e_ref, p_ref, pt_ref, k_ref, coup_ref)
    s_high, s_low = split2(jnp.concatenate([h, v], axis=0))
    a_high, a_low = split2(all_ref[...])
    both = dot_nt(jnp.concatenate([s_high, s_low], axis=0), a_high)
    panel = both[:32] + both[32:] + dot_nt(s_high, a_low)
    for i in range(out_ref.shape[0]):
        out_ref[i] = panel


def add_kernel(parts_ref, out_ref):
    total = parts_ref[0]
    for i in range(1, parts_ref.shape[0]):
        total = total + parts_ref[i]
    for i in range(out_ref.shape[0]):
        out_ref[i] = total


def last_kernel(scale, parts_ref, projected_ref, correlation_ref):
    total = parts_ref[0]
    for i in range(1, parts_ref.shape[0]):
        total = total + parts_ref[i]
    flipped = (total * scale).T
    projected_ref[...] = flipped[:, 0:BANDS]
    correlation_ref[...] = flipped[:, BANDS:]


VM = pl.BlockSpec(memory_space=pltpu.VMEM)
SM = pl.BlockSpec(memory_space=pltpu.SMEM)


def call(kernel, outs, ins, *args):
    return pl.pallas_call(
        kernel,
        out_shape=[jax.ShapeDtypeStruct(s, t) for s, t in outs],
        in_specs=ins,
        out_specs=[VM] * len(outs),
        compiler_params=pltpu.CompilerParams(vmem_limit_bytes=40 * 2**20),
    )(*args)


def shifted(block, distance):
    size = lax.axis_size("fe")
    return lax.ppermute(block, "fe", [(i, (i + distance) % size) for i in range(size)])


def on_device(wavefunctions, potential, element_matrix, projectors, coupling, connectivity, send_list, atom_of_cell):
    fe_count = lax.axis_size("fe")
    fe = lax.axis_index("fe").astype(jnp.int32)
    place = jnp.stack([(fe + fe_count - 1) % fe_count, fe])
    send = send_list.reshape(1, GHOST)
    pot = potential.reshape(1, NODES)
    x, g, up, down, inner = call(
        first_kernel,
        [((64, NPC), F32), ((BANDS, GHOST), F32), ((48, 640), F32), ((24, 384), F32), ((2, NPC, LANES), BF16)],
        [VM, VM, VM, SM, VM],
        wavefunctions, connectivity, send, atom_of_cell, projectors,
    )
    up, down = shifted(up, 1), shifted(down, -1)
    e, maps = call(
        local_kernel,
        [((2, NPC, NPC), BF16), ((8, NODES), jnp.int32)],
        [VM, VM, VM],
        connectivity, send, element_matrix,
    )
    p, pt, k, coup, index = call(
        joined_kernel,
        [((2, 256, NPC), BF16), ((2, NPC, 256), BF16), ((512, 256), BF16), ((8, 256), F32), ((8, NODES), jnp.int32)],
        [VM, VM, VM, SM, SM, VM, VM],
        up, down, maps, atom_of_cell, place, projectors, coupling,
    )
    previous = current = wavefunctions
    for step in range(DEGREE):
        new, x, g, up, down = call(
            functools.partial(step_kernel, step == 0),
            [((BANDS, NODES), F32), ((64, NPC), F32), ((BANDS, GHOST), F32), ((BANDS, 640), F32), ((BANDS, 384), F32)],
            [VM] * 16,
            current, previous, x, g, up, down, connectivity, send, index, pot, e, p, pt, k, coup, inner,
        )
        previous, current = current, new
        up, down = shifted(up, 1), shifted(down, -1)
    everyone = lax.all_gather(current, "band", axis=0, tiled=True)
    (copies,) = call(
        gram_kernel,
        [((4, 32, LANES), F32)],
        [VM] * 14,
        current, everyone, x, g, up, down, connectivity, index, pot, e, p, pt, k, coup,
    )
    near = [[4 * i + j for j in range(4)] for i in range(fe_count // 4)]
    far = [[4 * i + j for i in range(fe_count // 4)] for j in range(4)]
    parts = lax.all_to_all(copies, "fe", 0, 0, axis_index_groups=near)
    (copies,) = call(add_kernel, [((fe_count // 4, 32, LANES), F32)], [VM], parts)
    parts = lax.all_to_all(copies, "fe", 0, 0, axis_index_groups=far)
    projected, correlation = call(
        functools.partial(last_kernel, 1.0 / (NODES * fe_count)),
        [((LANES, BANDS), F32), ((LANES, BANDS), F32)],
        [VM],
        parts,
    )
    return current, projected, correlation


def solution(mesh):
    in_specs = (
        P("band", "fe"),
        P("fe"),
        P(),
        P("fe", None, None),
        P(),
        P("fe", None),
        P("fe"),
        P("fe"),
    )
    out_specs = (P("band", "fe"), P(None, "band"), P(None, "band"))
    return jax.shard_map(on_device, mesh=mesh, in_specs=in_specs, out_specs=out_specs, check_vma=False)
```

time: 713 us -> 159 us (0.22)
  the two profiles are of different devices: /device:TPU:2 before, /device:TPU:32 now
where the time goes in v1:
time: 159 us; the launch traced here: 158 us
  blocking collectives  65 us (41%)
  starting transfers between devices  57.2 us (36%)
  Pallas kernels  22.3 us (14%)
  waiting for transfers between devices  7.45 us (5%)
  local copies, waits for them, and re-layouts  5.04 us (3%)
    ppermute x14, starting transfers between devices, shifted(): lax.ppermute(block, 'fe', [(i, (i + distance) % size) for i in range(size)])  57.2 us
    all_to_all x1, blocking collectives, on_device(): parts = lax.all_to_all(copies, 'fe', 0, 0, axis_index_groups=far)  39.9 us
    pallas_call x12, Pallas kernels, call(): pl.pallas_call(kernel, out_shape=[jax.ShapeDtypeStruct(s, t) for s, t in...  22.3 us
    all_gather x1, blocking collectives, on_device(): everyone = lax.all_gather(current, 'band', axis=0, tiled=True)  13.8 us
    all_to_all x1, blocking collectives, on_device(): parts = lax.all_to_all(copies, 'fe', 0, 0, axis_index_groups=near)  11.3 us
    ppermute x14, waiting for transfers between devices, shifted(): lax.ppermute(block, 'fe', [(i, (i + distance) % size) for i in range(size)])  7.45 us
    unnamed x20, local copies, waits for them, and re-layouts  5.04 us
  transfers between devices with their start and end apart: 14, of which 5 were waited for; matrix products, arithmetic and copies ran while one was open for 0% of the time, Pallas kernels for 1%

profile of v1, /device:TPU:32, one launch (start us, length us, event | category | flops | bytes accessed | tf_op | source)
XLA Modules:
  0.0 158.0 jit_solution(13408580987156860388)
XLA Ops:
  0.7 1.0 copy.11.proj_ref
  1.6 0.0 copy-start.5
  1.7 0.0 copy-start.6
  1.7 0.6 copy-done.5
  2.3 1.2 shard_map.103
  3.5 3.5 %collective-permute-start = (f32[48,640]{1,0:T(8,128)S(1)}, f32[48,640]{1,0:T(8,128)S(1)}, u32[]{:S(2)}, u32[]{:S(2)}) collective-permute-start(f32[48,640]{1,0:T(8,128)S(1)} %get-tuple-element.49), channel_id=1, source_target_pairs={{0,8},{8,16},{16,24},{24,32},{32,40},{40,48},{48,56},{56,64},{64,7... | collective-permute-start | bytes 368648 | tf_op jit(solution)/shard_map/ppermute | solution.py:302
  7.0 4.5 %collective-permute-start.1 = (f32[24,384]{1,0:T(8,128)S(1)}, f32[24,384]{1,0:T(8,128)S(1)}, u32[]{:S(2)}, u32[]{:S(2)}) collective-permute-start(f32[24,384]{1,0:T(8,128)S(1)} %get-tuple-element.50), channel_id=1, source_target_pairs={{0,504},{8,0},{16,8},{24,16},{32,24},{40,32},{48,40},{56,48},{64,5... | collective-permute-start | bytes 110600 | tf_op jit(solution)/shard_map/ppermute | solution.py:302
  11.5 0.1 pad_add_fusion.place_ref
  11.6 0.1 copy.13.coupling_ref
  11.7 0.0 copy-start.1
  11.7 1.2 copy-done.1
  12.9 2.2 %shard_map.104 = (bf16[2,512,512]{2,1,0:T(8,128)(2,1)S(1)}, s32[8,1024]{1,0:T(8,128)S(1)}) custom-call(s32[4,512]{1,0:T(4,128)S(1)} %copy-done.2, s32[1,256]{1,0:T(1,128)S(1)} %bitcast.12, f32[512,512]{1,0:T(8,128)S(1)} %copy-done.1), custom_call_target="tpu_custom_call" | custom-call | tf_op jit(solution)/shard_map/pallas_call | solution.py:291
  15.1 1.0 shard_map.105
  16.1 0.0 copy-start.4
  16.1 0.7 copy-done.4
  16.8 2.5 %shard_map.106 = (f32[16,1024]{1,0:T(8,128)S(1)}, f32[64,512]{1,0:T(8,128)S(1)}, f32[16,256]{1,0:T(8,128)S(1)}, f32[16,640]{1,0:T(8,128)S(1)}, f32[16,384]{1,0:T(8,128)S(1)}) custom-call(f32[16,1024]{1,0:T(8,128)S(1)} %copy-done, f32[16,1024]{1,0:T(8,128)S(1)} %copy-done, f32[64,512]{1,0:T(8,128)S(1)} %get-tuple-element.47.x_ref, ...), custom_call_target="tpu_custom_call" | custom-call | tf_op jit(solution)/shard_map/pallas_call | solution.py:291
  19.3 1.9 %collective-permute-start.2 = (f32[16,640]{1,0:T(8,128)S(1)}, f32[16,640]{1,0:T(8,128)S(1)}, u32[]{:S(2)}, u32[]{:S(2)}) collective-permute-start(f32[16,640]{1,0:T(8,128)S(1)} %get-tuple-element.62), channel_id=1, source_target_pairs={{0,8},{8,16},{16,24},{24,32},{32,40},{40,48},{48,56},{56,64},{64,7... | collective-permute-start | bytes 122888 | tf_op jit(solution)/shard_map/ppermute | solution.py:302
  21.2 6.0 %collective-permute-start.3 = (f32[16,384]{1,0:T(8,128)S(1)}, f32[16,384]{1,0:T(8,128)S(1)}, u32[]{:S(2)}, u32[]{:S(2)}) collective-permute-start(f32[16,384]{1,0:T(8,128)S(1)} %get-tuple-element.63), channel_id=1, source_target_pairs={{0,504},{8,0},{16,8},{24,16},{32,24},{40,32},{48,40},{56,48},{64,5... | collective-permute-start | bytes 73736 | tf_op jit(solution)/shard_map/ppermute | solution.py:302
  27.3 1.5 collective-permute-done.3.down_ref
  28.8 0.0 collective-permute-done.2.up_ref
  28.8 2.5 %shard_map.107 = (f32[16,1024]{1,0:T(8,128)S(1)}, f32[64,512]{1,0:T(8,128)S(1)}, f32[16,256]{1,0:T(8,128)S(1)}, f32[16,640]{1,0:T(8,128)S(1)}, f32[16,384]{1,0:T(8,128)S(1)}) custom-call(f32[16,1024]{1,0:T(8,128)S(1)} %get-tuple-element.59.v_ref.prev_ref, f32[16,1024]{1,0:T(8,128)S(1)} %copy-done, f32[64,512]{1,0:T(8,128)S(1)} %get-tuple-element.60.x_ref, ...), custom_call_target="tpu_custom_call" | custom-call | tf_op jit(solution)/shard_map/pallas_call | solution.py:291
  31.3 2.3 %collective-permute-start.4 = (f32[16,640]{1,0:T(8,128)S(1)}, f32[16,640]{1,0:T(8,128)S(1)}, u32[]{:S(2)}, u32[]{:S(2)}) collective-permute-start(f32[16,640]{1,0:T(8,128)S(1)} %get-tuple-element.67), channel_id=1, source_target_pairs={{0,8},{8,16},{16,24},{24,32},{32,40},{40,48},{48,56},{56,64},{64,7... | collective-permute-start | bytes 122888 | tf_op jit(solution)/shard_map/ppermute | solution.py:302
  33.6 5.9 %collective-permute-start.5 = (f32[16,384]{1,0:T(8,128)S(1)}, f32[16,384]{1,0:T(8,128)S(1)}, u32[]{:S(2)}, u32[]{:S(2)}) collective-permute-start(f32[16,384]{1,0:T(8,128)S(1)} %get-tuple-element.68), channel_id=1, source_target_pairs={{0,504},{8,0},{16,8},{24,16},{32,24},{40,32},{48,40},{56,48},{64,5... | collective-permute-start | bytes 73736 | tf_op jit(solution)/shard_map/ppermute | solution.py:302
  39.5 1.5 collective-permute-done.5.down_ref
  41.0 2.5 %shard_map.108 = (f32[16,1024]{1,0:T(8,128)S(1)}, f32[64,512]{1,0:T(8,128)S(1)}, f32[16,256]{1,0:T(8,128)S(1)}, f32[16,640]{1,0:T(8,128)S(1)}, f32[16,384]{1,0:T(8,128)S(1)}) custom-call(f32[16,1024]{1,0:T(8,128)S(1)} %get-tuple-element.64.v_ref.prev_ref, f32[16,1024]{1,0:T(8,128)S(1)} %get-tuple-element.59.v_ref.prev_ref, ...), custom_call_target="tpu_custom_call" | custom-call | tf_op jit(solution)/shard_map/pallas_call | solution.py:291
  43.5 4.1 %collective-permute-start.6 = (f32[16,640]{1,0:T(8,128)S(1)}, f32[16,640]{1,0:T(8,128)S(1)}, u32[]{:S(2)}, u32[]{:S(2)}) collective-permute-start(f32[16,640]{1,0:T(8,128)S(1)} %get-tuple-element.72), channel_id=1, source_target_pairs={{0,8},{8,16},{16,24},{24,32},{32,40},{40,48},{48,56},{56,64},{64,7... | collective-permute-start | bytes 122888 | tf_op jit(solution)/shard_map/ppermute | solution.py:302
  47.6 4.2 %collective-permute-start.7 = (f32[16,384]{1,0:T(8,128)S(1)}, f32[16,384]{1,0:T(8,128)S(1)}, u32[]{:S(2)}, u32[]{:S(2)}) collective-permute-start(f32[16,384]{1,0:T(8,128)S(1)} %get-tuple-element.73), channel_id=1, source_target_pairs={{0,504},{8,0},{16,8},{24,16},{32,24},{40,32},{48,40},{56,48},{64,5... | collective-permute-start | bytes 73736 | tf_op jit(solution)/shard_map/ppermute | solution.py:302
  51.8 1.5 collective-permute-done.7.down_ref
  53.3 0.0 collective-permute-done.6.up_ref
  53.3 2.5 %shard_map.109 = (f32[16,1024]{1,0:T(8,128)S(1)}, f32[64,512]{1,0:T(8,128)S(1)}, f32[16,256]{1,0:T(8,128)S(1)}, f32[16,640]{1,0:T(8,128)S(1)}, f32[16,384]{1,0:T(8,128)S(1)}) custom-call(f32[16,1024]{1,0:T(8,128)S(1)} %get-tuple-element.69.v_ref.prev_ref, f32[16,1024]{1,0:T(8,128)S(1)} %get-tuple-element.64.v_ref.prev_ref, ...), custom_call_target="tpu_custom_call" | custom-call | tf_op jit(solution)/shard_map/pallas_call | solution.py:291
  55.8 4.0 %collective-permute-start.8 = (f32[16,640]{1,0:T(8,128)S(1)}, f32[16,640]{1,0:T(8,128)S(1)}, u32[]{:S(2)}, u32[]{:S(2)}) collective-permute-start(f32[16,640]{1,0:T(8,128)S(1)} %get-tuple-element.77), channel_id=1, source_target_pairs={{0,8},{8,16},{16,24},{24,32},{32,40},{40,48},{48,56},{56,64},{64,7... | collective-permute-start | bytes 122888 | tf_op jit(solution)/shard_map/ppermute | solution.py:302
  59.9 4.4 %collective-permute-start.9 = (f32[16,384]{1,0:T(8,128)S(1)}, f32[16,384]{1,0:T(8,128)S(1)}, u32[]{:S(2)}, u32[]{:S(2)}) collective-permute-start(f32[16,384]{1,0:T(8,128)S(1)} %get-tuple-element.78), channel_id=1, source_target_pairs={{0,504},{8,0},{16,8},{24,16},{32,24},{40,32},{48,40},{56,48},{64,5... | collective-permute-start | bytes 73736 | tf_op jit(solution)/shard_map/ppermute | solution.py:302
  64.2 1.4 collective-permute-done.9.down_ref
  65.6 2.5 %shard_map.110 = (f32[16,1024]{1,0:T(8,128)S(1)}, f32[64,512]{1,0:T(8,128)S(1)}, f32[16,256]{1,0:T(8,128)S(1)}, f32[16,640]{1,0:T(8,128)S(1)}, f32[16,384]{1,0:T(8,128)S(1)}) custom-call(f32[16,1024]{1,0:T(8,128)S(1)} %get-tuple-element.74.v_ref.prev_ref, f32[16,1024]{1,0:T(8,128)S(1)} %get-tuple-element.69.v_ref.prev_ref, ...), custom_call_target="tpu_custom_call" | custom-call | tf_op jit(solution)/shard_map/pallas_call | solution.py:291
  68.1 4.0 %collective-permute-start.10 = (f32[16,640]{1,0:T(8,128)S(1)}, f32[16,640]{1,0:T(8,128)S(1)}, u32[]{:S(2)}, u32[]{:S(2)}) collective-permute-start(f32[16,640]{1,0:T(8,128)S(1)} %get-tuple-element.82), channel_id=1, source_target_pairs={{0,8},{8,16},{16,24},{24,32},{32,40},{40,48},{48,56},{56,64},{64,7... | collective-permute-start | bytes 122888 | tf_op jit(solution)/shard_map/ppermute | solution.py:302
  72.1 4.2 %collective-permute-start.11 = (f32[16,384]{1,0:T(8,128)S(1)}, f32[16,384]{1,0:T(8,128)S(1)}, u32[]{:S(2)}, u32[]{:S(2)}) collective-permute-start(f32[16,384]{1,0:T(8,128)S(1)} %get-tuple-element.83), channel_id=1, source_target_pairs={{0,504},{8,0},{16,8},{24,16},{32,24},{40,32},{48,40},{56,48},{64,5... | collective-permute-start | bytes 73736 | tf_op jit(solution)/shard_map/ppermute | solution.py:302
  76.3 1.5 collective-permute-done.11.down_ref
  77.8 3.0 %shard_map.111 = (f32[16,1024]{1,0:T(8,128)}, f32[64,512]{1,0:T(8,128)S(1)}, f32[16,256]{1,0:T(8,128)S(1)}, f32[16,640]{1,0:T(8,128)S(1)}, f32[16,384]{1,0:T(8,128)S(1)}) custom-call(f32[16,1024]{1,0:T(8,128)S(1)} %get-tuple-element.79.v_ref, f32[16,1024]{1,0:T(8,128)S(1)} %get-tuple-element.74.v_ref.prev_ref, f32[64,512]{1,0:T(8,128)S(1)} %get-tuple-element.80.x_ref, ...), custom_call_target="tpu_custom_call" | custom-call | tf_op jit(solution)/shard_map/pallas_call | solution.py:291
  80.9 6.3 %collective-permute-start.13 = (f32[16,384]{1,0:T(8,128)S(1)}, f32[16,384]{1,0:T(8,128)S(1)}, u32[]{:S(2)}, u32[]{:S(2)}) collective-permute-start(f32[16,384]{1,0:T(8,128)S(1)} %get-tuple-element.88), channel_id=1, source_target_pairs={{0,504},{8,0},{16,8},{24,16},{32,24},{40,32},{48,40},{56,48},{64,5... | collective-permute-start | bytes 73736 | tf_op jit(solution)/shard_map/ppermute | solution.py:302
  87.2 1.9 %collective-permute-start.12 = (f32[16,640]{1,0:T(8,128)S(1)}, f32[16,640]{1,0:T(8,128)S(1)}, u32[]{:S(2)}, u32[]{:S(2)}) collective-permute-start(f32[16,640]{1,0:T(8,128)S(1)} %get-tuple-element.87), channel_id=1, source_target_pairs={{0,8},{8,16},{16,24},{24,32},{32,40},{40,48},{48,56},{56,64},{64,7... | collective-permute-start | bytes 122888 | tf_op jit(solution)/shard_map/ppermute | solution.py:302
  89.1 0.0 copy-start.3
  89.1 13.8 %all_gather.3.all_ref = f32[128,1024]{1,0:T(8,128)S(1)} all-gather(f32[16,1024]{1,0:T(8,128)} %get-tuple-element.91.v_ref), channel_id=1, replica_groups=mesh['fe'=64,'band'=8] {'band'}, dimensions={0}, use_global_device_ids=true | all-gather | bytes 589824 | tf_op jit(solution)/shard_map/all_gather | solution.py:340
  102.9 2.3 %shard_map.112 = f32[4,32,128]{2,1,0:T(8,128)S(1)} custom-call(f32[16,1024]{1,0:T(8,128)S(1)} %copy-done.3, f32[128,1024]{1,0:T(8,128)S(1)} %all_gather.3.all_ref, f32[64,512]{1,0:T(8,128)S(1)} %get-tuple-element.85.x_ref, f32[16,256]{1,0:T(8,128)S(1)} %get-tuple-element.86.g_ref, f32[16,640]{1,0:T(8,128)S(1)} %collective-permute-done.12.up_ref, ...), custom_call_target="tpu_custom_call" | custom-call | tf_op jit(solution)/shard_map/pallas_call | solution.py:291
  105.2 11.3 %all_to_all.10.parts_ref = f32[4,32,128]{2,1,0:T(8,128)S(1)} all-to-all(f32[4,32,128]{2,1,0:T(8,128)S(1)} %shard_map.112), channel_id=1, replica_groups={{0,8,16,24},{32,40,48,56},{64,72,80,88},{96,104,112,120},{128,136,144,1..., dimensions={0} | all-to-all | bytes 131072 | tf_op jit(solution)/shard_map/all_to_all | solution.py:349
  116.6 39.9 %all_to_all.11.parts_ref = f32[16,32,128]{2,1,0:T(8,128)S(1)} all-to-all(f32[16,32,128]{2,1,0:T(8,128)S(1)} %shard_map.113), channel_id=1, replica_groups={{0,32,64,96,128,160,192,224,256,288,320,352,384,416,448,480},{8,40,72,1..., dimensions={0} | all-to-all | bytes 524288 | tf_op jit(solution)/shard_map/all_to_all | solution.py:351
  156.5 0.2 shard_map.114
  156.7 0.7 copy.14
  157.3 0.7 copy.15
  (16 shorter events, 0.1 us)
Async XLA Ops:
  0.6 1.0 copy-start.2
  0.6 1.0 copy-start
  1.6 0.7 copy-start.5
  1.7 0.7 copy-start.6
  2.3 9.2 %copy-start.7 = (f32[512,18]{0,1:T(8,128)S(1)}, f32[512,18]{0,1:T(8,128)}, u32[]{:S(2)}) copy-start(f32[512,18]{0,1:T(8,128)} %param.12) | copy-start | bytes 110596
  3.5 11.6 %collective-permute-start = (f32[48,640]{1,0:T(8,128)S(1)}, f32[48,640]{1,0:T(8,128)S(1)}, u32[]{:S(2)}, u32[]{:S(2)}) collective-permute-start(f32[48,640]{1,0:T(8,128)S(1)} %get-tuple-element.49), channel_id=1, source_target_pairs={{0,8},{8,16},{16,24},{24,32},{32,40},{40,48},{48,56},{56,64},{64,7... | collective-permute-start | bytes 368648 | tf_op jit(solution)/shard_map/ppermute | solution.py:302
  7.0 8.1 %collective-permute-start.1 = (f32[24,384]{1,0:T(8,128)S(1)}, f32[24,384]{1,0:T(8,128)S(1)}, u32[]{:S(2)}, u32[]{:S(2)}) collective-permute-start(f32[24,384]{1,0:T(8,128)S(1)} %get-tuple-element.50), channel_id=1, source_target_pairs={{0,504},{8,0},{16,8},{24,16},{32,24},{40,32},{48,40},{56,48},{64,5... | collective-permute-start | bytes 110600 | tf_op jit(solution)/shard_map/ppermute | solution.py:302
  11.7 1.2 copy-start.1
  16.1 0.7 copy-start.4
  19.3 9.5 %collective-permute-start.2 = (f32[16,640]{1,0:T(8,128)S(1)}, f32[16,640]{1,0:T(8,128)S(1)}, u32[]{:S(2)}, u32[]{:S(2)}) collective-permute-start(f32[16,640]{1,0:T(8,128)S(1)} %get-tuple-element.62), channel_id=1, source_target_pairs={{0,8},{8,16},{16,24},{24,32},{32,40},{40,48},{48,56},{56,64},{64,7... | collective-permute-start | bytes 122888 | tf_op jit(solution)/shard_map/ppermute | solution.py:302
  21.2 7.5 %collective-permute-start.3 = (f32[16,384]{1,0:T(8,128)S(1)}, f32[16,384]{1,0:T(8,128)S(1)}, u32[]{:S(2)}, u32[]{:S(2)}) collective-permute-start(f32[16,384]{1,0:T(8,128)S(1)} %get-tuple-element.63), channel_id=1, source_target_pairs={{0,504},{8,0},{16,8},{24,16},{32,24},{40,32},{48,40},{56,48},{64,5... | collective-permute-start | bytes 73736 | tf_op jit(solution)/shard_map/ppermute | solution.py:302
  31.3 9.8 %collective-permute-start.4 = (f32[16,640]{1,0:T(8,128)S(1)}, f32[16,640]{1,0:T(8,128)S(1)}, u32[]{:S(2)}, u32[]{:S(2)}) collective-permute-start(f32[16,640]{1,0:T(8,128)S(1)} %get-tuple-element.67), channel_id=1, source_target_pairs={{0,8},{8,16},{16,24},{24,32},{32,40},{40,48},{48,56},{56,64},{64,7... | collective-permute-start | bytes 122888 | tf_op jit(solution)/shard_map/ppermute | solution.py:302
  33.6 7.4 %collective-permute-start.5 = (f32[16,384]{1,0:T(8,128)S(1)}, f32[16,384]{1,0:T(8,128)S(1)}, u32[]{:S(2)}, u32[]{:S(2)}) collective-permute-start(f32[16,384]{1,0:T(8,128)S(1)} %get-tuple-element.68), channel_id=1, source_target_pairs={{0,504},{8,0},{16,8},{24,16},{32,24},{40,32},{48,40},{56,48},{64,5... | collective-permute-start | bytes 73736 | tf_op jit(solution)/shard_map/ppermute | solution.py:302
  43.5 9.8 %collective-permute-start.6 = (f32[16,640]{1,0:T(8,128)S(1)}, f32[16,640]{1,0:T(8,128)S(1)}, u32[]{:S(2)}, u32[]{:S(2)}) collective-permute-start(f32[16,640]{1,0:T(8,128)S(1)} %get-tuple-element.72), channel_id=1, source_target_pairs={{0,8},{8,16},{16,24},{24,32},{32,40},{40,48},{48,56},{56,64},{64,7... | collective-permute-start | bytes 122888 | tf_op jit(solution)/shard_map/ppermute | solution.py:302
  47.6 5.7 %collective-permute-start.7 = (f32[16,384]{1,0:T(8,128)S(1)}, f32[16,384]{1,0:T(8,128)S(1)}, u32[]{:S(2)}, u32[]{:S(2)}) collective-permute-start(f32[16,384]{1,0:T(8,128)S(1)} %get-tuple-element.73), channel_id=1, source_target_pairs={{0,504},{8,0},{16,8},{24,16},{32,24},{40,32},{48,40},{56,48},{64,5... | collective-permute-start | bytes 73736 | tf_op jit(solution)/shard_map/ppermute | solution.py:302
  55.8 9.8 %collective-permute-start.8 = (f32[16,640]{1,0:T(8,128)S(1)}, f32[16,640]{1,0:T(8,128)S(1)}, u32[]{:S(2)}, u32[]{:S(2)}) collective-permute-start(f32[16,640]{1,0:T(8,128)S(1)} %get-tuple-element.77), channel_id=1, source_target_pairs={{0,8},{8,16},{16,24},{24,32},{32,40},{40,48},{48,56},{56,64},{64,7... | collective-permute-start | bytes 122888 | tf_op jit(solution)/shard_map/ppermute | solution.py:302
  59.9 5.7 %collective-permute-start.9 = (f32[16,384]{1,0:T(8,128)S(1)}, f32[16,384]{1,0:T(8,128)S(1)}, u32[]{:S(2)}, u32[]{:S(2)}) collective-permute-start(f32[16,384]{1,0:T(8,128)S(1)} %get-tuple-element.78), channel_id=1, source_target_pairs={{0,504},{8,0},{16,8},{24,16},{32,24},{40,32},{48,40},{56,48},{64,5... | collective-permute-start | bytes 73736 | tf_op jit(solution)/shard_map/ppermute | solution.py:302
  68.1 9.8 %collective-permute-start.10 = (f32[16,640]{1,0:T(8,128)S(1)}, f32[16,640]{1,0:T(8,128)S(1)}, u32[]{:S(2)}, u32[]{:S(2)}) collective-permute-start(f32[16,640]{1,0:T(8,128)S(1)} %get-tuple-element.82), channel_id=1, source_target_pairs={{0,8},{8,16},{16,24},{24,32},{32,40},{40,48},{48,56},{56,64},{64,7... | collective-permute-start | bytes 122888 | tf_op jit(solution)/shard_map/ppermute | solution.py:302
  72.1 5.7 %collective-permute-start.11 = (f32[16,384]{1,0:T(8,128)S(1)}, f32[16,384]{1,0:T(8,128)S(1)}, u32[]{:S(2)}, u32[]{:S(2)}) collective-permute-start(f32[16,384]{1,0:T(8,128)S(1)} %get-tuple-element.83), channel_id=1, source_target_pairs={{0,504},{8,0},{16,8},{24,16},{32,24},{40,32},{48,40},{56,48},{64,5... | collective-permute-start | bytes 73736 | tf_op jit(solution)/shard_map/ppermute | solution.py:302
  80.9 22.0 %collective-permute-start.13 = (f32[16,384]{1,0:T(8,128)S(1)}, f32[16,384]{1,0:T(8,128)S(1)}, u32[]{:S(2)}, u32[]{:S(2)}) collective-permute-start(f32[16,384]{1,0:T(8,128)S(1)} %get-tuple-element.88), channel_id=1, source_target_pairs={{0,504},{8,0},{16,8},{24,16},{32,24},{40,32},{48,40},{56,48},{64,5... | collective-permute-start | bytes 73736 | tf_op jit(solution)/shard_map/ppermute | solution.py:302
  87.2 15.8 %collective-permute-start.12 = (f32[16,640]{1,0:T(8,128)S(1)}, f32[16,640]{1,0:T(8,128)S(1)}, u32[]{:S(2)}, u32[]{:S(2)}) collective-permute-start(f32[16,640]{1,0:T(8,128)S(1)} %get-tuple-element.87), channel_id=1, source_target_pairs={{0,8},{8,16},{16,24},{24,32},{32,40},{40,48},{48,56},{56,64},{64,7... | collective-permute-start | bytes 122888 | tf_op jit(solution)/shard_map/ppermute | solution.py:302
  89.1 13.8 %copy-start.3 = (f32[16,1024]{1,0:T(8,128)S(1)}, f32[16,1024]{1,0:T(8,128)}, u32[]{:S(2)}) copy-start(f32[16,1024]{1,0:T(8,128)} %get-tuple-element.91.v_ref) | copy-start | bytes 196612

commit v2 on v1

--- a/solution.py
+++ b/solution.py
@@ -278,9 +278,8 @@
     total = parts_ref[0]
     for i in range(1, parts_ref.shape[0]):
         total = total + parts_ref[i]
-    flipped = (total * scale).T
-    projected_ref[...] = flipped[:, 0:BANDS]
-    correlation_ref[...] = flipped[:, BANDS:]
+    projected_ref[...] = total[0:BANDS] * scale
+    correlation_ref[...] = total[BANDS:] * scale
 
 
 VM = pl.BlockSpec(memory_space=pltpu.VMEM)
@@ -336,8 +335,11 @@
             current, previous, x, g, up, down, connectivity, send, index, pot, e, p, pt, k, coup, inner,
         )
         previous, current = current, new
+        if step == DEGREE - 1:
+            bands = lax.axis_size("band")
+            everyone = lax.all_to_all(jnp.broadcast_to(current[None], (bands,) + current.shape), "band", 0, 0)
+            everyone = everyone.reshape(bands * BANDS, NODES)
         up, down = shifted(up, 1), shifted(down, -1)
-    everyone = lax.all_gather(current, "band", axis=0, tiled=True)
     (copies,) = call(
         gram_kernel,
         [((4, 32, LANES), F32)],
@@ -351,11 +353,11 @@
     parts = lax.all_to_all(copies, "fe", 0, 0, axis_index_groups=far)
     projected, correlation = call(
         functools.partial(last_kernel, 1.0 / (NODES * fe_count)),
-        [((LANES, BANDS), F32), ((LANES, BANDS), F32)],
+        [((BANDS, LANES), F32), ((BANDS, LANES), F32)],
         [VM],
         parts,
     )
-    return current, projected, correlation
+    return current, projected.T, correlation.T
 
 
 def solution(mesh):

time: 159 us -> 152 us (0.956)
  blocking collectives: 65 us -> 50.4 us
  starting transfers between devices: 57.2 us -> 61.6 us
  waiting for transfers between devices: 7.45 us -> 9.56 us
    all_gather x1 -> x0, blocking collectives: 13.8 us -> none  [on_device(): everyone = lax.all_gather(current, 'band', axis=0, tiled=True)]
    all_to_all x0 -> x1, starting transfers between devices: none -> 4.43 us  [on_device(): lax.all_to_all(jnp.broadcast_to(current[None], (bands,) + current.shape),...]
    broadcast_in_dim x0 -> x1, local copies, waits for them, and re-layouts: none -> 1.68 us  [on_device(): jnp.broadcast_to(current[None], (bands,) + current.shape)]
    all_to_all x1, blocking collectives: 39.9 us -> 38.3 us  [on_device(): parts = lax.all_to_all(copies, 'fe', 0, 0, axis_index_groups=far)]
    unnamed x20 -> x18, local copies, waits for them, and re-layouts: 5.04 us -> 3.7 us
  transfers between devices with their start and end apart: 14 -> 15, of which waited for: 5 -> 7; matrix products, arithmetic and copies ran while one was open for 0% -> 0% of each run, Pallas kernels for 1% -> 1%
where the time goes in v2:
time: 152 us; the launch traced here: 151 us
  starting transfers between devices  61.6 us (41%)
  blocking collectives  50.4 us (33%)
  Pallas kernels  22.8 us (15%)
  waiting for transfers between devices  9.56 us (6%)
  local copies, waits for them, and re-layouts  5.38 us (4%)
    ppermute x14, starting transfers between devices, shifted(): lax.ppermute(block, 'fe', [(i, (i + distance) % size) for i in range(size)])  57.2 us
    all_to_all x1, blocking collectives, on_device(): parts = lax.all_to_all(copies, 'fe', 0, 0, axis_index_groups=far)  38.3 us
    pallas_call x12, Pallas kernels, call(): pl.pallas_call(kernel, out_shape=[jax.ShapeDtypeStruct(s, t) for s, t in...  22.8 us
    all_to_all x1, blocking collectives, on_device(): parts = lax.all_to_all(copies, 'fe', 0, 0, axis_index_groups=near)  12.1 us
    ppermute x14, waiting for transfers between devices, shifted(): lax.ppermute(block, 'fe', [(i, (i + distance) % size) for i in range(size)])  8.96 us
    all_to_all x1, starting transfers between devices, on_device(): lax.all_to_all(jnp.broadcast_to(current[None], (bands,) + current.shape),...  4.43 us
    unnamed x18, local copies, waits for them, and re-layouts  3.7 us
  transfers between devices with their start and end apart: 15, of which 7 were waited for; matrix products, arithmetic and copies ran while one was open for 0% of the time, Pallas kernels for 1%

profile of v2, /device:TPU:32, one launch (start us, length us, event | category | flops | bytes accessed | tf_op | source)
XLA Modules:
  0.0 150.7 jit_solution(12909176393730872473)
XLA Ops:
  0.7 1.0 copy.11.proj_ref
  1.6 0.0 copy-start.5
  1.7 0.0 copy-start.6
  1.7 0.6 copy-done.5
  2.3 1.2 shard_map.103
  3.5 3.5 %collective-permute-start = (f32[48,640]{1,0:T(8,128)S(1)}, f32[48,640]{1,0:T(8,128)S(1)}, u32[]{:S(2)}, u32[]{:S(2)}) collective-permute-start(f32[48,640]{1,0:T(8,128)S(1)} %get-tuple-element.49), channel_id=1, source_target_pairs={{0,8},{8,16},{16,24},{24,32},{32,40},{40,48},{48,56},{56,64},{64,7... | collective-permute-start | bytes 368648 | tf_op jit(solution)/shard_map/ppermute | solution.py:301
  7.0 4.5 %collective-permute-start.1 = (f32[24,384]{1,0:T(8,128)S(1)}, f32[24,384]{1,0:T(8,128)S(1)}, u32[]{:S(2)}, u32[]{:S(2)}) collective-permute-start(f32[24,384]{1,0:T(8,128)S(1)} %get-tuple-element.50), channel_id=1, source_target_pairs={{0,504},{8,0},{16,8},{24,16},{32,24},{40,32},{48,40},{56,48},{64,5... | collective-permute-start | bytes 110600 | tf_op jit(solution)/shard_map/ppermute | solution.py:301
  11.5 0.1 pad_add_fusion.place_ref
  11.6 0.1 copy.13.coupling_ref
  11.7 0.0 copy-start.1
  11.7 1.2 copy-done.1
  12.9 2.2 %shard_map.104 = (bf16[2,512,512]{2,1,0:T(8,128)(2,1)S(1)}, s32[8,1024]{1,0:T(8,128)S(1)}) custom-call(s32[4,512]{1,0:T(4,128)S(1)} %copy-done.2, s32[1,256]{1,0:T(1,128)S(1)} %bitcast.16, f32[512,512]{1,0:T(8,128)S(1)} %copy-done.1), custom_call_target="tpu_custom_call" | custom-call | tf_op jit(solution)/shard_map/pallas_call | solution.py:290
  15.1 0.0 collective-permute-done.1.down_ref
  15.1 1.0 shard_map.105
  16.1 0.0 copy-start.4
  16.1 0.7 copy-done.4
  16.8 2.5 %shard_map.106 = (f32[16,1024]{1,0:T(8,128)S(1)}, f32[64,512]{1,0:T(8,128)S(1)}, f32[16,256]{1,0:T(8,128)S(1)}, f32[16,640]{1,0:T(8,128)S(1)}, f32[16,384]{1,0:T(8,128)S(1)}) custom-call(f32[16,1024]{1,0:T(8,128)S(1)} %copy-done, f32[16,1024]{1,0:T(8,128)S(1)} %copy-done, f32[64,512]{1,0:T(8,128)S(1)} %get-tuple-element.47.x_ref, ...), custom_call_target="tpu_custom_call" | custom-call | tf_op jit(solution)/shard_map/pallas_call | solution.py:290
  19.3 1.9 %collective-permute-start.2 = (f32[16,640]{1,0:T(8,128)S(1)}, f32[16,640]{1,0:T(8,128)S(1)}, u32[]{:S(2)}, u32[]{:S(2)}) collective-permute-start(f32[16,640]{1,0:T(8,128)S(1)} %get-tuple-element.62), channel_id=1, source_target_pairs={{0,8},{8,16},{16,24},{24,32},{32,40},{40,48},{48,56},{56,64},{64,7... | collective-permute-start | bytes 122888 | tf_op jit(solution)/shard_map/ppermute | solution.py:301
  21.2 6.0 %collective-permute-start.3 = (f32[16,384]{1,0:T(8,128)S(1)}, f32[16,384]{1,0:T(8,128)S(1)}, u32[]{:S(2)}, u32[]{:S(2)}) collective-permute-start(f32[16,384]{1,0:T(8,128)S(1)} %get-tuple-element.63), channel_id=1, source_target_pairs={{0,504},{8,0},{16,8},{24,16},{32,24},{40,32},{48,40},{56,48},{64,5... | collective-permute-start | bytes 73736 | tf_op jit(solution)/shard_map/ppermute | solution.py:301
  27.3 1.5 collective-permute-done.3.down_ref
  28.8 0.0 collective-permute-done.2.up_ref
  28.8 2.5 %shard_map.107 = (f32[16,1024]{1,0:T(8,128)S(1)}, f32[64,512]{1,0:T(8,128)S(1)}, f32[16,256]{1,0:T(8,128)S(1)}, f32[16,640]{1,0:T(8,128)S(1)}, f32[16,384]{1,0:T(8,128)S(1)}) custom-call(f32[16,1024]{1,0:T(8,128)S(1)} %get-tuple-element.59.v_ref.prev_ref, f32[16,1024]{1,0:T(8,128)S(1)} %copy-done, f32[64,512]{1,0:T(8,128)S(1)} %get-tuple-element.60.x_ref, ...), custom_call_target="tpu_custom_call" | custom-call | tf_op jit(solution)/shard_map/pallas_call | solution.py:290
  31.3 2.3 %collective-permute-start.4 = (f32[16,640]{1,0:T(8,128)S(1)}, f32[16,640]{1,0:T(8,128)S(1)}, u32[]{:S(2)}, u32[]{:S(2)}) collective-permute-start(f32[16,640]{1,0:T(8,128)S(1)} %get-tuple-element.67), channel_id=1, source_target_pairs={{0,8},{8,16},{16,24},{24,32},{32,40},{40,48},{48,56},{56,64},{64,7... | collective-permute-start | bytes 122888 | tf_op jit(solution)/shard_map/ppermute | solution.py:301
  33.6 5.9 %collective-permute-start.5 = (f32[16,384]{1,0:T(8,128)S(1)}, f32[16,384]{1,0:T(8,128)S(1)}, u32[]{:S(2)}, u32[]{:S(2)}) collective-permute-start(f32[16,384]{1,0:T(8,128)S(1)} %get-tuple-element.68), channel_id=1, source_target_pairs={{0,504},{8,0},{16,8},{24,16},{32,24},{40,32},{48,40},{56,48},{64,5... | collective-permute-start | bytes 73736 | tf_op jit(solution)/shard_map/ppermute | solution.py:301
  39.5 1.5 collective-permute-done.5.down_ref
  41.0 2.5 %shard_map.108 = (f32[16,1024]{1,0:T(8,128)S(1)}, f32[64,512]{1,0:T(8,128)S(1)}, f32[16,256]{1,0:T(8,128)S(1)}, f32[16,640]{1,0:T(8,128)S(1)}, f32[16,384]{1,0:T(8,128)S(1)}) custom-call(f32[16,1024]{1,0:T(8,128)S(1)} %get-tuple-element.64.v_ref.prev_ref, f32[16,1024]{1,0:T(8,128)S(1)} %get-tuple-element.59.v_ref.prev_ref, ...), custom_call_target="tpu_custom_call" | custom-call | tf_op jit(solution)/shard_map/pallas_call | solution.py:290
  43.5 4.1 %collective-permute-start.6 = (f32[16,640]{1,0:T(8,128)S(1)}, f32[16,640]{1,0:T(8,128)S(1)}, u32[]{:S(2)}, u32[]{:S(2)}) collective-permute-start(f32[16,640]{1,0:T(8,128)S(1)} %get-tuple-element.72), channel_id=1, source_target_pairs={{0,8},{8,16},{16,24},{24,32},{32,40},{40,48},{48,56},{56,64},{64,7... | collective-permute-start | bytes 122888 | tf_op jit(solution)/shard_map/ppermute | solution.py:301
  47.6 4.2 %collective-permute-start.7 = (f32[16,384]{1,0:T(8,128)S(1)}, f32[16,384]{1,0:T(8,128)S(1)}, u32[]{:S(2)}, u32[]{:S(2)}) collective-permute-start(f32[16,384]{1,0:T(8,128)S(1)} %get-tuple-element.73), channel_id=1, source_target_pairs={{0,504},{8,0},{16,8},{24,16},{32,24},{40,32},{48,40},{56,48},{64,5... | collective-permute-start | bytes 73736 | tf_op jit(solution)/shard_map/ppermute | solution.py:301
  51.8 1.5 %collective-permute-done.7.down_ref = f32[16,384]{1,0:T(8,128)S(1)} collective-permute-done((f32[16,384]{1,0:T(8,128)S(1)}, f32[16,384]{1,0:T(8,128)S(1)}, u32[]{:S(2)}, u32[]{:S(2)}) %collective-permute-start.7) | collective-permute-done | bytes 24608 | tf_op jit(solution)/shard_map/ppermute | solution.py:301
  53.3 2.5 %shard_map.109 = (f32[16,1024]{1,0:T(8,128)S(1)}, f32[64,512]{1,0:T(8,128)S(1)}, f32[16,256]{1,0:T(8,128)S(1)}, f32[16,640]{1,0:T(8,128)S(1)}, f32[16,384]{1,0:T(8,128)S(1)}) custom-call(f32[16,1024]{1,0:T(8,128)S(1)} %get-tuple-element.69.v_ref.prev_ref, f32[16,1024]{1,0:T(8,128)S(1)} %get-tuple-element.64.v_ref.prev_ref, ...), custom_call_target="tpu_custom_call" | custom-call | tf_op jit(solution)/shard_map/pallas_call | solution.py:290
  55.8 4.0 %collective-permute-start.8 = (f32[16,640]{1,0:T(8,128)S(1)}, f32[16,640]{1,0:T(8,128)S(1)}, u32[]{:S(2)}, u32[]{:S(2)}) collective-permute-start(f32[16,640]{1,0:T(8,128)S(1)} %get-tuple-element.77), channel_id=1, source_target_pairs={{0,8},{8,16},{16,24},{24,32},{32,40},{40,48},{48,56},{56,64},{64,7... | collective-permute-start | bytes 122888 | tf_op jit(solution)/shard_map/ppermute | solution.py:301
  59.9 4.4 %collective-permute-start.9 = (f32[16,384]{1,0:T(8,128)S(1)}, f32[16,384]{1,0:T(8,128)S(1)}, u32[]{:S(2)}, u32[]{:S(2)}) collective-permute-start(f32[16,384]{1,0:T(8,128)S(1)} %get-tuple-element.78), channel_id=1, source_target_pairs={{0,504},{8,0},{16,8},{24,16},{32,24},{40,32},{48,40},{56,48},{64,5... | collective-permute-start | bytes 73736 | tf_op jit(solution)/shard_map/ppermute | solution.py:301
  64.2 1.4 collective-permute-done.9.down_ref
  65.6 2.5 %shard_map.110 = (f32[16,1024]{1,0:T(8,128)S(1)}, f32[64,512]{1,0:T(8,128)S(1)}, f32[16,256]{1,0:T(8,128)S(1)}, f32[16,640]{1,0:T(8,128)S(1)}, f32[16,384]{1,0:T(8,128)S(1)}) custom-call(f32[16,1024]{1,0:T(8,128)S(1)} %get-tuple-element.74.v_ref.prev_ref, f32[16,1024]{1,0:T(8,128)S(1)} %get-tuple-element.69.v_ref.prev_ref, ...), custom_call_target="tpu_custom_call" | custom-call | tf_op jit(solution)/shard_map/pallas_call | solution.py:290
  68.1 4.0 %collective-permute-start.10 = (f32[16,640]{1,0:T(8,128)S(1)}, f32[16,640]{1,0:T(8,128)S(1)}, u32[]{:S(2)}, u32[]{:S(2)}) collective-permute-start(f32[16,640]{1,0:T(8,128)S(1)} %get-tuple-element.82), channel_id=1, source_target_pairs={{0,8},{8,16},{16,24},{24,32},{32,40},{40,48},{48,56},{56,64},{64,7... | collective-permute-start | bytes 122888 | tf_op jit(solution)/shard_map/ppermute | solution.py:301
  72.1 4.2 %collective-permute-start.11 = (f32[16,384]{1,0:T(8,128)S(1)}, f32[16,384]{1,0:T(8,128)S(1)}, u32[]{:S(2)}, u32[]{:S(2)}) collective-permute-start(f32[16,384]{1,0:T(8,128)S(1)} %get-tuple-element.83), channel_id=1, source_target_pairs={{0,504},{8,0},{16,8},{24,16},{32,24},{40,32},{48,40},{56,48},{64,5... | collective-permute-start | bytes 73736 | tf_op jit(solution)/shard_map/ppermute | solution.py:301
  76.3 1.5 %collective-permute-done.11.down_ref = f32[16,384]{1,0:T(8,128)S(1)} collective-permute-done((f32[16,384]{1,0:T(8,128)S(1)}, f32[16,384]{1,0:T(8,128)S(1)}, u32[]{:S(2)}, u32[]{:S(2)}) %collective-permute-start.11) | collective-permute-done | bytes 24608 | tf_op jit(solution)/shard_map/ppermute | solution.py:301
  77.8 3.0 %shard_map.111 = (f32[16,1024]{1,0:T(8,128)}, f32[64,512]{1,0:T(8,128)S(1)}, f32[16,256]{1,0:T(8,128)S(1)}, f32[16,640]{1,0:T(8,128)S(1)}, f32[16,384]{1,0:T(8,128)S(1)}) custom-call(f32[16,1024]{1,0:T(8,128)S(1)} %get-tuple-element.79.v_ref, f32[16,1024]{1,0:T(8,128)S(1)} %get-tuple-element.74.v_ref.prev_ref, f32[64,512]{1,0:T(8,128)S(1)} %get-tuple-element.80.x_ref, ...), custom_call_target="tpu_custom_call" | custom-call | tf_op jit(solution)/shard_map/pallas_call | solution.py:290
  80.9 1.7 %broadcast_in_dim.2 = f32[8,16,1024]{2,1,0:T(8,128)} broadcast(f32[16,1024]{1,0:T(8,128)} %get-tuple-element.44.v_ref), dimensions={1,2} | broadcast | bytes 589824 | tf_op jit(solution)/shard_map/broadcast_in_dim | solution.py:340
  82.6 4.4 %all-to-all-start = ((f32[8,16,1024]{2,1,0:T(8,128)}), f32[8,16,1024]{2,1,0:T(8,128)S(1)}, u32[]{:S(2)}, u32[]{:S(2)}) async-start(f32[8,16,1024]{2,1,0:T(8,128)} %broadcast_in_dim.2), calls=%async_computation | async-start | bytes 1048576 | tf_op jit(solution)/shard_map/all_to_all | solution.py:340
  87.0 4.0 %collective-permute-start.12 = (f32[16,640]{1,0:T(8,128)S(1)}, f32[16,640]{1,0:T(8,128)S(1)}, u32[]{:S(2)}, u32[]{:S(2)}) collective-permute-start(f32[16,640]{1,0:T(8,128)S(1)} %get-tuple-element.87), channel_id=1, source_target_pairs={{0,8},{8,16},{16,24},{24,32},{32,40},{40,48},{48,56},{56,64},{64,7... | collective-permute-start | bytes 122888 | tf_op jit(solution)/shard_map/ppermute | solution.py:301
  91.0 4.2 %collective-permute-start.13 = (f32[16,384]{1,0:T(8,128)S(1)}, f32[16,384]{1,0:T(8,128)S(1)}, u32[]{:S(2)}, u32[]{:S(2)}) collective-permute-start(f32[16,384]{1,0:T(8,128)S(1)} %get-tuple-element.88), channel_id=1, source_target_pairs={{0,504},{8,0},{16,8},{24,16},{32,24},{40,32},{48,40},{56,48},{64,5... | collective-permute-start | bytes 73736 | tf_op jit(solution)/shard_map/ppermute | solution.py:301
  95.2 1.5 %collective-permute-done.13.down_ref = f32[16,384]{1,0:T(8,128)S(1)} collective-permute-done((f32[16,384]{1,0:T(8,128)S(1)}, f32[16,384]{1,0:T(8,128)S(1)}, u32[]{:S(2)}, u32[]{:S(2)}) %collective-permute-start.13) | collective-permute-done | bytes 24608 | tf_op jit(solution)/shard_map/ppermute | solution.py:301
  96.8 0.6 all-to-all-done
  97.4 2.3 %shard_map.112 = f32[4,32,128]{2,1,0:T(8,128)S(1)} custom-call(f32[16,1024]{1,0:T(8,128)S(1)} %copy-done.3, f32[128,1024]{1,0:T(8,128)S(1)} %bitcast.7, f32[64,512]{1,0:T(8,128)S(1)} %get-tuple-element.85.x_ref, f32[16,256]{1,0:T(8,128)S(1)} %get-tuple-element.86.g_ref, f32[16,640]{1,0:T(8,128)S(1)} %collective-permute-done.12.up_ref, ...), custom_call_target="tpu_custom_call" | custom-call | tf_op jit(solution)/shard_map/pallas_call | solution.py:290
  99.7 12.1 %all_to_all.15.parts_ref = f32[4,32,128]{2,1,0:T(8,128)S(1)} all-to-all(f32[4,32,128]{2,1,0:T(8,128)S(1)} %shard_map.112), channel_id=1, replica_groups={{0,8,16,24},{32,40,48,56},{64,72,80,88},{96,104,112,120},{128,136,144,1..., dimensions={0} | all-to-all | bytes 131072 | tf_op jit(solution)/shard_map/all_to_all | solution.py:351
  111.8 38.3 %all_to_all.16.parts_ref = f32[16,32,128]{2,1,0:T(8,128)S(1)} all-to-all(f32[16,32,128]{2,1,0:T(8,128)S(1)} %shard_map.113), channel_id=1, replica_groups={{0,32,64,96,128,160,192,224,256,288,320,352,384,416,448,480},{8,40,72,1..., dimensions={0} | all-to-all | bytes 524288 | tf_op jit(solution)/shard_map/all_to_all | solution.py:353
  150.1 0.6 shard_map.114
  (16 shorter events, 0.1 us)
Async XLA Ops:
  0.6 1.0 copy-start.2
  0.6 1.0 copy-start
  1.6 0.7 copy-start.5
  1.7 0.7 copy-start.6
  2.3 9.2 %copy-start.7 = (f32[512,18]{0,1:T(8,128)S(1)}, f32[512,18]{0,1:T(8,128)}, u32[]{:S(2)}) copy-start(f32[512,18]{0,1:T(8,128)} %param.12) | copy-start | bytes 110596
  3.5 11.6 %collective-permute-start = (f32[48,640]{1,0:T(8,128)S(1)}, f32[48,640]{1,0:T(8,128)S(1)}, u32[]{:S(2)}, u32[]{:S(2)}) collective-permute-start(f32[48,640]{1,0:T(8,128)S(1)} %get-tuple-element.49), channel_id=1, source_target_pairs={{0,8},{8,16},{16,24},{24,32},{32,40},{40,48},{48,56},{56,64},{64,7... | collective-permute-start | bytes 368648 | tf_op jit(solution)/shard_map/ppermute | solution.py:301
  7.0 8.1 %collective-permute-start.1 = (f32[24,384]{1,0:T(8,128)S(1)}, f32[24,384]{1,0:T(8,128)S(1)}, u32[]{:S(2)}, u32[]{:S(2)}) collective-permute-start(f32[24,384]{1,0:T(8,128)S(1)} %get-tuple-element.50), channel_id=1, source_target_pairs={{0,504},{8,0},{16,8},{24,16},{32,24},{40,32},{48,40},{56,48},{64,5... | collective-permute-start | bytes 110600 | tf_op jit(solution)/shard_map/ppermute | solution.py:301
  11.7 1.2 copy-start.1
  16.1 0.7 copy-start.4
  19.3 9.5 %collective-permute-start.2 = (f32[16,640]{1,0:T(8,128)S(1)}, f32[16,640]{1,0:T(8,128)S(1)}, u32[]{:S(2)}, u32[]{:S(2)}) collective-permute-start(f32[16,640]{1,0:T(8,128)S(1)} %get-tuple-element.62), channel_id=1, source_target_pairs={{0,8},{8,16},{16,24},{24,32},{32,40},{40,48},{48,56},{56,64},{64,7... | collective-permute-start | bytes 122888 | tf_op jit(solution)/shard_map/ppermute | solution.py:301
  21.2 7.5 %collective-permute-start.3 = (f32[16,384]{1,0:T(8,128)S(1)}, f32[16,384]{1,0:T(8,128)S(1)}, u32[]{:S(2)}, u32[]{:S(2)}) collective-permute-start(f32[16,384]{1,0:T(8,128)S(1)} %get-tuple-element.63), channel_id=1, source_target_pairs={{0,504},{8,0},{16,8},{24,16},{32,24},{40,32},{48,40},{56,48},{64,5... | collective-permute-start | bytes 73736 | tf_op jit(solution)/shard_map/ppermute | solution.py:301
  31.3 9.8 %collective-permute-start.4 = (f32[16,640]{1,0:T(8,128)S(1)}, f32[16,640]{1,0:T(8,128)S(1)}, u32[]{:S(2)}, u32[]{:S(2)}) collective-permute-start(f32[16,640]{1,0:T(8,128)S(1)} %get-tuple-element.67), channel_id=1, source_target_pairs={{0,8},{8,16},{16,24},{24,32},{32,40},{40,48},{48,56},{56,64},{64,7... | collective-permute-start | bytes 122888 | tf_op jit(solution)/shard_map/ppermute | solution.py:301
  33.6 7.4 %collective-permute-start.5 = (f32[16,384]{1,0:T(8,128)S(1)}, f32[16,384]{1,0:T(8,128)S(1)}, u32[]{:S(2)}, u32[]{:S(2)}) collective-permute-start(f32[16,384]{1,0:T(8,128)S(1)} %get-tuple-element.68), channel_id=1, source_target_pairs={{0,504},{8,0},{16,8},{24,16},{32,24},{40,32},{48,40},{56,48},{64,5... | collective-permute-start | bytes 73736 | tf_op jit(solution)/shard_map/ppermute | solution.py:301
  43.5 9.8 %collective-permute-start.6 = (f32[16,640]{1,0:T(8,128)S(1)}, f32[16,640]{1,0:T(8,128)S(1)}, u32[]{:S(2)}, u32[]{:S(2)}) collective-permute-start(f32[16,640]{1,0:T(8,128)S(1)} %get-tuple-element.72), channel_id=1, source_target_pairs={{0,8},{8,16},{16,24},{24,32},{32,40},{40,48},{48,56},{56,64},{64,7... | collective-permute-start | bytes 122888 | tf_op jit(solution)/shard_map/ppermute | solution.py:301
  47.6 5.7 %collective-permute-start.7 = (f32[16,384]{1,0:T(8,128)S(1)}, f32[16,384]{1,0:T(8,128)S(1)}, u32[]{:S(2)}, u32[]{:S(2)}) collective-permute-start(f32[16,384]{1,0:T(8,128)S(1)} %get-tuple-element.73), channel_id=1, source_target_pairs={{0,504},{8,0},{16,8},{24,16},{32,24},{40,32},{48,40},{56,48},{64,5... | collective-permute-start | bytes 73736 | tf_op jit(solution)/shard_map/ppermute | solution.py:301
  55.8 9.8 %collective-permute-start.8 = (f32[16,640]{1,0:T(8,128)S(1)}, f32[16,640]{1,0:T(8,128)S(1)}, u32[]{:S(2)}, u32[]{:S(2)}) collective-permute-start(f32[16,640]{1,0:T(8,128)S(1)} %get-tuple-element.77), channel_id=1, source_target_pairs={{0,8},{8,16},{16,24},{24,32},{32,40},{40,48},{48,56},{56,64},{64,7... | collective-permute-start | bytes 122888 | tf_op jit(solution)/shard_map/ppermute | solution.py:301
  59.9 5.7 %collective-permute-start.9 = (f32[16,384]{1,0:T(8,128)S(1)}, f32[16,384]{1,0:T(8,128)S(1)}, u32[]{:S(2)}, u32[]{:S(2)}) collective-permute-start(f32[16,384]{1,0:T(8,128)S(1)} %get-tuple-element.78), channel_id=1, source_target_pairs={{0,504},{8,0},{16,8},{24,16},{32,24},{40,32},{48,40},{56,48},{64,5... | collective-permute-start | bytes 73736 | tf_op jit(solution)/shard_map/ppermute | solution.py:301
  68.1 9.8 %collective-permute-start.10 = (f32[16,640]{1,0:T(8,128)S(1)}, f32[16,640]{1,0:T(8,128)S(1)}, u32[]{:S(2)}, u32[]{:S(2)}) collective-permute-start(f32[16,640]{1,0:T(8,128)S(1)} %get-tuple-element.82), channel_id=1, source_target_pairs={{0,8},{8,16},{16,24},{24,32},{32,40},{40,48},{48,56},{56,64},{64,7... | collective-permute-start | bytes 122888 | tf_op jit(solution)/shard_map/ppermute | solution.py:301
  72.1 5.7 %collective-permute-start.11 = (f32[16,384]{1,0:T(8,128)S(1)}, f32[16,384]{1,0:T(8,128)S(1)}, u32[]{:S(2)}, u32[]{:S(2)}) collective-permute-start(f32[16,384]{1,0:T(8,128)S(1)} %get-tuple-element.83), channel_id=1, source_target_pairs={{0,504},{8,0},{16,8},{24,16},{32,24},{40,32},{48,40},{56,48},{64,5... | collective-permute-start | bytes 73736 | tf_op jit(solution)/shard_map/ppermute | solution.py:301
  82.6 14.8 %copy-start.3 = (f32[16,1024]{1,0:T(8,128)S(1)}, f32[16,1024]{1,0:T(8,128)}, u32[]{:S(2)}) copy-start(f32[16,1024]{1,0:T(8,128)} %get-tuple-element.44.v_ref) | copy-start | bytes 196612
  82.6 14.8 %all-to-all-start = ((f32[8,16,1024]{2,1,0:T(8,128)}), f32[8,16,1024]{2,1,0:T(8,128)S(1)}, u32[]{:S(2)}, u32[]{:S(2)}) async-start(f32[8,16,1024]{2,1,0:T(8,128)} %broadcast_in_dim.2), calls=%async_computation | async-start | bytes 1048576 | tf_op jit(solution)/shard_map/all_to_all | solution.py:340
  87.0 9.7 %collective-permute-start.12 = (f32[16,640]{1,0:T(8,128)S(1)}, f32[16,640]{1,0:T(8,128)S(1)}, u32[]{:S(2)}, u32[]{:S(2)}) collective-permute-start(f32[16,640]{1,0:T(8,128)S(1)} %get-tuple-element.87), channel_id=1, source_target_pairs={{0,8},{8,16},{16,24},{24,32},{32,40},{40,48},{48,56},{56,64},{64,7... | collective-permute-start | bytes 122888 | tf_op jit(solution)/shard_map/ppermute | solution.py:301
  91.0 5.7 %collective-permute-start.13 = (f32[16,384]{1,0:T(8,128)S(1)}, f32[16,384]{1,0:T(8,128)S(1)}, u32[]{:S(2)}, u32[]{:S(2)}) collective-permute-start(f32[16,384]{1,0:T(8,128)S(1)} %get-tuple-element.88), channel_id=1, source_target_pairs={{0,504},{8,0},{16,8},{24,16},{32,24},{40,32},{48,40},{56,48},{64,5... | collective-permute-start | bytes 73736 | tf_op jit(solution)/shard_map/ppermute | solution.py:301

commit v3 on v2

v3 whole, which is shorter than its diff:
```python
import functools

import jax
import jax.numpy as jnp
from jax import lax
from jax.experimental import pallas as pl
from jax.experimental.pallas import tpu as pltpu
from jax.sharding import PartitionSpec as P

NPROJ = 18
ATOM_DEV = 8
DEGREE = 6
CENTER = 0.9
HALF_WIDTH = 1.1
BANDS = 16
NODES = 1024
NPC = 512
GHOST = 256
LANES = 128
SLOT = 32
F32 = jnp.float32
BF16 = jnp.bfloat16


def dot(a, b):
    return lax.dot_general(a, b, (((1,), (0,)), ((), ())), preferred_element_type=F32)


def dot_nt(a, b):
    return lax.dot_general(a, b, (((1,), (1,)), ((), ())), preferred_element_type=F32)


def split2(x):
    high = x.astype(BF16)
    return high, (x - high.astype(F32)).astype(BF16)


def split3(x):
    high = x.astype(BF16)
    rest = x - high.astype(F32)
    mid = rest.astype(BF16)
    return high, mid, (rest - mid.astype(F32)).astype(BF16)


def product(x_high, x_low, w_high, w_low):
    rows = x_high.shape[0]
    both = dot(jnp.concatenate([x_high, x_low], axis=0), w_high)
    return both[:rows] + both[rows:] + dot(x_high, w_low)


def blocks_of(x):
    return [x[:, i : i + LANES] for i in range(0, x.shape[1], LANES)]


def pick(sources, index, first=0):
    rows = sources[0].shape[0]
    index = jnp.broadcast_to(index, (rows, LANES))
    lane = index & (LANES - 1)
    block = index >> 7
    total = jnp.zeros((rows, LANES), F32)
    for k, source in enumerate(sources):
        value = jnp.take_along_axis(source, lane, axis=1, mode="promise_in_bounds")
        total = jnp.where(block == first + k, value, total)
    return total


def pick_row(sources, index, first=0):
    return jnp.concatenate([pick(sources, i, first) for i in blocks_of(index)], axis=1)


def column(row):
    return jnp.broadcast_to(row, (LANES, row.shape[1])).T


def lane_iota(rows, lanes):
    return lax.broadcasted_iota(jnp.int32, (rows, lanes), 1)


def row_iota(rows, lanes):
    return lax.broadcasted_iota(jnp.int32, (rows, lanes), 0)


def padded_projectors(cell):
    return jnp.concatenate([cell, jnp.zeros((SLOT - NPROJ, NPC), F32)], axis=0)


def pack_message(vectors, partials, conn_ref, send_ref, up_ref, down_ref):
    sources = blocks_of(vectors)
    up_ref[0:BANDS, 0:NPC] = pick_row(sources, conn_ref[3:4, :])
    up_ref[0:BANDS, NPC:] = partials
    down_ref[0:BANDS, 0:GHOST] = pick_row(sources, send_ref[...])
    down_ref[0:BANDS, GHOST:] = partials


def first_kernel(v_ref, conn_ref, send_ref, atom_ref, proj_ref, up_ref, down_ref):
    v = v_ref[...]
    sources = blocks_of(v)
    cells = [pick_row(sources, conn_ref[c : c + 1, :]) for c in range(3)]
    stacked = [padded_projectors(proj_ref[:, c, :]) for c in range(3)] + [jnp.zeros((SLOT, NPC), F32)]
    t_high, t_low = split2(jnp.concatenate(stacked, axis=0).T)
    x_high, x_low = split2(jnp.concatenate(cells, axis=0))
    wide = product(x_high, x_low, t_high, t_low)
    which = lane_iota(BANDS, LANES) >> 5
    partials = jnp.zeros((BANDS, LANES), F32)
    for c in range(3):
        partials = jnp.where(which == c, wide[c * BANDS : (c + 1) * BANDS], partials)
    which = lane_iota(1, LANES) >> 5
    atoms = jnp.zeros((1, LANES), F32)
    for c in range(4):
        atoms = jnp.where(which == c, atom_ref[c].astype(F32), atoms)
    edge = conn_ref[3:4, :]
    names = column(edge.astype(F32))
    position = row_iota(NPC, LANES).astype(F32)
    inverse = []
    for k in range(GHOST // LANES):
        slot = (lane_iota(NPC, LANES) + (NODES + k * LANES)).astype(F32)
        inverse.append(jnp.max(jnp.where(names == slot, position, -1.0), axis=0, keepdims=True))
    up_ref[...] = jnp.zeros_like(up_ref)
    down_ref[...] = jnp.zeros_like(down_ref)
    pack_message(v, partials, conn_ref, send_ref, up_ref, down_ref)
    up_ref[16 : 16 + NPROJ, 0:NPC] = proj_ref[:, 3, :]
    up_ref[40:41, 0:NPC] = edge.astype(F32)
    up_ref[41:42, 0:GHOST] = jnp.concatenate(inverse, axis=1)
    up_ref[42:43, 0:LANES] = atoms
    down_ref[16:17, 0:LANES] = atoms


def local_kernel(conn_ref, send_ref, element_ref, proj_ref, down_ref, e_ref, maps_ref, p_ref, pt_ref, downo_ref):
    downo_ref[...] = down_ref[...]
    high, low = split2(element_ref[...])
    e_ref[0] = high
    e_ref[1] = low
    least = [jnp.full((1, LANES), 4.0 * NPC, F32)] * (NODES // LANES)
    most = [jnp.full((1, LANES), -1.0, F32)] * (NODES // LANES)
    position = row_iota(NPC, LANES).astype(F32)
    node = lane_iota(NPC, LANES).astype(F32)
    for c in range(4):
        names = column(conn_ref[c : c + 1, :].astype(F32))
        place = position + float(c * NPC)
        thirds = jnp.concatenate(split3(padded_projectors(proj_ref[:, c, :])), axis=0)
        for k in range(0, NODES // LANES, 2):
            hits = []
            for j in (k, k + 1):
                same = names == node + float(j * LANES)
                least[j] = jnp.minimum(least[j], jnp.min(jnp.where(same, place, 4.0 * NPC), axis=0, keepdims=True))
                most[j] = jnp.maximum(most[j], jnp.max(jnp.where(same, place, -1.0), axis=0, keepdims=True))
                hits.append(jnp.where(same, 1.0, 0.0).astype(BF16))
            parts = dot(thirds, jnp.concatenate(hits, axis=1))
            p_ref[c * SLOT : (c + 1) * SLOT, k * LANES : (k + 2) * LANES] = parts[:SLOT] + parts[SLOT : 2 * SLOT] + parts[2 * SLOT :]
    inner = jnp.concatenate([p_ref[0 : 3 * SLOT, :], jnp.zeros((SLOT, NODES), F32)], axis=0)
    pt_ref[0], pt_ref[1] = split2(inner.T)
    names = column(send_ref[...].astype(F32))
    maps_ref[...] = jnp.zeros_like(maps_ref)
    for k in range(NODES // LANES):
        here = slice(k * LANES, (k + 1) * LANES)
        maps_ref[0:1, here] = least[k].astype(jnp.int32)
        maps_ref[1:2, here] = jnp.where(most[k] > least[k], most[k], -1.0).astype(jnp.int32)
        same = names == node[:GHOST] + float(k * LANES)
        maps_ref[2:3, here] = jnp.max(jnp.where(same, position[:GHOST], -1.0), axis=0, keepdims=True).astype(jnp.int32)


def joined_kernel(up_ref, down_ref, maps_ref, atom_ref, place_ref, proj_ref, coupling_ref, pn_ref, p_ref, pe_ref, k_ref, coup_ref, index_ref):
    low_atoms, high_atoms = up_ref[42:43, 0:LANES], down_ref[16:17, 0:LANES]
    which = lane_iota(1, LANES) >> 5
    own = jnp.full((1, LANES), -100.0, F32)
    for c in range(4):
        own = jnp.where(which == c, atom_ref[c].astype(F32), own)
    edge_low = jnp.broadcast_to(low_atoms[:, 96:97] - float(ATOM_DEV), (1, LANES))
    edges = jnp.where(which == 0, atom_ref[3].astype(F32), jnp.where(which == 1, edge_low, -200.0))
    from_upper = jnp.where(which < 3, high_atoms + float(ATOM_DEV), -300.0)
    from_lower = jnp.where(which < 3, low_atoms - float(ATOM_DEV), -400.0)
    source = jnp.concatenate([jnp.where(which < 3, own, -500.0), edges, from_upper, from_lower], axis=1)
    inside = (lane_iota(SLOT, 4 * LANES) & (SLOT - 1)) == row_iota(SLOT, 4 * LANES)
    rows = []
    for c in range(5):
        if c < 4:
            same = source == atom_ref[c].astype(F32)
        else:
            same = source == jnp.concatenate([edge_low] * 4, axis=1)
        rows.append(jnp.where(inside & jnp.broadcast_to(same, inside.shape), 1.0, 0.0))
    rows.append(jnp.zeros((3 * SLOT, 4 * LANES), F32))
    k_ref[...] = jnp.concatenate(rows, axis=0).T.astype(BF16)
    lower = coupling_ref[pl.ds(pl.multiple_of(place_ref[0] * ATOM_DEV, ATOM_DEV), ATOM_DEV), :]
    mine = coupling_ref[pl.ds(pl.multiple_of(place_ref[1] * ATOM_DEV, ATOM_DEV), ATOM_DEV), :]
    pair = jnp.concatenate([lower, mine], axis=0)
    pair = jnp.concatenate([pair, jnp.zeros((2 * ATOM_DEV, SLOT - NPROJ), F32)], axis=1)
    wide = jnp.concatenate([pair] * 8, axis=1)
    target = jnp.concatenate([own, jnp.where(which == 0, edge_low, -200.0)], axis=1)
    slot = row_iota(2 * ATOM_DEV, 2 * LANES).astype(F32)
    chosen = jnp.where(jnp.broadcast_to(target, slot.shape) == slot, wide, 0.0)
    coup_ref[...] = jnp.broadcast_to(jnp.sum(chosen, axis=0, keepdims=True), coup_ref.shape)
    low = padded_projectors(up_ref[16 : 16 + NPROJ, 0:NPC])
    stacked = jnp.concatenate([padded_projectors(proj_ref[:, 3, :]), low, jnp.zeros((2 * SLOT, NPC), F32)], axis=0)
    pe_ref[0], pe_ref[1] = split2(stacked.T)
    index_ref[...] = jnp.zeros_like(index_ref)
    index_ref[0:2, :] = maps_ref[0:2, :]
    sent = maps_ref[2:3, :]
    rows8 = [jnp.broadcast_to(b, (8, LANES)) for b in blocks_of(up_ref[41:42, 0:GHOST])]
    third = pick_row(rows8, sent)
    third = jnp.where(jnp.broadcast_to(sent, third.shape) >= 0, third, -1.0)[0:1].astype(jnp.int32)
    index_ref[2:3, :] = third
    index_ref[3:4, 0:NPC] = up_ref[40:41, 0:NPC].astype(jnp.int32) - NODES
    spread = jnp.concatenate([pn_ref[...], pick_row(blocks_of(low), third), jnp.zeros((3 * SLOT, NODES), F32)], axis=0)
    p_ref[0], p_ref[1] = split2(spread)


def inner_kernel(mode, v_ref, prev_ref, conn_ref, maps_ref, pot_ref, e_ref, base_ref):
    v = v_ref[...]
    sources = blocks_of(v)
    cells = [pick_row(sources, conn_ref[c : c + 1, :]) for c in range(3)]
    x_high, x_low = split2(jnp.concatenate(cells, axis=0))
    y = product(x_high, x_low, e_ref[0], e_ref[1])
    blocks = []
    for c in range(3):
        blocks += blocks_of(y[c * BANDS : (c + 1) * BANDS])
    for k in range(NODES // LANES):
        here = slice(k * LANES, (k + 1) * LANES)
        h = pick(blocks, maps_ref[0:1, here]) + pick(blocks, maps_ref[1:2, here]) + pot_ref[:, here] * v[:, here]
        if mode == "first":
            h = (h - CENTER * v[:, here]) * (1.0 / HALF_WIDTH)
        elif mode == "middle":
            h = (h - CENTER * v[:, here]) * (2.0 / HALF_WIDTH) - prev_ref[:, here]
        base_ref[:, here] = h


def outer(ups_ref, downs_ref, up_ref, down_ref, conn_ref, index_ref, e_ref, p_ref, pe_ref, k_ref, coup_ref):
    edge = ups_ref[0:BANDS, 0:NPC] + pick_row(blocks_of(down_ref[0:BANDS, 0:GHOST]), conn_ref[3:4, :] - NODES)
    low = up_ref[0:BANDS, 0:NPC] + pick_row(blocks_of(downs_ref[0:BANDS, 0:GHOST]), index_ref[3:4, 0:NPC])
    x_high, x_low = split2(jnp.concatenate([edge, low], axis=0))
    wide = product(x_high, x_low, pe_ref[0], pe_ref[1])
    which = lane_iota(BANDS, LANES) >> 5
    edges = jnp.where(which == 0, wide[:BANDS], jnp.where(which == 1, wide[BANDS:], 0.0))
    partials = jnp.concatenate([ups_ref[0:BANDS, NPC:], edges, down_ref[0:BANDS, GHOST:], up_ref[0:BANDS, NPC:]], axis=1)
    sums = dot(jnp.concatenate(split3(partials), axis=0), k_ref[...])
    w_high, w_low = split2((sums[0:16] + sums[16:32] + sums[32:48]) * coup_ref[0:1, :])
    nonlocal_part = product(w_high, w_low, p_ref[0], p_ref[1])
    y = product(x_high, x_low, e_ref[0], e_ref[1])
    own, other = blocks_of(y[:BANDS]), blocks_of(y[BANDS:])
    out = []
    for k in range(NODES // LANES):
        here = slice(k * LANES, (k + 1) * LANES)
        total = pick(own, index_ref[0:1, here], 12) + pick(own, index_ref[1:2, here], 12)
        out.append(total + pick(other, index_ref[2:3, here]))
    return jnp.concatenate(out, axis=1) + nonlocal_part


def outer_kernel(factor, base_ref, ups_ref, downs_ref, up_ref, down_ref, conn_ref, index_ref, e_ref, p_ref, pe_ref, k_ref, coup_ref,
                 send_ref, pt_ref, new_ref, upo_ref, downo_ref):
    h = outer(ups_ref, downs_ref, up_ref, down_ref, conn_ref, index_ref, e_ref, p_ref, pe_ref, k_ref, coup_ref)
    new = base_ref[...] + h * factor
    new_ref[...] = new
    v_high, v_low = split2(new)
    pack_message(new, product(v_high, v_low, pt_ref[0], pt_ref[1]), conn_ref, send_ref, upo_ref, downo_ref)


def gram_kernel(base_ref, ups_ref, downs_ref, up_ref, down_ref, conn_ref, index_ref, e_ref, p_ref, pe_ref, k_ref, coup_ref,
                v_ref, all_ref, out_ref):
    h = base_ref[...] + outer(ups_ref, downs_ref, up_ref, down_ref, conn_ref, index_ref, e_ref, p_ref, pe_ref, k_ref, coup_ref)
    s_high, s_low = split2(jnp.concatenate([h, v_ref[...]], axis=0))
    a_high, a_low = split2(all_ref[...])
    both = dot_nt(jnp.concatenate([s_high, s_low], axis=0), a_high)
    panel = both[:32] + both[32:] + dot_nt(s_high, a_low)
    for i in range(out_ref.shape[0]):
        out_ref[i] = panel


def add_kernel(parts_ref, out_ref):
    total = parts_ref[0]
    for i in range(1, parts_ref.shape[0]):
        total = total + parts_ref[i]
    for i in range(out_ref.shape[0]):
        out_ref[i] = total


def last_kernel(scale, parts_ref, projected_ref, correlation_ref):
    total = parts_ref[0]
    for i in range(1, parts_ref.shape[0]):
        total = total + parts_ref[i]
    projected_ref[...] = total[0:BANDS] * scale
    correlation_ref[...] = total[BANDS:] * scale


VM = pl.BlockSpec(memory_space=pltpu.VMEM)
SM = pl.BlockSpec(memory_space=pltpu.SMEM)


def call(kernel, outs, ins, *args):
    return pl.pallas_call(
        kernel,
        out_shape=[jax.ShapeDtypeStruct(s, t) for s, t in outs],
        in_specs=ins,
        out_specs=[VM] * len(outs),
        compiler_params=pltpu.CompilerParams(vmem_limit_bytes=40 * 2**20),
    )(*args)


def shifted(block, distance):
    size = lax.axis_size("fe")
    return lax.ppermute(block, "fe", [(i, (i + distance) % size) for i in range(size)])


def on_device(wavefunctions, potential, element_matrix, projectors, coupling, connectivity, send_list, atom_of_cell):
    fe_count = lax.axis_size("fe")
    fe = lax.axis_index("fe").astype(jnp.int32)
    place = jnp.stack([(fe + fe_count - 1) % fe_count, fe])
    send = send_list.reshape(1, GHOST)
    pot = potential.reshape(1, NODES)
    proj = projectors.transpose(1, 0, 2)
    ups, downs = call(
        first_kernel,
        [((48, 640), F32), ((24, 384), F32)],
        [VM, VM, VM, SM, VM],
        wavefunctions, connectivity, send, atom_of_cell, proj,
    )
    up = shifted(ups, 1)
    e, maps, pn, pt, downs = call(
        local_kernel,
        [((2, NPC, NPC), BF16), ((8, NODES), jnp.int32), ((4 * SLOT, NODES), F32), ((2, NODES, LANES), BF16), ((24, 384), F32)],
        [VM] * 5,
        connectivity, send, element_matrix, proj, downs,
    )
    down = shifted(downs, -1)

    def inner(mode, v, previous):
        return call(functools.partial(inner_kernel, mode), [((BANDS, NODES), F32)], [VM] * 6, v, previous, connectivity, maps, pot, e)[0]

    previous = current = wavefunctions
    base = inner("first", current, previous)
    p, pe, k, coup, index = call(
        joined_kernel,
        [((2, 256, NODES), BF16), ((2, NPC, LANES), BF16), ((512, 256), BF16), ((8, 256), F32), ((8, NODES), jnp.int32)],
        [VM, VM, VM, SM, SM, VM, VM, VM],
        up, down, maps, atom_of_cell, place, proj, coupling, pn,
    )
    shared = (connectivity, index, e, p, pe, k, coup)
    for step in range(DEGREE):
        last = step == DEGREE - 1
        new, ups, downs = call(
            functools.partial(outer_kernel, (1.0 if step == 0 else 2.0) / HALF_WIDTH),
            [((BANDS, NODES), F32), ((BANDS, 640), F32), ((BANDS, 384), F32)],
            [VM] * 14,
            base, ups, downs, up, down, *shared, send, pt,
        )
        previous, current = current, new
        if last:
            bands = lax.axis_size("band")
            everyone = lax.all_to_all(jnp.broadcast_to(current[None], (bands,) + current.shape), "band", 0, 0)
            everyone = everyone.reshape(-1, NODES)
        up, down = shifted(ups, 1), shifted(downs, -1)
        base = inner("last" if last else "middle", current, previous)
    (copies,) = call(
        gram_kernel,
        [((4, 32, LANES), F32)],
        [VM] * 14,
        base, ups, downs, up, down, *shared, current, everyone,
    )
    near = [[4 * i + j for j in range(4)] for i in range(fe_count // 4)]
    far = [[4 * i + j for i in range(fe_count // 4)] for j in range(4)]
    parts = lax.all_to_all(copies, "fe", 0, 0, axis_index_groups=near)
    (copies,) = call(add_kernel, [((fe_count // 4, 32, LANES), F32)], [VM], parts)
    parts = lax.all_to_all(copies, "fe", 0, 0, axis_index_groups=far)
    projected, correlation = call(
        functools.partial(last_kernel, 1.0 / (NODES * fe_count)),
        [((BANDS, LANES), F32), ((BANDS, LANES), F32)],
        [VM],
        parts,
    )
    return current, projected.T, correlation.T


def solution(mesh):
    in_specs = (
        P("band", "fe"),
        P("fe"),
        P(),
        P("fe", None, None),
        P(),
        P("fe", None),
        P("fe"),
        P("fe"),
    )
    out_specs = (P("band", "fe"), P(None, "band"), P(None, "band"))
    return jax.shard_map(on_device, mesh=mesh, in_specs=in_specs, out_specs=out_specs, check_vma=False)
```

time: 152 us -> 157 us (1.033)
  local copies, waits for them, and re-layouts: 5.38 us -> 12.9 us
  waiting for transfers between devices: 9.56 us -> 2.52 us
  Pallas kernels: 22.8 us -> 26.4 us
    unnamed x18 -> x49, local copies, waits for them, and re-layouts: 3.7 us -> 11.2 us
    ppermute x14, waiting for transfers between devices: 8.96 us -> 2.52 us  [shifted(): lax.ppermute(block, 'fe', [(i, (i + distance) % size) for i in range(size)])]
    pallas_call x12 -> x19, Pallas kernels: 22.8 us -> 26.4 us  [call(): pl.pallas_call(kernel, out_shape=[jax.ShapeDtypeStruct(s, t) for s, t in...]
  transfers between devices with their start and end apart: 15 -> 15, of which waited for: 7 -> 6; matrix products, arithmetic and copies ran while one was open for 0% -> 1% of each run, Pallas kernels for 1% -> 7%
where the time goes in v3:
time: 157 us; the launch traced here: 156 us
  starting transfers between devices  61.6 us (39%)
  blocking collectives  50.9 us (32%)
  Pallas kernels  26.4 us (17%)
  local copies, waits for them, and re-layouts  12.9 us (8%)
  waiting for transfers between devices  2.52 us (2%)
    ppermute x14, starting transfers between devices, shifted(): lax.ppermute(block, 'fe', [(i, (i + distance) % size) for i in range(size)])  57.2 us
    all_to_all x1, blocking collectives, on_device(): parts = lax.all_to_all(copies, 'fe', 0, 0, axis_index_groups=far)  38.3 us
    pallas_call x19, Pallas kernels, call(): pl.pallas_call(kernel, out_shape=[jax.ShapeDtypeStruct(s, t) for s, t in...  26.4 us
    all_to_all x1, blocking collectives, on_device(): parts = lax.all_to_all(copies, 'fe', 0, 0, axis_index_groups=near)  12.7 us
    unnamed x49, local copies, waits for them, and re-layouts  11.2 us
    all_to_all x1, starting transfers between devices, on_device(): lax.all_to_all(jnp.broadcast_to(current[None], (bands,) + current.shape),...  4.43 us
  transfers between devices with their start and end apart: 15, of which 6 were waited for; matrix products, arithmetic and copies ran while one was open for 1% of the time, Pallas kernels for 7%

profile of v3, /device:TPU:32, one launch (start us, length us, event | category | flops | bytes accessed | tf_op | source)
XLA Modules:
  0.0 155.9 jit_solution(1365591860107980736)
XLA Ops:
  0.7 0.7 copy-done.17
  1.3 0.7 copy-done
  2.0 0.9 copy-done.2
  2.9 0.8 copy-done.4
  3.8 1.8 %shard_map.103 = (f32[48,640]{1,0:T(8,128)}, f32[24,384]{1,0:T(8,128)S(1)}) custom-call(f32[16,1024]{1,0:T(8,128)S(1)} %copy-done.4, s32[4,512]{1,0:T(4,128)S(1)} %copy-done, s32[1,256]{1,0:T(1,128)S(1)} %bitcast.19, s32[4]{0:T(128)S(1)} %copy-done.21, f32[18,4,512]{2,1,0:T(4,128)S(1)} %bitcast.9), custom_call_target="tpu_custom_call" | custom-call | tf_op jit(solution)/shard_map/pallas_call | solution.py:288
  5.5 3.5 %collective-permute-start = (f32[48,640]{1,0:T(8,128)}, f32[48,640]{1,0:T(8,128)S(1)}, u32[]{:S(2)}, u32[]{:S(2)}) collective-permute-start(f32[48,640]{1,0:T(8,128)} %get-tuple-element.38.ups_ref), channel_id=1, source_target_pairs={{0,8},{8,16},{16,24},{24,32},{32,40},{40,48},{48,56},{56,64},{64,7... | collective-permute-start | bytes 368648 | tf_op jit(solution)/shard_map/ppermute | solution.py:299
  9.0 1.2 copy-done.7
  10.2 3.2 %shard_map.104 = (bf16[2,512,512]{2,1,0:T(8,128)(2,1)S(1)}, s32[8,1024]{1,0:T(8,128)S(1)}, f32[128,1024]{1,0:T(8,128)S(1)}, bf16[2,1024,128]{2,1,0:T(8,128)(2,1)S(1)}, f32[24,384]{1,0:T(8,128)}) custom-call(s32[4,512]{1,0:T(4,128)S(1)} %copy-done.1, s32[1,256]{1,0:T(1,128)S(1)} %bitcast.20, f32[512,512]{1,0:T(8,128)S(1)} %copy-done.7, ...), custom_call_target="tpu_custom_call" | custom-call | tf_op jit(solution)/shard_map/pallas_call | solution.py:288
  13.5 4.5 %collective-permute-start.1 = (f32[24,384]{1,0:T(8,128)}, f32[24,384]{1,0:T(8,128)S(1)}, u32[]{:S(2)}, u32[]{:S(2)}) collective-permute-start(f32[24,384]{1,0:T(8,128)} %get-tuple-element.39.downs_ref), channel_id=1, source_target_pairs={{0,504},{8,0},{16,8},{24,16},{32,24},{40,32},{48,40},{56,48},{64,5... | collective-permute-start | bytes 110600 | tf_op jit(solution)/shard_map/ppermute | solution.py:299
  18.0 0.6 pad_add_fusion.place_ref
  18.6 1.7 %copy.11.coupling_ref = f32[512,18]{1,0:T(8,128)} copy(f32[512,18]{0,1:T(8,128)} %param.12) | data formatting | bytes 73728 | tf_op args[4]
  20.3 0.7 copy-done.13
  21.0 1.1 shard_map.105.base_ref
  22.7 1.0 copy-done.10
  23.8 0.8 copy-done.16
  24.5 1.1 shard_map.106
  25.7 0.7 copy-done.18
  26.4 2.4 %shard_map.107 = (f32[16,1024]{1,0:T(8,128)S(1)}, f32[16,640]{1,0:T(8,128)S(1)}, f32[16,384]{1,0:T(8,128)S(1)}) custom-call(f32[16,1024]{1,0:T(8,128)S(1)} %shard_map.105.base_ref, f32[48,640]{1,0:T(8,128)} %get-tuple-element.38.ups_ref, f32[24,384]{1,0:T(8,128)} %get-tuple-element.39.downs_ref, f32[48,640]{1,0:T(8,128)S(1)} %collective-permute-done.up_ref, ...), custom_call_target="tpu_custom_call" | custom-call | tf_op jit(solution)/shard_map/pallas_call | solution.py:288
  28.8 1.9 %collective-permute-start.2 = (f32[16,640]{1,0:T(8,128)S(1)}, f32[16,640]{1,0:T(8,128)S(1)}, u32[]{:S(2)}, u32[]{:S(2)}) collective-permute-start(f32[16,640]{1,0:T(8,128)S(1)} %get-tuple-element.48.ups_ref), channel_id=1, source_target_pairs={{0,8},{8,16},{16,24},{24,32},{32,40},{40,48},{48,56},{56,64},{64,7... | collective-permute-start | bytes 122888 | tf_op jit(solution)/shard_map/ppermute | solution.py:299
  30.7 6.0 %collective-permute-start.3 = (f32[16,384]{1,0:T(8,128)S(1)}, f32[16,384]{1,0:T(8,128)S(1)}, u32[]{:S(2)}, u32[]{:S(2)}) collective-permute-start(f32[16,384]{1,0:T(8,128)S(1)} %get-tuple-element.49.downs_ref), channel_id=1, source_target_pairs={{0,504},{8,0},{16,8},{24,16},{32,24},{40,32},{48,40},{56,48},{64,5... | collective-permute-start | bytes 73736 | tf_op jit(solution)/shard_map/ppermute | solution.py:299
  36.7 1.1 shard_map.108.base_ref
  38.2 1.5 shard_map.109
  39.8 2.1 %collective-permute-start.4 = (f32[16,640]{1,0:T(8,128)S(1)}, f32[16,640]{1,0:T(8,128)S(1)}, u32[]{:S(2)}, u32[]{:S(2)}) collective-permute-start(f32[16,640]{1,0:T(8,128)S(1)} %get-tuple-element.51.ups_ref), channel_id=1, source_target_pairs={{0,8},{8,16},{16,24},{24,32},{32,40},{40,48},{48,56},{56,64},{64,7... | collective-permute-start | bytes 122888 | tf_op jit(solution)/shard_map/ppermute | solution.py:299
  41.8 6.2 %collective-permute-start.5 = (f32[16,384]{1,0:T(8,128)S(1)}, f32[16,384]{1,0:T(8,128)S(1)}, u32[]{:S(2)}, u32[]{:S(2)}) collective-permute-start(f32[16,384]{1,0:T(8,128)S(1)} %get-tuple-element.52.downs_ref), channel_id=1, source_target_pairs={{0,504},{8,0},{16,8},{24,16},{32,24},{40,32},{48,40},{56,48},{64,5... | collective-permute-start | bytes 73736 | tf_op jit(solution)/shard_map/ppermute | solution.py:299
  48.0 1.1 shard_map.110.base_ref
  49.5 1.5 shard_map.111
  51.0 4.1 %collective-permute-start.6 = (f32[16,640]{1,0:T(8,128)S(1)}, f32[16,640]{1,0:T(8,128)S(1)}, u32[]{:S(2)}, u32[]{:S(2)}) collective-permute-start(f32[16,640]{1,0:T(8,128)S(1)} %get-tuple-element.54.ups_ref), channel_id=1, source_target_pairs={{0,8},{8,16},{16,24},{24,32},{32,40},{40,48},{48,56},{56,64},{64,7... | collective-permute-start | bytes 122888 | tf_op jit(solution)/shard_map/ppermute | solution.py:299
  55.1 4.2 %collective-permute-start.7 = (f32[16,384]{1,0:T(8,128)S(1)}, f32[16,384]{1,0:T(8,128)S(1)}, u32[]{:S(2)}, u32[]{:S(2)}) collective-permute-start(f32[16,384]{1,0:T(8,128)S(1)} %get-tuple-element.55.downs_ref), channel_id=1, source_target_pairs={{0,504},{8,0},{16,8},{24,16},{32,24},{40,32},{48,40},{56,48},{64,5... | collective-permute-start | bytes 73736 | tf_op jit(solution)/shard_map/ppermute | solution.py:299
  59.3 1.1 shard_map.112.base_ref
  60.8 1.5 shard_map.113
  62.3 4.0 %collective-permute-start.8 = (f32[16,640]{1,0:T(8,128)S(1)}, f32[16,640]{1,0:T(8,128)S(1)}, u32[]{:S(2)}, u32[]{:S(2)}) collective-permute-start(f32[16,640]{1,0:T(8,128)S(1)} %get-tuple-element.57.ups_ref), channel_id=1, source_target_pairs={{0,8},{8,16},{16,24},{24,32},{32,40},{40,48},{48,56},{56,64},{64,7... | collective-permute-start | bytes 122888 | tf_op jit(solution)/shard_map/ppermute | solution.py:299
  66.4 4.4 %collective-permute-start.9 = (f32[16,384]{1,0:T(8,128)S(1)}, f32[16,384]{1,0:T(8,128)S(1)}, u32[]{:S(2)}, u32[]{:S(2)}) collective-permute-start(f32[16,384]{1,0:T(8,128)S(1)} %get-tuple-element.58.downs_ref), channel_id=1, source_target_pairs={{0,504},{8,0},{16,8},{24,16},{32,24},{40,32},{48,40},{56,48},{64,5... | collective-permute-start | bytes 73736 | tf_op jit(solution)/shard_map/ppermute | solution.py:299
  70.7 1.1 shard_map.114.base_ref
  72.1 1.5 shard_map.115
  73.6 4.0 %collective-permute-start.10 = (f32[16,640]{1,0:T(8,128)S(1)}, f32[16,640]{1,0:T(8,128)S(1)}, u32[]{:S(2)}, u32[]{:S(2)}) collective-permute-start(f32[16,640]{1,0:T(8,128)S(1)} %get-tuple-element.60.ups_ref), channel_id=1, source_target_pairs={{0,8},{8,16},{16,24},{24,32},{32,40},{40,48},{48,56},{56,64},{64,7... | collective-permute-start | bytes 122888 | tf_op jit(solution)/shard_map/ppermute | solution.py:299
  77.6 4.2 %collective-permute-start.11 = (f32[16,384]{1,0:T(8,128)S(1)}, f32[16,384]{1,0:T(8,128)S(1)}, u32[]{:S(2)}, u32[]{:S(2)}) collective-permute-start(f32[16,384]{1,0:T(8,128)S(1)} %get-tuple-element.61.downs_ref), channel_id=1, source_target_pairs={{0,504},{8,0},{16,8},{24,16},{32,24},{40,32},{48,40},{56,48},{64,5... | collective-permute-start | bytes 73736 | tf_op jit(solution)/shard_map/ppermute | solution.py:299
  81.8 1.1 shard_map.116.base_ref
  83.4 2.0 %shard_map.117 = (f32[16,1024]{1,0:T(8,128)}, f32[16,640]{1,0:T(8,128)S(1)}, f32[16,384]{1,0:T(8,128)S(1)}) custom-call(f32[16,1024]{1,0:T(8,128)S(1)} %shard_map.116.base_ref, f32[16,640]{1,0:T(8,128)S(1)} %get-tuple-element.60.ups_ref, f32[16,384]{1,0:T(8,128)S(1)} %get-tuple-element.61.downs_ref, f32[16,640]{1,0:T(8,128)S(1)} %collective-permute-done.10.up_ref, ...), custom_call_target="tpu_custom_call" | custom-call | tf_op jit(solution)/shard_map/pallas_call | solution.py:288
  85.3 1.7 %broadcast_in_dim.2 = f32[8,16,1024]{2,1,0:T(8,128)} broadcast(f32[16,1024]{1,0:T(8,128)} %get-tuple-element.32.v_ref), dimensions={1,2} | broadcast | bytes 589824 | tf_op jit(solution)/shard_map/broadcast_in_dim | solution.py:347
  87.0 4.4 %all-to-all-start = ((f32[8,16,1024]{2,1,0:T(8,128)}), f32[8,16,1024]{2,1,0:T(8,128)S(1)}, u32[]{:S(2)}, u32[]{:S(2)}) async-start(f32[8,16,1024]{2,1,0:T(8,128)} %broadcast_in_dim.2), calls=%async_computation | async-start | bytes 1048576 | tf_op jit(solution)/shard_map/all_to_all | solution.py:347
  91.5 4.0 %collective-permute-start.12 = (f32[16,640]{1,0:T(8,128)S(1)}, f32[16,640]{1,0:T(8,128)S(1)}, u32[]{:S(2)}, u32[]{:S(2)}) collective-permute-start(f32[16,640]{1,0:T(8,128)S(1)} %get-tuple-element.63.ups_ref), channel_id=1, source_target_pairs={{0,8},{8,16},{16,24},{24,32},{32,40},{40,48},{48,56},{56,64},{64,7... | collective-permute-start | bytes 122888 | tf_op jit(solution)/shard_map/ppermute | solution.py:299
  95.5 4.2 %collective-permute-start.13 = (f32[16,384]{1,0:T(8,128)S(1)}, f32[16,384]{1,0:T(8,128)S(1)}, u32[]{:S(2)}, u32[]{:S(2)}) collective-permute-start(f32[16,384]{1,0:T(8,128)S(1)} %get-tuple-element.64.downs_ref), channel_id=1, source_target_pairs={{0,504},{8,0},{16,8},{24,16},{32,24},{40,32},{48,40},{56,48},{64,5... | collective-permute-start | bytes 73736 | tf_op jit(solution)/shard_map/ppermute | solution.py:299
  99.7 1.1 shard_map.118.base_ref
  101.8 0.7 copy-done.20
  102.6 1.7 %shard_map.119 = f32[4,32,128]{2,1,0:T(8,128)S(1)} custom-call(f32[16,1024]{1,0:T(8,128)S(1)} %shard_map.118.base_ref, f32[16,640]{1,0:T(8,128)S(1)} %get-tuple-element.63.ups_ref, f32[16,384]{1,0:T(8,128)S(1)} %get-tuple-element.64.downs_ref, f32[16,640]{1,0:T(8,128)S(1)} %collective-permute-done.12.up_ref, f32[16,384]{1,0:T(8,128)S(1)} %copy-done.20, ...), custom_call_target="tpu_custom_call" | custom-call | tf_op jit(solution)/shard_map/pallas_call | solution.py:288
  104.3 12.7 %all_to_all.15.parts_ref = f32[4,32,128]{2,1,0:T(8,128)S(1)} all-to-all(f32[4,32,128]{2,1,0:T(8,128)S(1)} %shard_map.119), channel_id=1, replica_groups={{0,8,16,24},{32,40,48,56},{64,72,80,88},{96,104,112,120},{128,136,144,1..., dimensions={0} | all-to-all | bytes 131072 | tf_op jit(solution)/shard_map/all_to_all | solution.py:359
  117.0 38.3 %all_to_all.16.parts_ref = f32[16,32,128]{2,1,0:T(8,128)S(1)} all-to-all(f32[16,32,128]{2,1,0:T(8,128)S(1)} %shard_map.120), channel_id=1, replica_groups={{0,32,64,96,128,160,192,224,256,288,320,352,384,416,448,480},{8,40,72,1..., dimensions={0} | all-to-all | bytes 524288 | tf_op jit(solution)/shard_map/all_to_all | solution.py:361
  155.2 0.6 shard_map.121
  (54 shorter events, 3.8 us)
Async XLA Ops:
  0.6 0.7 copy-start.17
  0.6 0.7 copy-start.21
  1.3 0.7 copy-start
  2.0 0.9 copy-start.2
  2.9 0.8 copy-start.4
  3.8 5.2 %copy-start.1 = (s32[4,512]{1,0:T(4,128)S(1)}, s32[4,512]{1,0:T(4,128)}, u32[]{:S(2)}) copy-start(s32[4,512]{1,0:T(4,128)} %conn_ref.31) | copy-start | bytes 24580
  3.8 5.2 %copy-start.3 = (f32[4,18,512]{2,0,1:T(4,128)S(1)}, f32[4,18,512]{2,0,1:T(4,128)}, u32[]{:S(2)}) copy-start(f32[4,18,512]{2,0,1:T(4,128)} %param.11) | copy-start | bytes 442372
  5.5 17.2 %collective-permute-start = (f32[48,640]{1,0:T(8,128)}, f32[48,640]{1,0:T(8,128)S(1)}, u32[]{:S(2)}, u32[]{:S(2)}) collective-permute-start(f32[48,640]{1,0:T(8,128)} %get-tuple-element.38.ups_ref), channel_id=1, source_target_pairs={{0,8},{8,16},{16,24},{24,32},{32,40},{40,48},{48,56},{56,64},{64,7... | collective-permute-start | bytes 368648 | tf_op jit(solution)/shard_map/ppermute | solution.py:299
  9.0 1.2 copy-start.7
  13.5 8.5 %copy-start.9 = (f32[128,1024]{1,0:T(8,128)}, f32[128,1024]{1,0:T(8,128)S(1)}, u32[]{:S(2)}) copy-start(f32[128,1024]{1,0:T(8,128)S(1)} %get-tuple-element.40.pn_ref) | copy-start | bytes 1572868
  13.5 8.6 %collective-permute-start.1 = (f32[24,384]{1,0:T(8,128)}, f32[24,384]{1,0:T(8,128)S(1)}, u32[]{:S(2)}, u32[]{:S(2)}) collective-permute-start(f32[24,384]{1,0:T(8,128)} %get-tuple-element.39.downs_ref), channel_id=1, source_target_pairs={{0,504},{8,0},{16,8},{24,16},{32,24},{40,32},{48,40},{56,48},{64,5... | collective-permute-start | bytes 110600 | tf_op jit(solution)/shard_map/ppermute | solution.py:299
  18.6 1.7 %copy-start.5 = (f32[16,1024]{1,0:T(8,128)S(1)}, f32[16,1024]{1,0:T(8,128)}, u32[]{:S(2)}) copy-start(f32[16,1024]{1,0:T(8,128)} %prev_ref.3) | copy-start | bytes 196612
  20.3 0.7 copy-start.13
  21.0 1.7 %copy-start.6 = (f32[512,18]{1,0:T(8,128)S(1)}, f32[512,18]{1,0:T(8,128)}, u32[]{:S(2)}) copy-start(f32[512,18]{1,0:T(8,128)} %copy.11.coupling_ref) | copy-start | bytes 110596
  22.0 0.7 copy-start.22
  22.1 0.7 copy-start.23
  22.1 0.6 copy-start.15
  22.7 1.0 copy-start.10
  23.8 0.8 copy-start.16
  25.7 57.7 %copy-start.11 = (f32[8,256]{1,0:T(8,128)}, f32[8,256]{1,0:T(8,128)S(1)}, u32[]{:S(2)}) copy-start(f32[8,256]{1,0:T(8,128)S(1)} %get-tuple-element.45.coup_ref) | copy-start | bytes 24580
  25.7 0.7 copy-start.18
  28.8 9.5 %collective-permute-start.2 = (f32[16,640]{1,0:T(8,128)S(1)}, f32[16,640]{1,0:T(8,128)S(1)}, u32[]{:S(2)}, u32[]{:S(2)}) collective-permute-start(f32[16,640]{1,0:T(8,128)S(1)} %get-tuple-element.48.ups_ref), channel_id=1, source_target_pairs={{0,8},{8,16},{16,24},{24,32},{32,40},{40,48},{48,56},{56,64},{64,7... | collective-permute-start | bytes 122888 | tf_op jit(solution)/shard_map/ppermute | solution.py:299
  30.7 7.5 %collective-permute-start.3 = (f32[16,384]{1,0:T(8,128)S(1)}, f32[16,384]{1,0:T(8,128)S(1)}, u32[]{:S(2)}, u32[]{:S(2)}) collective-permute-start(f32[16,384]{1,0:T(8,128)S(1)} %get-tuple-element.49.downs_ref), channel_id=1, source_target_pairs={{0,504},{8,0},{16,8},{24,16},{32,24},{40,32},{48,40},{56,48},{64,5... | collective-permute-start | bytes 73736 | tf_op jit(solution)/shard_map/ppermute | solution.py:299
  39.8 9.8 %collective-permute-start.4 = (f32[16,640]{1,0:T(8,128)S(1)}, f32[16,640]{1,0:T(8,128)S(1)}, u32[]{:S(2)}, u32[]{:S(2)}) collective-permute-start(f32[16,640]{1,0:T(8,128)S(1)} %get-tuple-element.51.ups_ref), channel_id=1, source_target_pairs={{0,8},{8,16},{16,24},{24,32},{32,40},{40,48},{48,56},{56,64},{64,7... | collective-permute-start | bytes 122888 | tf_op jit(solution)/shard_map/ppermute | solution.py:299
  41.8 7.7 %collective-permute-start.5 = (f32[16,384]{1,0:T(8,128)S(1)}, f32[16,384]{1,0:T(8,128)S(1)}, u32[]{:S(2)}, u32[]{:S(2)}) collective-permute-start(f32[16,384]{1,0:T(8,128)S(1)} %get-tuple-element.52.downs_ref), channel_id=1, source_target_pairs={{0,504},{8,0},{16,8},{24,16},{32,24},{40,32},{48,40},{56,48},{64,5... | collective-permute-start | bytes 73736 | tf_op jit(solution)/shard_map/ppermute | solution.py:299
  51.0 9.8 %collective-permute-start.6 = (f32[16,640]{1,0:T(8,128)S(1)}, f32[16,640]{1,0:T(8,128)S(1)}, u32[]{:S(2)}, u32[]{:S(2)}) collective-permute-start(f32[16,640]{1,0:T(8,128)S(1)} %get-tuple-element.54.ups_ref), channel_id=1, source_target_pairs={{0,8},{8,16},{16,24},{24,32},{32,40},{40,48},{48,56},{56,64},{64,7... | collective-permute-start | bytes 122888 | tf_op jit(solution)/shard_map/ppermute | solution.py:299
  55.1 5.7 %collective-permute-start.7 = (f32[16,384]{1,0:T(8,128)S(1)}, f32[16,384]{1,0:T(8,128)S(1)}, u32[]{:S(2)}, u32[]{:S(2)}) collective-permute-start(f32[16,384]{1,0:T(8,128)S(1)} %get-tuple-element.55.downs_ref), channel_id=1, source_target_pairs={{0,504},{8,0},{16,8},{24,16},{32,24},{40,32},{48,40},{56,48},{64,5... | collective-permute-start | bytes 73736 | tf_op jit(solution)/shard_map/ppermute | solution.py:299
  62.3 9.8 %collective-permute-start.8 = (f32[16,640]{1,0:T(8,128)S(1)}, f32[16,640]{1,0:T(8,128)S(1)}, u32[]{:S(2)}, u32[]{:S(2)}) collective-permute-start(f32[16,640]{1,0:T(8,128)S(1)} %get-tuple-element.57.ups_ref), channel_id=1, source_target_pairs={{0,8},{8,16},{16,24},{24,32},{32,40},{40,48},{48,56},{56,64},{64,7... | collective-permute-start | bytes 122888 | tf_op jit(solution)/shard_map/ppermute | solution.py:299
  66.4 5.7 %collective-permute-start.9 = (f32[16,384]{1,0:T(8,128)S(1)}, f32[16,384]{1,0:T(8,128)S(1)}, u32[]{:S(2)}, u32[]{:S(2)}) collective-permute-start(f32[16,384]{1,0:T(8,128)S(1)} %get-tuple-element.58.downs_ref), channel_id=1, source_target_pairs={{0,504},{8,0},{16,8},{24,16},{32,24},{40,32},{48,40},{56,48},{64,5... | collective-permute-start | bytes 73736 | tf_op jit(solution)/shard_map/ppermute | solution.py:299
  73.6 9.8 %collective-permute-start.10 = (f32[16,640]{1,0:T(8,128)S(1)}, f32[16,640]{1,0:T(8,128)S(1)}, u32[]{:S(2)}, u32[]{:S(2)}) collective-permute-start(f32[16,640]{1,0:T(8,128)S(1)} %get-tuple-element.60.ups_ref), channel_id=1, source_target_pairs={{0,8},{8,16},{16,24},{24,32},{32,40},{40,48},{48,56},{56,64},{64,7... | collective-permute-start | bytes 122888 | tf_op jit(solution)/shard_map/ppermute | solution.py:299
  77.6 5.7 %collective-permute-start.11 = (f32[16,384]{1,0:T(8,128)S(1)}, f32[16,384]{1,0:T(8,128)S(1)}, u32[]{:S(2)}, u32[]{:S(2)}) collective-permute-start(f32[16,384]{1,0:T(8,128)S(1)} %get-tuple-element.61.downs_ref), channel_id=1, source_target_pairs={{0,504},{8,0},{16,8},{24,16},{32,24},{40,32},{48,40},{56,48},{64,5... | collective-permute-start | bytes 73736 | tf_op jit(solution)/shard_map/ppermute | solution.py:299
  87.0 12.7 %copy-start.8 = (f32[16,1024]{1,0:T(8,128)S(1)}, f32[16,1024]{1,0:T(8,128)}, u32[]{:S(2)}) copy-start(f32[16,1024]{1,0:T(8,128)} %get-tuple-element.32.v_ref) | copy-start | bytes 196612
  87.0 12.7 %copy-start.14 = (f32[1024]{0:T(1024)S(1)}, f32[1024]{0:T(1024)}, u32[]{:S(2)}) copy-start(f32[1024]{0:T(1024)} %param.9) | copy-start | bytes 12292
  87.0 14.8 %all-to-all-start = ((f32[8,16,1024]{2,1,0:T(8,128)}), f32[8,16,1024]{2,1,0:T(8,128)S(1)}, u32[]{:S(2)}, u32[]{:S(2)}) async-start(f32[8,16,1024]{2,1,0:T(8,128)} %broadcast_in_dim.2), calls=%async_computation | async-start | bytes 1048576 | tf_op jit(solution)/shard_map/all_to_all | solution.py:347
  91.5 10.4 %collective-permute-start.12 = (f32[16,640]{1,0:T(8,128)S(1)}, f32[16,640]{1,0:T(8,128)S(1)}, u32[]{:S(2)}, u32[]{:S(2)}) collective-permute-start(f32[16,640]{1,0:T(8,128)S(1)} %get-tuple-element.63.ups_ref), channel_id=1, source_target_pairs={{0,8},{8,16},{16,24},{24,32},{32,40},{40,48},{48,56},{56,64},{64,7... | collective-permute-start | bytes 122888 | tf_op jit(solution)/shard_map/ppermute | solution.py:299
  95.5 6.3 %copy-start.12 = (f32[8,256]{1,0:T(8,128)S(1)}, f32[8,256]{1,0:T(8,128)}, u32[]{:S(2)}) copy-start(f32[8,256]{1,0:T(8,128)} %copy-done.11) | copy-start | bytes 24580
  95.5 5.7 %collective-permute-start.13 = (f32[16,384]{1,0:T(8,128)S(1)}, f32[16,384]{1,0:T(8,128)S(1)}, u32[]{:S(2)}, u32[]{:S(2)}) collective-permute-start(f32[16,384]{1,0:T(8,128)S(1)} %get-tuple-element.64.downs_ref), channel_id=1, source_target_pairs={{0,504},{8,0},{16,8},{24,16},{32,24},{40,32},{48,40},{56,48},{64,5... | collective-permute-start | bytes 73736 | tf_op jit(solution)/shard_map/ppermute | solution.py:299
  101.2 0.6 copy-start.19
  101.8 0.7 copy-start.20

commit v4 on v3

--- a/solution.py
+++ b/solution.py
@@ -92,11 +92,11 @@
     down_ref[0:BANDS, GHOST:] = partials
 
 
-def first_kernel(v_ref, conn_ref, send_ref, atom_ref, proj_ref, up_ref, down_ref):
+def first_kernel(v_ref, conn_ref, send_ref, atom_ref, proj_ref, pot_ref, coupling_ref, up_ref, down_ref):
     v = v_ref[...]
     sources = blocks_of(v)
     cells = [pick_row(sources, conn_ref[c : c + 1, :]) for c in range(3)]
-    stacked = [padded_projectors(proj_ref[:, c, :]) for c in range(3)] + [jnp.zeros((SLOT, NPC), F32)]
+    stacked = [padded_projectors(proj_ref[c]) for c in range(3)] + [jnp.zeros((SLOT, NPC), F32)]
     t_high, t_low = split2(jnp.concatenate(stacked, axis=0).T)
     x_high, x_low = split2(jnp.concatenate(cells, axis=0))
     wide = product(x_high, x_low, t_high, t_low)
@@ -118,7 +118,7 @@
     up_ref[...] = jnp.zeros_like(up_ref)
     down_ref[...] = jnp.zeros_like(down_ref)
     pack_message(v, partials, conn_ref, send_ref, up_ref, down_ref)
-    up_ref[16 : 16 + NPROJ, 0:NPC] = proj_ref[:, 3, :]
+    up_ref[16 : 16 + NPROJ, 0:NPC] = proj_ref[3]
     up_ref[40:41, 0:NPC] = edge.astype(F32)
     up_ref[41:42, 0:GHOST] = jnp.concatenate(inverse, axis=1)
     up_ref[42:43, 0:LANES] = atoms
@@ -137,7 +137,7 @@
     for c in range(4):
         names = column(conn_ref[c : c + 1, :].astype(F32))
         place = position + float(c * NPC)
-        thirds = jnp.concatenate(split3(padded_projectors(proj_ref[:, c, :])), axis=0)
+        thirds = jnp.concatenate(split3(padded_projectors(proj_ref[c])), axis=0)
         for k in range(0, NODES // LANES, 2):
             hits = []
             for j in (k, k + 1):
@@ -159,7 +159,7 @@
         maps_ref[2:3, here] = jnp.max(jnp.where(same, position[:GHOST], -1.0), axis=0, keepdims=True).astype(jnp.int32)
 
 
-def joined_kernel(up_ref, down_ref, maps_ref, atom_ref, place_ref, proj_ref, coupling_ref, pn_ref, p_ref, pe_ref, k_ref, coup_ref, index_ref):
+def joined_kernel(up_ref, down_ref, maps_ref, atom_ref, proj_ref, coupling_ref, pn_ref, p_ref, pe_ref, k_ref, index_ref):
     low_atoms, high_atoms = up_ref[42:43, 0:LANES], down_ref[16:17, 0:LANES]
     which = lane_iota(1, LANES) >> 5
     own = jnp.full((1, LANES), -100.0, F32)
@@ -180,17 +180,8 @@
         rows.append(jnp.where(inside & jnp.broadcast_to(same, inside.shape), 1.0, 0.0))
     rows.append(jnp.zeros((3 * SLOT, 4 * LANES), F32))
     k_ref[...] = jnp.concatenate(rows, axis=0).T.astype(BF16)
-    lower = coupling_ref[pl.ds(pl.multiple_of(place_ref[0] * ATOM_DEV, ATOM_DEV), ATOM_DEV), :]
-    mine = coupling_ref[pl.ds(pl.multiple_of(place_ref[1] * ATOM_DEV, ATOM_DEV), ATOM_DEV), :]
-    pair = jnp.concatenate([lower, mine], axis=0)
-    pair = jnp.concatenate([pair, jnp.zeros((2 * ATOM_DEV, SLOT - NPROJ), F32)], axis=1)
-    wide = jnp.concatenate([pair] * 8, axis=1)
-    target = jnp.concatenate([own, jnp.where(which == 0, edge_low, -200.0)], axis=1)
-    slot = row_iota(2 * ATOM_DEV, 2 * LANES).astype(F32)
-    chosen = jnp.where(jnp.broadcast_to(target, slot.shape) == slot, wide, 0.0)
-    coup_ref[...] = jnp.broadcast_to(jnp.sum(chosen, axis=0, keepdims=True), coup_ref.shape)
     low = padded_projectors(up_ref[16 : 16 + NPROJ, 0:NPC])
-    stacked = jnp.concatenate([padded_projectors(proj_ref[:, 3, :]), low, jnp.zeros((2 * SLOT, NPC), F32)], axis=0)
+    stacked = jnp.concatenate([padded_projectors(proj_ref[3]), low, jnp.zeros((2 * SLOT, NPC), F32)], axis=0)
     pe_ref[0], pe_ref[1] = split2(stacked.T)
     index_ref[...] = jnp.zeros_like(index_ref)
     index_ref[0:2, :] = maps_ref[0:2, :]
@@ -200,7 +191,22 @@
     third = jnp.where(jnp.broadcast_to(sent, third.shape) >= 0, third, -1.0)[0:1].astype(jnp.int32)
     index_ref[2:3, :] = third
     index_ref[3:4, 0:NPC] = up_ref[40:41, 0:NPC].astype(jnp.int32) - NODES
-    spread = jnp.concatenate([pn_ref[...], pick_row(blocks_of(low), third), jnp.zeros((3 * SLOT, NODES), F32)], axis=0)
+    size = lax.axis_size("fe")
+    fe = lax.axis_index("fe")
+    below = lax.rem(fe + size - 1, size)
+    row = lane_iota(1, coupling_ref.shape[1])
+    offset = row - below * ATOM_DEV
+    slots = jnp.where((offset >= 0) & (offset < ATOM_DEV), offset, -600)
+    offset = row - fe * ATOM_DEV
+    slots = jnp.where((offset >= 0) & (offset < ATOM_DEV), offset + ATOM_DEV, slots).astype(F32)
+    factors = []
+    for c in range(5):
+        name = atom_ref[c].astype(F32) if c < 4 else jnp.broadcast_to(edge_low[:, 0:1], slots.shape)
+        mine = jnp.where(jnp.broadcast_to(slots == name, coupling_ref.shape), coupling_ref[...], 0.0)
+        factors.append(jnp.sum(mine, axis=1, keepdims=True))
+        factors.append(jnp.zeros((SLOT - NPROJ, 1), F32))
+    spread = jnp.concatenate([pn_ref[...], pick_row(blocks_of(low), third)], axis=0) * jnp.concatenate(factors, axis=0)
+    spread = jnp.concatenate([spread, jnp.zeros((3 * SLOT, NODES), F32)], axis=0)
     p_ref[0], p_ref[1] = split2(spread)
 
 
@@ -223,7 +229,7 @@
         base_ref[:, here] = h
 
 
-def outer(ups_ref, downs_ref, up_ref, down_ref, conn_ref, index_ref, e_ref, p_ref, pe_ref, k_ref, coup_ref):
+def outer(ups_ref, downs_ref, up_ref, down_ref, conn_ref, index_ref, e_ref, p_ref, pe_ref, k_ref):
     edge = ups_ref[0:BANDS, 0:NPC] + pick_row(blocks_of(down_ref[0:BANDS, 0:GHOST]), conn_ref[3:4, :] - NODES)
     low = up_ref[0:BANDS, 0:NPC] + pick_row(blocks_of(downs_ref[0:BANDS, 0:GHOST]), index_ref[3:4, 0:NPC])
     x_high, x_low = split2(jnp.concatenate([edge, low], axis=0))
@@ -232,7 +238,7 @@
     edges = jnp.where(which == 0, wide[:BANDS], jnp.where(which == 1, wide[BANDS:], 0.0))
     partials = jnp.concatenate([ups_ref[0:BANDS, NPC:], edges, down_ref[0:BANDS, GHOST:], up_ref[0:BANDS, NPC:]], axis=1)
     sums = dot(jnp.concatenate(split3(partials), axis=0), k_ref[...])
-    w_high, w_low = split2((sums[0:16] + sums[16:32] + sums[32:48]) * coup_ref[0:1, :])
+    w_high, w_low = split2(sums[0:16] + sums[16:32] + sums[32:48])
     nonlocal_part = product(w_high, w_low, p_ref[0], p_ref[1])
     y = product(x_high, x_low, e_ref[0], e_ref[1])
     own, other = blocks_of(y[:BANDS]), blocks_of(y[BANDS:])
@@ -244,18 +250,21 @@
     return jnp.concatenate(out, axis=1) + nonlocal_part
 
 
-def outer_kernel(factor, base_ref, ups_ref, downs_ref, up_ref, down_ref, conn_ref, index_ref, e_ref, p_ref, pe_ref, k_ref, coup_ref,
-                 send_ref, pt_ref, new_ref, upo_ref, downo_ref):
-    h = outer(ups_ref, downs_ref, up_ref, down_ref, conn_ref, index_ref, e_ref, p_ref, pe_ref, k_ref, coup_ref)
+def outer_kernel(factor, base_ref, ups_ref, downs_ref, up_ref, down_ref, conn_ref, index_ref, e_ref, p_ref, pe_ref, k_ref,
+                 send_ref, pt_ref, new_ref, upo_ref, downo_ref, *copies_ref):
+    h = outer(ups_ref, downs_ref, up_ref, down_ref, conn_ref, index_ref, e_ref, p_ref, pe_ref, k_ref)
     new = base_ref[...] + h * factor
     new_ref[...] = new
+    for ref in copies_ref:
+        for i in range(ref.shape[0]):
+            ref[i] = new
     v_high, v_low = split2(new)
     pack_message(new, product(v_high, v_low, pt_ref[0], pt_ref[1]), conn_ref, send_ref, upo_ref, downo_ref)
 
 
-def gram_kernel(base_ref, ups_ref, downs_ref, up_ref, down_ref, conn_ref, index_ref, e_ref, p_ref, pe_ref, k_ref, coup_ref,
+def gram_kernel(base_ref, ups_ref, downs_ref, up_ref, down_ref, conn_ref, index_ref, e_ref, p_ref, pe_ref, k_ref,
                 v_ref, all_ref, out_ref):
-    h = base_ref[...] + outer(ups_ref, downs_ref, up_ref, down_ref, conn_ref, index_ref, e_ref, p_ref, pe_ref, k_ref, coup_ref)
+    h = base_ref[...] + outer(ups_ref, downs_ref, up_ref, down_ref, conn_ref, index_ref, e_ref, p_ref, pe_ref, k_ref)
     s_high, s_low = split2(jnp.concatenate([h, v_ref[...]], axis=0))
     a_high, a_low = split2(all_ref[...])
     both = dot_nt(jnp.concatenate([s_high, s_low], axis=0), a_high)
@@ -290,7 +299,7 @@
         out_shape=[jax.ShapeDtypeStruct(s, t) for s, t in outs],
         in_specs=ins,
         out_specs=[VM] * len(outs),
-        compiler_params=pltpu.CompilerParams(vmem_limit_bytes=40 * 2**20),
+        compiler_params=pltpu.CompilerParams(vmem_limit_bytes=24 * 2**20),
     )(*args)
 
 
@@ -301,57 +310,53 @@
 
 def on_device(wavefunctions, potential, element_matrix, projectors, coupling, connectivity, send_list, atom_of_cell):
     fe_count = lax.axis_size("fe")
-    fe = lax.axis_index("fe").astype(jnp.int32)
-    place = jnp.stack([(fe + fe_count - 1) % fe_count, fe])
-    send = send_list.reshape(1, GHOST)
-    pot = potential.reshape(1, NODES)
-    proj = projectors.transpose(1, 0, 2)
+    v, conn, send = wavefunctions, connectivity, send_list.reshape(1, GHOST)
+    pot, couple = potential.reshape(1, NODES), coupling.T
     ups, downs = call(
         first_kernel,
         [((48, 640), F32), ((24, 384), F32)],
-        [VM, VM, VM, SM, VM],
-        wavefunctions, connectivity, send, atom_of_cell, proj,
+        [VM, VM, VM, SM, VM, VM, VM],
+        v, conn, send, atom_of_cell, projectors, pot, couple,
     )
     up = shifted(ups, 1)
     e, maps, pn, pt, downs = call(
         local_kernel,
         [((2, NPC, NPC), BF16), ((8, NODES), jnp.int32), ((4 * SLOT, NODES), F32), ((2, NODES, LANES), BF16), ((24, 384), F32)],
         [VM] * 5,
-        connectivity, send, element_matrix, proj, downs,
+        conn, send, element_matrix, projectors, downs,
     )
     down = shifted(downs, -1)
 
     def inner(mode, v, previous):
-        return call(functools.partial(inner_kernel, mode), [((BANDS, NODES), F32)], [VM] * 6, v, previous, connectivity, maps, pot, e)[0]
-
-    previous = current = wavefunctions
+        return call(functools.partial(inner_kernel, mode), [((BANDS, NODES), F32)], [VM] * 6, v, previous, conn, maps, pot, e)[0]
+
+    previous = current = v
     base = inner("first", current, previous)
-    p, pe, k, coup, index = call(
+    p, pe, k, index = call(
         joined_kernel,
-        [((2, 256, NODES), BF16), ((2, NPC, LANES), BF16), ((512, 256), BF16), ((8, 256), F32), ((8, NODES), jnp.int32)],
-        [VM, VM, VM, SM, SM, VM, VM, VM],
-        up, down, maps, atom_of_cell, place, proj, coupling, pn,
-    )
-    shared = (connectivity, index, e, p, pe, k, coup)
+        [((2, 256, NODES), BF16), ((2, NPC, LANES), BF16), ((512, 256), BF16), ((8, NODES), jnp.int32)],
+        [VM, VM, VM, SM, VM, VM, VM],
+        up, down, maps, atom_of_cell, projectors, couple, pn,
+    )
+    shared = (conn, index, e, p, pe, k)
     for step in range(DEGREE):
         last = step == DEGREE - 1
-        new, ups, downs = call(
+        copied = [((lax.axis_size("band"), BANDS, NODES), F32)] if last else []
+        new, ups, downs, *copied = call(
             functools.partial(outer_kernel, (1.0 if step == 0 else 2.0) / HALF_WIDTH),
-            [((BANDS, NODES), F32), ((BANDS, 640), F32), ((BANDS, 384), F32)],
-            [VM] * 14,
+            [((BANDS, NODES), F32), ((BANDS, 640), F32), ((BANDS, 384), F32)] + copied,
+            [VM] * 13,
             base, ups, downs, up, down, *shared, send, pt,
         )
         previous, current = current, new
         if last:
-            bands = lax.axis_size("band")
-            everyone = lax.all_to_all(jnp.broadcast_to(current[None], (bands,) + current.shape), "band", 0, 0)
-            everyone = everyone.reshape(-1, NODES)
+            everyone = lax.all_to_all(copied[0], "band", 0, 0).reshape(-1, NODES)
         up, down = shifted(ups, 1), shifted(downs, -1)
         base = inner("last" if last else "middle", current, previous)
     (copies,) = call(
         gram_kernel,
         [((4, 32, LANES), F32)],
-        [VM] * 14,
+        [VM] * 13,
         base, ups, downs, up, down, *shared, current, everyone,
     )
     near = [[4 * i + j for j in range(4)] for i in range(fe_count // 4)]

time: 157 us -> 146 us (0.930)
  local copies, waits for them, and re-layouts: 12.9 us -> 3.68 us
  Pallas kernels: 26.4 us -> 24.4 us
    unnamed x49 -> x19, local copies, waits for them, and re-layouts: 11.2 us -> 3.68 us
    pallas_call x19, Pallas kernels: 26.4 us -> 24.4 us  [call(): pl.pallas_call(kernel, out_shape=[jax.ShapeDtypeStruct(s, t) for s, t in...]
    broadcast_in_dim x1 -> x0, local copies, waits for them, and re-layouts: 1.7 us -> none  [on_device(): jnp.broadcast_to(current[None], (bands,) + current.shape)]
  transfers between devices with their start and end apart: 15 -> 15, of which waited for: 6 -> 8; matrix products, arithmetic and copies ran while one was open for 1% -> 0% of each run, Pallas kernels for 7% -> 7%
where the time goes in v4:
time: 146 us; the launch traced here: 145 us
  starting transfers between devices  61.9 us (42%)
  blocking collectives  50.4 us (35%)
  Pallas kernels  24.4 us (17%)
  waiting for transfers between devices  3.73 us (3%)
  local copies, waits for them, and re-layouts  3.68 us (3%)
    ppermute x14, starting transfers between devices, shifted(): lax.ppermute(block, 'fe', [(i, (i + distance) % size) for i in range(size)])  57.4 us
    all_to_all x1, blocking collectives, on_device(): parts = lax.all_to_all(copies, 'fe', 0, 0, axis_index_groups=far)  37.5 us
    pallas_call x19, Pallas kernels, call(): pl.pallas_call(kernel, out_shape=[jax.ShapeDtypeStruct(s, t) for s, t in...  24.4 us
    all_to_all x1, blocking collectives, on_device(): parts = lax.all_to_all(copies, 'fe', 0, 0, axis_index_groups=near)  12.9 us
    all_to_all x1, starting transfers between devices, on_device(): everyone = lax.all_to_all(copied[0], 'band', 0, 0).reshape(-1, NODES)  4.43 us
    unnamed x19, local copies, waits for them, and re-layouts  3.68 us
    ppermute x14, waiting for transfers between devices, shifted(): lax.ppermute(block, 'fe', [(i, (i + distance) % size) for i in range(size)])  3.13 us
  transfers between devices with their start and end apart: 15, of which 8 were waited for; matrix products, arithmetic and copies ran while one was open for 0% of the time, Pallas kernels for 7%

profile of v4, /device:TPU:32, one launch (start us, length us, event | category | flops | bytes accessed | tf_op | source)
XLA Modules:
  0.0 144.9 jit_solution(5837009023555642258)
XLA Ops:
  0.7 1.0 copy.12.proj_ref
  1.7 0.6 copy-done.4
  2.4 0.0 copy-done.7
  2.4 1.1 shard_map.103
  3.5 3.5 %collective-permute-start = (f32[48,640]{1,0:T(8,128)S(1)}, f32[48,640]{1,0:T(8,128)S(1)}, u32[]{:S(2)}, u32[]{:S(2)}) collective-permute-start(f32[48,640]{1,0:T(8,128)S(1)} %get-tuple-element.38.ups_ref), channel_id=1, source_target_pairs={{0,8},{8,16},{16,24},{24,32},{32,40},{40,48},{48,56},{56,64},{64,7... | collective-permute-start | bytes 368648 | tf_op jit(solution)/shard_map/ppermute | solution.py:308
  7.0 1.2 copy-done.2
  8.2 2.7 %shard_map.104 = (bf16[2,512,512]{2,1,0:T(8,128)(2,1)S(1)}, s32[8,1024]{1,0:T(8,128)S(1)}, f32[128,1024]{1,0:T(8,128)S(1)}, bf16[2,1024,128]{2,1,0:T(8,128)(2,1)S(1)}, f32[24,384]{1,0:T(8,128)S(1)}) custom-call(s32[4,512]{1,0:T(4,128)S(1)} %copy-done, s32[1,256]{1,0:T(1,128)S(1)} %bitcast.18, f32[512,512]{1,0:T(8,128)S(1)} %copy-done.2, ...), custom_call_target="tpu_custom_call" | custom-call | tf_op jit(solution)/shard_map/pallas_call | solution.py:297
  10.9 4.5 %collective-permute-start.1 = (f32[24,384]{1,0:T(8,128)S(1)}, f32[24,384]{1,0:T(8,128)S(1)}, u32[]{:S(2)}, u32[]{:S(2)}) collective-permute-start(f32[24,384]{1,0:T(8,128)S(1)} %get-tuple-element.39.downs_ref), channel_id=1, source_target_pairs={{0,504},{8,0},{16,8},{24,16},{32,24},{40,32},{48,40},{56,48},{64,5... | collective-permute-start | bytes 110600 | tf_op jit(solution)/shard_map/ppermute | solution.py:308
  15.4 1.1 shard_map.105.base_ref
  16.5 0.5 collective-permute-done.1.down_ref
  17.0 1.1 shard_map.106
  18.2 1.5 %shard_map.107 = (f32[16,1024]{1,0:T(8,128)S(1)}, f32[16,640]{1,0:T(8,128)S(1)}, f32[16,384]{1,0:T(8,128)S(1)}) custom-call(f32[16,1024]{1,0:T(8,128)S(1)} %shard_map.105.base_ref, f32[48,640]{1,0:T(8,128)S(1)} %get-tuple-element.38.ups_ref, f32[24,384]{1,0:T(8,128)S(1)} %get-tuple-element.39.downs_ref, f32[48,640]{1,0:T(8,128)S(1)} %collective-permute-done.up_ref, ...), custom_call_target="tpu_custom_call" | custom-call | tf_op jit(solution)/shard_map/pallas_call | solution.py:297
  19.7 3.3 %collective-permute-start.2 = (f32[16,640]{1,0:T(8,128)S(1)}, f32[16,640]{1,0:T(8,128)S(1)}, u32[]{:S(2)}, u32[]{:S(2)}) collective-permute-start(f32[16,640]{1,0:T(8,128)S(1)} %get-tuple-element.47.ups_ref), channel_id=1, source_target_pairs={{0,8},{8,16},{16,24},{24,32},{32,40},{40,48},{48,56},{56,64},{64,7... | collective-permute-start | bytes 122888 | tf_op jit(solution)/shard_map/ppermute | solution.py:308
  22.9 5.0 %collective-permute-start.3 = (f32[16,384]{1,0:T(8,128)S(1)}, f32[16,384]{1,0:T(8,128)S(1)}, u32[]{:S(2)}, u32[]{:S(2)}) collective-permute-start(f32[16,384]{1,0:T(8,128)S(1)} %get-tuple-element.48.downs_ref), channel_id=1, source_target_pairs={{0,504},{8,0},{16,8},{24,16},{32,24},{40,32},{48,40},{56,48},{64,5... | collective-permute-start | bytes 73736 | tf_op jit(solution)/shard_map/ppermute | solution.py:308
  27.9 1.1 shard_map.108.base_ref
  29.0 0.4 collective-permute-done.3.down_ref
  29.4 1.5 %shard_map.109 = (f32[16,1024]{1,0:T(8,128)S(1)}, f32[16,640]{1,0:T(8,128)S(1)}, f32[16,384]{1,0:T(8,128)S(1)}) custom-call(f32[16,1024]{1,0:T(8,128)S(1)} %shard_map.108.base_ref, f32[16,640]{1,0:T(8,128)S(1)} %get-tuple-element.47.ups_ref, f32[16,384]{1,0:T(8,128)S(1)} %get-tuple-element.48.downs_ref, f32[16,640]{1,0:T(8,128)S(1)} %collective-permute-done.2.up_ref, ...), custom_call_target="tpu_custom_call" | custom-call | tf_op jit(solution)/shard_map/pallas_call | solution.py:297
  31.0 4.1 %collective-permute-start.4 = (f32[16,640]{1,0:T(8,128)S(1)}, f32[16,640]{1,0:T(8,128)S(1)}, u32[]{:S(2)}, u32[]{:S(2)}) collective-permute-start(f32[16,640]{1,0:T(8,128)S(1)} %get-tuple-element.50.ups_ref), channel_id=1, source_target_pairs={{0,8},{8,16},{16,24},{24,32},{32,40},{40,48},{48,56},{56,64},{64,7... | collective-permute-start | bytes 122888 | tf_op jit(solution)/shard_map/ppermute | solution.py:308
  35.0 4.2 %collective-permute-start.5 = (f32[16,384]{1,0:T(8,128)S(1)}, f32[16,384]{1,0:T(8,128)S(1)}, u32[]{:S(2)}, u32[]{:S(2)}) collective-permute-start(f32[16,384]{1,0:T(8,128)S(1)} %get-tuple-element.51.downs_ref), channel_id=1, source_target_pairs={{0,504},{8,0},{16,8},{24,16},{32,24},{40,32},{48,40},{56,48},{64,5... | collective-permute-start | bytes 73736 | tf_op jit(solution)/shard_map/ppermute | solution.py:308
  39.2 1.1 shard_map.110.base_ref
  40.3 0.5 collective-permute-done.5.down_ref
  40.8 1.5 %shard_map.111 = (f32[16,1024]{1,0:T(8,128)S(1)}, f32[16,640]{1,0:T(8,128)S(1)}, f32[16,384]{1,0:T(8,128)S(1)}) custom-call(f32[16,1024]{1,0:T(8,128)S(1)} %shard_map.110.base_ref, f32[16,640]{1,0:T(8,128)S(1)} %get-tuple-element.50.ups_ref, f32[16,384]{1,0:T(8,128)S(1)} %get-tuple-element.51.downs_ref, f32[16,640]{1,0:T(8,128)S(1)} %collective-permute-done.4.up_ref, ...), custom_call_target="tpu_custom_call" | custom-call | tf_op jit(solution)/shard_map/pallas_call | solution.py:297
  42.3 4.0 %collective-permute-start.6 = (f32[16,640]{1,0:T(8,128)S(1)}, f32[16,640]{1,0:T(8,128)S(1)}, u32[]{:S(2)}, u32[]{:S(2)}) collective-permute-start(f32[16,640]{1,0:T(8,128)S(1)} %get-tuple-element.53.ups_ref), channel_id=1, source_target_pairs={{0,8},{8,16},{16,24},{24,32},{32,40},{40,48},{48,56},{56,64},{64,7... | collective-permute-start | bytes 122888 | tf_op jit(solution)/shard_map/ppermute | solution.py:308
  46.3 4.2 %collective-permute-start.7 = (f32[16,384]{1,0:T(8,128)S(1)}, f32[16,384]{1,0:T(8,128)S(1)}, u32[]{:S(2)}, u32[]{:S(2)}) collective-permute-start(f32[16,384]{1,0:T(8,128)S(1)} %get-tuple-element.54.downs_ref), channel_id=1, source_target_pairs={{0,504},{8,0},{16,8},{24,16},{32,24},{40,32},{48,40},{56,48},{64,5... | collective-permute-start | bytes 73736 | tf_op jit(solution)/shard_map/ppermute | solution.py:308
  50.5 1.1 shard_map.112.base_ref
  51.6 0.5 collective-permute-done.7.down_ref
  52.0 1.5 %shard_map.113 = (f32[16,1024]{1,0:T(8,128)S(1)}, f32[16,640]{1,0:T(8,128)S(1)}, f32[16,384]{1,0:T(8,128)S(1)}) custom-call(f32[16,1024]{1,0:T(8,128)S(1)} %shard_map.112.base_ref, f32[16,640]{1,0:T(8,128)S(1)} %get-tuple-element.53.ups_ref, f32[16,384]{1,0:T(8,128)S(1)} %get-tuple-element.54.downs_ref, f32[16,640]{1,0:T(8,128)S(1)} %collective-permute-done.6.up_ref, ...), custom_call_target="tpu_custom_call" | custom-call | tf_op jit(solution)/shard_map/pallas_call | solution.py:297
  53.5 4.0 %collective-permute-start.8 = (f32[16,640]{1,0:T(8,128)S(1)}, f32[16,640]{1,0:T(8,128)S(1)}, u32[]{:S(2)}, u32[]{:S(2)}) collective-permute-start(f32[16,640]{1,0:T(8,128)S(1)} %get-tuple-element.56.ups_ref), channel_id=1, source_target_pairs={{0,8},{8,16},{16,24},{24,32},{32,40},{40,48},{48,56},{56,64},{64,7... | collective-permute-start | bytes 122888 | tf_op jit(solution)/shard_map/ppermute | solution.py:308
  57.6 4.4 %collective-permute-start.9 = (f32[16,384]{1,0:T(8,128)S(1)}, f32[16,384]{1,0:T(8,128)S(1)}, u32[]{:S(2)}, u32[]{:S(2)}) collective-permute-start(f32[16,384]{1,0:T(8,128)S(1)} %get-tuple-element.57.downs_ref), channel_id=1, source_target_pairs={{0,504},{8,0},{16,8},{24,16},{32,24},{40,32},{48,40},{56,48},{64,5... | collective-permute-start | bytes 73736 | tf_op jit(solution)/shard_map/ppermute | solution.py:308
  61.9 1.1 shard_map.114.base_ref
  63.0 0.3 collective-permute-done.9.down_ref
  63.3 1.5 %shard_map.115 = (f32[16,1024]{1,0:T(8,128)S(1)}, f32[16,640]{1,0:T(8,128)S(1)}, f32[16,384]{1,0:T(8,128)S(1)}) custom-call(f32[16,1024]{1,0:T(8,128)S(1)} %shard_map.114.base_ref, f32[16,640]{1,0:T(8,128)S(1)} %get-tuple-element.56.ups_ref, f32[16,384]{1,0:T(8,128)S(1)} %get-tuple-element.57.downs_ref, f32[16,640]{1,0:T(8,128)S(1)} %collective-permute-done.8.up_ref, ...), custom_call_target="tpu_custom_call" | custom-call | tf_op jit(solution)/shard_map/pallas_call | solution.py:297
  64.8 4.0 %collective-permute-start.10 = (f32[16,640]{1,0:T(8,128)S(1)}, f32[16,640]{1,0:T(8,128)S(1)}, u32[]{:S(2)}, u32[]{:S(2)}) collective-permute-start(f32[16,640]{1,0:T(8,128)S(1)} %get-tuple-element.59.ups_ref), channel_id=1, source_target_pairs={{0,8},{8,16},{16,24},{24,32},{32,40},{40,48},{48,56},{56,64},{64,7... | collective-permute-start | bytes 122888 | tf_op jit(solution)/shard_map/ppermute | solution.py:308
  68.9 4.2 %collective-permute-start.11 = (f32[16,384]{1,0:T(8,128)S(1)}, f32[16,384]{1,0:T(8,128)S(1)}, u32[]{:S(2)}, u32[]{:S(2)}) collective-permute-start(f32[16,384]{1,0:T(8,128)S(1)} %get-tuple-element.60.downs_ref), channel_id=1, source_target_pairs={{0,504},{8,0},{16,8},{24,16},{32,24},{40,32},{48,40},{56,48},{64,5... | collective-permute-start | bytes 73736 | tf_op jit(solution)/shard_map/ppermute | solution.py:308
  73.0 1.1 shard_map.116.base_ref
  74.1 0.5 collective-permute-done.11.down_ref
  74.6 2.0 %shard_map.117 = (f32[16,1024]{1,0:T(8,128)}, f32[16,640]{1,0:T(8,128)S(1)}, f32[16,384]{1,0:T(8,128)S(1)}, f32[8,16,1024]{2,1,0:T(8,128)S(1)}) custom-call(f32[16,1024]{1,0:T(8,128)S(1)} %shard_map.116.base_ref, f32[16,640]{1,0:T(8,128)S(1)} %get-tuple-element.59.ups_ref, f32[16,384]{1,0:T(8,128)S(1)} %get-tuple-element.60.downs_ref, ...), custom_call_target="tpu_custom_call" | custom-call | tf_op jit(solution)/shard_map/pallas_call | solution.py:297
  76.6 0.8 copy-done.3
  77.4 4.4 %all-to-all-start = ((f32[8,16,1024]{2,1,0:T(8,128)}), f32[8,16,1024]{2,1,0:T(8,128)S(1)}, u32[]{:S(2)}, u32[]{:S(2)}) async-start(f32[8,16,1024]{2,1,0:T(8,128)} %copy-done.3), calls=%async_computation | async-start | bytes 1048576 | tf_op jit(solution)/shard_map/all_to_all | solution.py:353
  81.8 4.0 %collective-permute-start.12 = (f32[16,640]{1,0:T(8,128)S(1)}, f32[16,640]{1,0:T(8,128)S(1)}, u32[]{:S(2)}, u32[]{:S(2)}) collective-permute-start(f32[16,640]{1,0:T(8,128)S(1)} %get-tuple-element.62.ups_ref), channel_id=1, source_target_pairs={{0,8},{8,16},{16,24},{24,32},{32,40},{40,48},{48,56},{56,64},{64,7... | collective-permute-start | bytes 122888 | tf_op jit(solution)/shard_map/ppermute | solution.py:308
  85.8 4.2 %collective-permute-start.13 = (f32[16,384]{1,0:T(8,128)S(1)}, f32[16,384]{1,0:T(8,128)S(1)}, u32[]{:S(2)}, u32[]{:S(2)}) collective-permute-start(f32[16,384]{1,0:T(8,128)S(1)} %get-tuple-element.63.downs_ref), channel_id=1, source_target_pairs={{0,504},{8,0},{16,8},{24,16},{32,24},{40,32},{48,40},{56,48},{64,5... | collective-permute-start | bytes 73736 | tf_op jit(solution)/shard_map/ppermute | solution.py:308
  90.0 1.1 shard_map.118.base_ref
  91.1 0.5 collective-permute-done.13.down_ref
  91.6 0.6 all-to-all-done
  92.2 1.7 %shard_map.119 = f32[4,32,128]{2,1,0:T(8,128)S(1)} custom-call(f32[16,1024]{1,0:T(8,128)S(1)} %shard_map.118.base_ref, f32[16,640]{1,0:T(8,128)S(1)} %get-tuple-element.62.ups_ref, f32[16,384]{1,0:T(8,128)S(1)} %get-tuple-element.63.downs_ref, f32[16,640]{1,0:T(8,128)S(1)} %collective-permute-done.12.up_ref, f32[16,384]{1,0:T(8,128)S(1)} %collective-permute-done.13.down_ref, ...), custom_call_target="tpu_custom_call" | custom-call | tf_op jit(solution)/shard_map/pallas_call | solution.py:297
  93.9 12.9 %all_to_all.15.parts_ref = f32[4,32,128]{2,1,0:T(8,128)S(1)} all-to-all(f32[4,32,128]{2,1,0:T(8,128)S(1)} %shard_map.119), channel_id=1, replica_groups={{0,8,16,24},{32,40,48,56},{64,72,80,88},{96,104,112,120},{128,136,144,1..., dimensions={0} | all-to-all | bytes 131072 | tf_op jit(solution)/shard_map/all_to_all | solution.py:364
  106.8 37.5 %all_to_all.16.parts_ref = f32[16,32,128]{2,1,0:T(8,128)S(1)} all-to-all(f32[16,32,128]{2,1,0:T(8,128)S(1)} %shard_map.120), channel_id=1, replica_groups={{0,32,64,96,128,160,192,224,256,288,320,352,384,416,448,480},{8,40,72,1..., dimensions={0} | all-to-all | bytes 524288 | tf_op jit(solution)/shard_map/all_to_all | solution.py:366
  144.2 0.6 shard_map.121
  (22 shorter events, 0.1 us)
Async XLA Ops:
  0.6 1.1 copy-start.6
  0.6 1.1 copy-start.1
  0.7 1.1 copy-start
  1.7 0.7 copy-start.4
  1.7 0.7 copy-start.7
  1.7 0.7 copy-start.8
  3.5 13.5 %collective-permute-start = (f32[48,640]{1,0:T(8,128)S(1)}, f32[48,640]{1,0:T(8,128)S(1)}, u32[]{:S(2)}, u32[]{:S(2)}) collective-permute-start(f32[48,640]{1,0:T(8,128)S(1)} %get-tuple-element.38.ups_ref), channel_id=1, source_target_pairs={{0,8},{8,16},{16,24},{24,32},{32,40},{40,48},{48,56},{56,64},{64,7... | collective-permute-start | bytes 368648 | tf_op jit(solution)/shard_map/ppermute | solution.py:308
  7.0 1.2 copy-start.2
  10.9 6.1 %collective-permute-start.1 = (f32[24,384]{1,0:T(8,128)S(1)}, f32[24,384]{1,0:T(8,128)S(1)}, u32[]{:S(2)}, u32[]{:S(2)}) collective-permute-start(f32[24,384]{1,0:T(8,128)S(1)} %get-tuple-element.39.downs_ref), channel_id=1, source_target_pairs={{0,504},{8,0},{16,8},{24,16},{32,24},{40,32},{48,40},{56,48},{64,5... | collective-permute-start | bytes 110600 | tf_op jit(solution)/shard_map/ppermute | solution.py:308
  19.7 9.8 %collective-permute-start.2 = (f32[16,640]{1,0:T(8,128)S(1)}, f32[16,640]{1,0:T(8,128)S(1)}, u32[]{:S(2)}, u32[]{:S(2)}) collective-permute-start(f32[16,640]{1,0:T(8,128)S(1)} %get-tuple-element.47.ups_ref), channel_id=1, source_target_pairs={{0,8},{8,16},{16,24},{24,32},{32,40},{40,48},{48,56},{56,64},{64,7... | collective-permute-start | bytes 122888 | tf_op jit(solution)/shard_map/ppermute | solution.py:308
  22.9 6.5 %collective-permute-start.3 = (f32[16,384]{1,0:T(8,128)S(1)}, f32[16,384]{1,0:T(8,128)S(1)}, u32[]{:S(2)}, u32[]{:S(2)}) collective-permute-start(f32[16,384]{1,0:T(8,128)S(1)} %get-tuple-element.48.downs_ref), channel_id=1, source_target_pairs={{0,504},{8,0},{16,8},{24,16},{32,24},{40,32},{48,40},{56,48},{64,5... | collective-permute-start | bytes 73736 | tf_op jit(solution)/shard_map/ppermute | solution.py:308
  31.0 9.8 %collective-permute-start.4 = (f32[16,640]{1,0:T(8,128)S(1)}, f32[16,640]{1,0:T(8,128)S(1)}, u32[]{:S(2)}, u32[]{:S(2)}) collective-permute-start(f32[16,640]{1,0:T(8,128)S(1)} %get-tuple-element.50.ups_ref), channel_id=1, source_target_pairs={{0,8},{8,16},{16,24},{24,32},{32,40},{40,48},{48,56},{56,64},{64,7... | collective-permute-start | bytes 122888 | tf_op jit(solution)/shard_map/ppermute | solution.py:308
  35.0 5.7 %collective-permute-start.5 = (f32[16,384]{1,0:T(8,128)S(1)}, f32[16,384]{1,0:T(8,128)S(1)}, u32[]{:S(2)}, u32[]{:S(2)}) collective-permute-start(f32[16,384]{1,0:T(8,128)S(1)} %get-tuple-element.51.downs_ref), channel_id=1, source_target_pairs={{0,504},{8,0},{16,8},{24,16},{32,24},{40,32},{48,40},{56,48},{64,5... | collective-permute-start | bytes 73736 | tf_op jit(solution)/shard_map/ppermute | solution.py:308
  42.3 9.8 %collective-permute-start.6 = (f32[16,640]{1,0:T(8,128)S(1)}, f32[16,640]{1,0:T(8,128)S(1)}, u32[]{:S(2)}, u32[]{:S(2)}) collective-permute-start(f32[16,640]{1,0:T(8,128)S(1)} %get-tuple-element.53.ups_ref), channel_id=1, source_target_pairs={{0,8},{8,16},{16,24},{24,32},{32,40},{40,48},{48,56},{56,64},{64,7... | collective-permute-start | bytes 122888 | tf_op jit(solution)/shard_map/ppermute | solution.py:308
  46.3 5.7 %collective-permute-start.7 = (f32[16,384]{1,0:T(8,128)S(1)}, f32[16,384]{1,0:T(8,128)S(1)}, u32[]{:S(2)}, u32[]{:S(2)}) collective-permute-start(f32[16,384]{1,0:T(8,128)S(1)} %get-tuple-element.54.downs_ref), channel_id=1, source_target_pairs={{0,504},{8,0},{16,8},{24,16},{32,24},{40,32},{48,40},{56,48},{64,5... | collective-permute-start | bytes 73736 | tf_op jit(solution)/shard_map/ppermute | solution.py:308
  53.5 9.8 %collective-permute-start.8 = (f32[16,640]{1,0:T(8,128)S(1)}, f32[16,640]{1,0:T(8,128)S(1)}, u32[]{:S(2)}, u32[]{:S(2)}) collective-permute-start(f32[16,640]{1,0:T(8,128)S(1)} %get-tuple-element.56.ups_ref), channel_id=1, source_target_pairs={{0,8},{8,16},{16,24},{24,32},{32,40},{40,48},{48,56},{56,64},{64,7... | collective-permute-start | bytes 122888 | tf_op jit(solution)/shard_map/ppermute | solution.py:308
  57.6 5.7 %collective-permute-start.9 = (f32[16,384]{1,0:T(8,128)S(1)}, f32[16,384]{1,0:T(8,128)S(1)}, u32[]{:S(2)}, u32[]{:S(2)}) collective-permute-start(f32[16,384]{1,0:T(8,128)S(1)} %get-tuple-element.57.downs_ref), channel_id=1, source_target_pairs={{0,504},{8,0},{16,8},{24,16},{32,24},{40,32},{48,40},{56,48},{64,5... | collective-permute-start | bytes 73736 | tf_op jit(solution)/shard_map/ppermute | solution.py:308
  64.8 9.8 %collective-permute-start.10 = (f32[16,640]{1,0:T(8,128)S(1)}, f32[16,640]{1,0:T(8,128)S(1)}, u32[]{:S(2)}, u32[]{:S(2)}) collective-permute-start(f32[16,640]{1,0:T(8,128)S(1)} %get-tuple-element.59.ups_ref), channel_id=1, source_target_pairs={{0,8},{8,16},{16,24},{24,32},{32,40},{40,48},{48,56},{56,64},{64,7... | collective-permute-start | bytes 122888 | tf_op jit(solution)/shard_map/ppermute | solution.py:308
  68.9 5.7 %collective-permute-start.11 = (f32[16,384]{1,0:T(8,128)S(1)}, f32[16,384]{1,0:T(8,128)S(1)}, u32[]{:S(2)}, u32[]{:S(2)}) collective-permute-start(f32[16,384]{1,0:T(8,128)S(1)} %get-tuple-element.60.downs_ref), channel_id=1, source_target_pairs={{0,504},{8,0},{16,8},{24,16},{32,24},{40,32},{48,40},{56,48},{64,5... | collective-permute-start | bytes 73736 | tf_op jit(solution)/shard_map/ppermute | solution.py:308
  76.6 0.8 copy-start.3
  77.4 12.6 %copy-start.5 = (f32[16,1024]{1,0:T(8,128)S(1)}, f32[16,1024]{1,0:T(8,128)}, u32[]{:S(2)}) copy-start(f32[16,1024]{1,0:T(8,128)} %get-tuple-element.32.v_ref) | copy-start | bytes 196612
  77.4 14.8 %all-to-all-start = ((f32[8,16,1024]{2,1,0:T(8,128)}), f32[8,16,1024]{2,1,0:T(8,128)S(1)}, u32[]{:S(2)}, u32[]{:S(2)}) async-start(f32[8,16,1024]{2,1,0:T(8,128)} %copy-done.3), calls=%async_computation | async-start | bytes 1048576 | tf_op jit(solution)/shard_map/all_to_all | solution.py:353
  81.8 9.7 %collective-permute-start.12 = (f32[16,640]{1,0:T(8,128)S(1)}, f32[16,640]{1,0:T(8,128)S(1)}, u32[]{:S(2)}, u32[]{:S(2)}) collective-permute-start(f32[16,640]{1,0:T(8,128)S(1)} %get-tuple-element.62.ups_ref), channel_id=1, source_target_pairs={{0,8},{8,16},{16,24},{24,32},{32,40},{40,48},{48,56},{56,64},{64,7... | collective-permute-start | bytes 122888 | tf_op jit(solution)/shard_map/ppermute | solution.py:308
  85.8 5.7 %collective-permute-start.13 = (f32[16,384]{1,0:T(8,128)S(1)}, f32[16,384]{1,0:T(8,128)S(1)}, u32[]{:S(2)}, u32[]{:S(2)}) collective-permute-start(f32[16,384]{1,0:T(8,128)S(1)} %get-tuple-element.63.downs_ref), channel_id=1, source_target_pairs={{0,504},{8,0},{16,8},{24,16},{32,24},{40,32},{48,40},{56,48},{64,5... | collective-permute-start | bytes 73736 | tf_op jit(solution)/shard_map/ppermute | solution.py:308

commit v5 on v4

--- a/solution.py
+++ b/solution.py
@@ -125,11 +125,11 @@
     down_ref[16:17, 0:LANES] = atoms
 
 
-def local_kernel(conn_ref, send_ref, element_ref, proj_ref, down_ref, e_ref, maps_ref, p_ref, pt_ref, downo_ref):
-    downo_ref[...] = down_ref[...]
-    high, low = split2(element_ref[...])
-    e_ref[0] = high
-    e_ref[1] = low
+def split_kernel(x_ref, out_ref):
+    out_ref[0], out_ref[1] = split2(x_ref[...])
+
+
+def local_kernel(conn_ref, send_ref, proj_ref, maps_ref, p_ref, pt_ref):
     least = [jnp.full((1, LANES), 4.0 * NPC, F32)] * (NODES // LANES)
     most = [jnp.full((1, LANES), -1.0, F32)] * (NODES // LANES)
     position = row_iota(NPC, LANES).astype(F32)
@@ -210,8 +210,10 @@
     p_ref[0], p_ref[1] = split2(spread)
 
 
-def inner_kernel(mode, v_ref, prev_ref, conn_ref, maps_ref, pot_ref, e_ref, base_ref):
+def inner_kernel(mode, v_ref, prev_ref, conn_ref, maps_ref, pot_ref, e_ref, base_ref, *result_ref):
     v = v_ref[...]
+    for ref in result_ref:
+        ref[...] = v
     sources = blocks_of(v)
     cells = [pick_row(sources, conn_ref[c : c + 1, :]) for c in range(3)]
     x_high, x_low = split2(jnp.concatenate(cells, axis=0))
@@ -229,14 +231,29 @@
         base_ref[:, here] = h
 
 
-def outer(ups_ref, downs_ref, up_ref, down_ref, conn_ref, index_ref, e_ref, p_ref, pe_ref, k_ref):
-    edge = ups_ref[0:BANDS, 0:NPC] + pick_row(blocks_of(down_ref[0:BANDS, 0:GHOST]), conn_ref[3:4, :] - NODES)
-    low = up_ref[0:BANDS, 0:NPC] + pick_row(blocks_of(downs_ref[0:BANDS, 0:GHOST]), index_ref[3:4, 0:NPC])
+def is_odd():
+    return lax.rem(lax.axis_index("fe"), 2) == 1
+
+
+def received(paired, one_ref, two_ref):
+    if not paired:
+        up, down = one_ref, two_ref
+        return up[0:BANDS, 0:NPC], up[0:BANDS, NPC:], down[0:BANDS, 0:GHOST], down[0:BANDS, GHOST:]
+    odd = is_odd()
+    one, two = one_ref[...], two_ref[...]
+    up, down = jnp.where(odd, two, one), jnp.where(odd, one[:, GHOST:], two[:, GHOST:])
+    return up[:, 0:NPC], up[:, NPC:], down[:, 0:GHOST], down[:, GHOST:]
+
+
+def outer(paired, ups_ref, downs_ref, one_ref, two_ref, conn_ref, index_ref, e_ref, p_ref, pe_ref, k_ref):
+    from_lower, lower_partials, from_upper, upper_partials = received(paired, one_ref, two_ref)
+    edge = ups_ref[0:BANDS, 0:NPC] + pick_row(blocks_of(from_upper), conn_ref[3:4, :] - NODES)
+    low = from_lower + pick_row(blocks_of(downs_ref[0:BANDS, 0:GHOST]), index_ref[3:4, 0:NPC])
     x_high, x_low = split2(jnp.concatenate([edge, low], axis=0))
     wide = product(x_high, x_low, pe_ref[0], pe_ref[1])
     which = lane_iota(BANDS, LANES) >> 5
     edges = jnp.where(which == 0, wide[:BANDS], jnp.where(which == 1, wide[BANDS:], 0.0))
-    partials = jnp.concatenate([ups_ref[0:BANDS, NPC:], edges, down_ref[0:BANDS, GHOST:], up_ref[0:BANDS, NPC:]], axis=1)
+    partials = jnp.concatenate([ups_ref[0:BANDS, NPC:], edges, upper_partials, lower_partials], axis=1)
     sums = dot(jnp.concatenate(split3(partials), axis=0), k_ref[...])
     w_high, w_low = split2(sums[0:16] + sums[16:32] + sums[32:48])
     nonlocal_part = product(w_high, w_low, p_ref[0], p_ref[1])
@@ -250,9 +267,9 @@
     return jnp.concatenate(out, axis=1) + nonlocal_part
 
 
-def outer_kernel(factor, base_ref, ups_ref, downs_ref, up_ref, down_ref, conn_ref, index_ref, e_ref, p_ref, pe_ref, k_ref,
-                 send_ref, pt_ref, new_ref, upo_ref, downo_ref, *copies_ref):
-    h = outer(ups_ref, downs_ref, up_ref, down_ref, conn_ref, index_ref, e_ref, p_ref, pe_ref, k_ref)
+def outer_kernel(paired, factor, base_ref, ups_ref, downs_ref, one_ref, two_ref, conn_ref, index_ref, e_ref, p_ref, pe_ref, k_ref,
+                 send_ref, pt_ref, new_ref, upo_ref, downo_ref, oneo_ref, twoo_ref, *copies_ref):
+    h = outer(paired, ups_ref, downs_ref, one_ref, two_ref, conn_ref, index_ref, e_ref, p_ref, pe_ref, k_ref)
     new = base_ref[...] + h * factor
     new_ref[...] = new
     for ref in copies_ref:
@@ -260,11 +277,16 @@
             ref[i] = new
     v_high, v_low = split2(new)
     pack_message(new, product(v_high, v_low, pt_ref[0], pt_ref[1]), conn_ref, send_ref, upo_ref, downo_ref)
-
-
-def gram_kernel(base_ref, ups_ref, downs_ref, up_ref, down_ref, conn_ref, index_ref, e_ref, p_ref, pe_ref, k_ref,
+    up = upo_ref[...]
+    down = jnp.concatenate([jnp.zeros((BANDS, GHOST), F32), downo_ref[...]], axis=1)
+    odd = is_odd()
+    oneo_ref[...] = jnp.where(odd, up, down)
+    twoo_ref[...] = jnp.where(odd, down, up)
+
+
+def gram_kernel(base_ref, ups_ref, downs_ref, one_ref, two_ref, conn_ref, index_ref, e_ref, p_ref, pe_ref, k_ref,
                 v_ref, all_ref, out_ref):
-    h = base_ref[...] + outer(ups_ref, downs_ref, up_ref, down_ref, conn_ref, index_ref, e_ref, p_ref, pe_ref, k_ref)
+    h = base_ref[...] + outer(True, ups_ref, downs_ref, one_ref, two_ref, conn_ref, index_ref, e_ref, p_ref, pe_ref, k_ref)
     s_high, s_low = split2(jnp.concatenate([h, v_ref[...]], axis=0))
     a_high, a_low = split2(all_ref[...])
     both = dot_nt(jnp.concatenate([s_high, s_low], axis=0), a_high)
@@ -306,6 +328,11 @@
 def shifted(block, distance):
     size = lax.axis_size("fe")
     return lax.ppermute(block, "fe", [(i, (i + distance) % size) for i in range(size)])
+
+
+def swapped(block, first):
+    size = lax.axis_size("fe")
+    return lax.ppermute(block, "fe", [(i, (i + 1 if i % 2 == first else i - 1) % size) for i in range(size)])
 
 
 def on_device(wavefunctions, potential, element_matrix, projectors, coupling, connectivity, send_list, atom_of_cell):
@@ -318,20 +345,21 @@
         [VM, VM, VM, SM, VM, VM, VM],
         v, conn, send, atom_of_cell, projectors, pot, couple,
     )
-    up = shifted(ups, 1)
-    e, maps, pn, pt, downs = call(
+    up, down = shifted(ups, 1), shifted(downs, -1)
+    maps, pn, pt = call(
         local_kernel,
-        [((2, NPC, NPC), BF16), ((8, NODES), jnp.int32), ((4 * SLOT, NODES), F32), ((2, NODES, LANES), BF16), ((24, 384), F32)],
-        [VM] * 5,
-        conn, send, element_matrix, projectors, downs,
-    )
-    down = shifted(downs, -1)
+        [((8, NODES), jnp.int32), ((4 * SLOT, NODES), F32), ((2, NODES, LANES), BF16)],
+        [VM] * 3,
+        conn, send, projectors,
+    )
+    (e,) = call(split_kernel, [((2, NPC, NPC), BF16)], [VM], element_matrix)
 
     def inner(mode, v, previous):
-        return call(functools.partial(inner_kernel, mode), [((BANDS, NODES), F32)], [VM] * 6, v, previous, conn, maps, pot, e)[0]
+        outs = [((BANDS, NODES), F32)] * (2 if mode == "last" else 1)
+        return call(functools.partial(inner_kernel, mode), outs, [VM] * 6, v, previous, conn, maps, pot, e)
 
     previous = current = v
-    base = inner("first", current, previous)
+    (base,) = inner("first", current, previous)
     p, pe, k, index = call(
         joined_kernel,
         [((2, 256, NODES), BF16), ((2, NPC, LANES), BF16), ((512, 256), BF16), ((8, NODES), jnp.int32)],
@@ -342,17 +370,17 @@
     for step in range(DEGREE):
         last = step == DEGREE - 1
         copied = [((lax.axis_size("band"), BANDS, NODES), F32)] if last else []
-        new, ups, downs, *copied = call(
-            functools.partial(outer_kernel, (1.0 if step == 0 else 2.0) / HALF_WIDTH),
-            [((BANDS, NODES), F32), ((BANDS, 640), F32), ((BANDS, 384), F32)] + copied,
+        new, ups, downs, one, two, *copied = call(
+            functools.partial(outer_kernel, step > 0, (1.0 if step == 0 else 2.0) / HALF_WIDTH),
+            [((BANDS, NODES), F32), ((BANDS, 640), F32), ((BANDS, 384), F32), ((BANDS, 640), F32), ((BANDS, 640), F32)] + copied,
             [VM] * 13,
             base, ups, downs, up, down, *shared, send, pt,
         )
         previous, current = current, new
         if last:
             everyone = lax.all_to_all(copied[0], "band", 0, 0).reshape(-1, NODES)
-        up, down = shifted(ups, 1), shifted(downs, -1)
-        base = inner("last" if last else "middle", current, previous)
+        up, down = swapped(one, 1), swapped(two, 0)
+        base, *result = inner("last" if last else "middle", current, current if last else previous)
     (copies,) = call(
         gram_kernel,
         [((4, 32, LANES), F32)],
@@ -370,7 +398,7 @@
         [VM],
         parts,
     )
-    return current, projected.T, correlation.T
+    return result[0], projected.T, correlation.T
 
 
 def solution(mesh):

time: 146 us -> 140 us (0.959)
  waiting for transfers between devices: 3.73 us -> 17.2 us
  blocking collectives: 50.4 us -> 39.1 us
  starting transfers between devices: 61.9 us -> 54.1 us
    ppermute x14 -> x2, starting transfers between devices: 57.4 us -> 7.95 us  [shifted(): lax.ppermute(block, 'fe', [(i, (i + distance) % size) for i in range(size)])]
    ppermute x0 -> x12, starting transfers between devices: none -> 41.8 us  [swapped(): lax.ppermute(block, 'fe', [(i, (i + 1 if i % 2 == first else i - 1) % siz...]
    ppermute x0 -> x12, waiting for transfers between devices: none -> 17.2 us  [swapped(): lax.ppermute(block, 'fe', [(i, (i + 1 if i % 2 == first else i - 1) % siz...]
    all_to_all x1, blocking collectives: 37.5 us -> 31.1 us  [on_device(): parts = lax.all_to_all(copies, 'fe', 0, 0, axis_index_groups=far)]
    all_to_all x1, blocking collectives: 12.9 us -> 8.01 us  [on_device(): parts = lax.all_to_all(copies, 'fe', 0, 0, axis_index_groups=near)]
    ppermute x14 -> x2, waiting for transfers between devices: 3.13 us -> 0.01 us  [shifted(): lax.ppermute(block, 'fe', [(i, (i + distance) % size) for i in range(size)])]
    pallas_call x19 -> x20, Pallas kernels: 24.4 us -> 24.5 us  [call(): pl.pallas_call(kernel, out_shape=[jax.ShapeDtypeStruct(s, t) for s, t in...]
    unnamed x19 -> x17, local copies, waits for them, and re-layouts: 3.68 us -> 3.67 us
  transfers between devices with their start and end apart: 15 -> 15, of which waited for: 8 -> 9; matrix products, arithmetic and copies ran while one was open for 0% -> 0% of each run, Pallas kernels for 7% -> 7%
where the time goes in v5:
time: 140 us
  starting transfers between devices  54.1 us (39%)
  blocking collectives  39.1 us (28%)
  Pallas kernels  24.5 us (18%)
  waiting for transfers between devices  17.2 us (12%)
  local copies, waits for them, and re-layouts  3.67 us (3%)
    ppermute x12, starting transfers between devices, swapped(): lax.ppermute(block, 'fe', [(i, (i + 1 if i % 2 == first else i - 1) % siz...  41.8 us
    all_to_all x1, blocking collectives, on_device(): parts = lax.all_to_all(copies, 'fe', 0, 0, axis_index_groups=far)  31.1 us
    pallas_call x20, Pallas kernels, call(): pl.pallas_call(kernel, out_shape=[jax.ShapeDtypeStruct(s, t) for s, t in...  24.5 us
    ppermute x12, waiting for transfers between devices, swapped(): lax.ppermute(block, 'fe', [(i, (i + 1 if i % 2 == first else i - 1) % siz...  17.2 us
    all_to_all x1, blocking collectives, on_device(): parts = lax.all_to_all(copies, 'fe', 0, 0, axis_index_groups=near)  8.01 us
    ppermute x2, starting transfers between devices, shifted(): lax.ppermute(block, 'fe', [(i, (i + distance) % size) for i in range(size)])  7.95 us
    all_to_all x1, starting transfers between devices, on_device(): everyone = lax.all_to_all(copied[0], 'band', 0, 0).reshape(-1, NODES)  4.3 us
    unnamed x17, local copies, waits for them, and re-layouts  3.67 us
  transfers between devices with their start and end apart: 15, of which 9 were waited for; matrix products, arithmetic and copies ran while one was open for 0% of the time, Pallas kernels for 7%

profile of v5, /device:TPU:32, one launch (start us, length us, event | category | flops | bytes accessed | tf_op | source)
XLA Modules:
  0.0 139.5 jit_solution(2407987741353038284)
XLA Ops:
  0.7 1.0 copy.11.proj_ref
  1.7 0.6 copy-done.4
  2.4 1.1 shard_map.106
  3.5 3.5 %collective-permute-start = (f32[48,640]{1,0:T(8,128)S(1)}, f32[48,640]{1,0:T(8,128)S(1)}, u32[]{:S(2)}, u32[]{:S(2)}) collective-permute-start(f32[48,640]{1,0:T(8,128)S(1)} %get-tuple-element.48.ups_ref), channel_id=1, source_target_pairs={{0,8},{8,16},{16,24},{24,32},{32,40},{40,48},{48,56},{56,64},{64,7... | collective-permute-start | bytes 368648 | tf_op jit(solution)/shard_map/ppermute | solution.py:330
  7.0 4.5 %collective-permute-start.1 = (f32[24,384]{1,0:T(8,128)S(1)}, f32[24,384]{1,0:T(8,128)S(1)}, u32[]{:S(2)}, u32[]{:S(2)}) collective-permute-start(f32[24,384]{1,0:T(8,128)S(1)} %get-tuple-element.49.downs_ref), channel_id=1, source_target_pairs={{0,504},{8,0},{16,8},{24,16},{32,24},{40,32},{48,40},{56,48},{64,5... | collective-permute-start | bytes 110600 | tf_op jit(solution)/shard_map/ppermute | solution.py:330
  11.5 2.5 %shard_map.103 = (s32[8,1024]{1,0:T(8,128)S(1)}, f32[128,1024]{1,0:T(8,128)S(1)}, bf16[2,1024,128]{2,1,0:T(8,128)(2,1)S(1)}) custom-call(s32[4,512]{1,0:T(4,128)S(1)} %copy-done, s32[1,256]{1,0:T(1,128)S(1)} %bitcast.18, f32[4,18,512]{2,1,0:T(8,128)S(1)} %copy.11.proj_ref), custom_call_target="tpu_custom_call" | custom-call | tf_op jit(solution)/shard_map/pallas_call | solution.py:319
  14.0 1.2 copy-done.2
  15.3 1.1 shard_map.105.base_ref
  16.4 1.1 shard_map.107
  17.6 1.5 %shard_map.108 = (f32[16,1024]{1,0:T(8,128)S(1)}, f32[16,640]{1,0:T(8,128)S(1)}, f32[16,384]{1,0:T(8,128)S(1)}, f32[16,640]{1,0:T(8,128)S(1)}, f32[16,640]{1,0:T(8,128)S(1)}) custom-call(f32[16,1024]{1,0:T(8,128)S(1)} %shard_map.105.base_ref, f32[48,640]{1,0:T(8,128)S(1)} %get-tuple-element.48.ups_ref, f32[24,384]{1,0:T(8,128)S(1)} %get-tuple-element.49.downs_ref, ...), custom_call_target="tpu_custom_call" | custom-call | tf_op jit(solution)/shard_map/pallas_call | solution.py:319
  19.1 3.0 %collective-permute-start.2 = (f32[16,640]{1,0:T(8,128)S(1)}, f32[16,640]{1,0:T(8,128)S(1)}, u32[]{:S(2)}, u32[]{:S(2)}) collective-permute-start(f32[16,640]{1,0:T(8,128)S(1)} %get-tuple-element.59), channel_id=1, source_target_pairs={{0,504},{8,16},{16,8},{24,32},{32,24},{40,48},{48,40},{56,64},{64,... | collective-permute-start | bytes 122888 | tf_op jit(solution)/shard_map/ppermute | solution.py:335
  22.1 1.9 %collective-permute-start.3 = (f32[16,640]{1,0:T(8,128)S(1)}, f32[16,640]{1,0:T(8,128)S(1)}, u32[]{:S(2)}, u32[]{:S(2)}) collective-permute-start(f32[16,640]{1,0:T(8,128)S(1)} %get-tuple-element.60), channel_id=1, source_target_pairs={{0,8},{8,0},{16,24},{24,16},{32,40},{40,32},{48,56},{56,48},{64,72... | collective-permute-start | bytes 122888 | tf_op jit(solution)/shard_map/ppermute | solution.py:335
  24.0 1.1 shard_map.109.base_ref
  25.1 2.0 %collective-permute-done.2.one_ref = f32[16,640]{1,0:T(8,128)S(1)} collective-permute-done((f32[16,640]{1,0:T(8,128)S(1)}, f32[16,640]{1,0:T(8,128)S(1)}, u32[]{:S(2)}, u32[]{:S(2)}) %collective-permute-start.2) | collective-permute-done | bytes 40992 | tf_op jit(solution)/shard_map/ppermute | solution.py:335
  27.1 0.9 collective-permute-done.3.two_ref
  28.0 1.5 %shard_map.110 = (f32[16,1024]{1,0:T(8,128)S(1)}, f32[16,640]{1,0:T(8,128)S(1)}, f32[16,384]{1,0:T(8,128)S(1)}, f32[16,640]{1,0:T(8,128)S(1)}, f32[16,640]{1,0:T(8,128)S(1)}) custom-call(f32[16,1024]{1,0:T(8,128)S(1)} %shard_map.109.base_ref, f32[16,640]{1,0:T(8,128)S(1)} %get-tuple-element.57.ups_ref, f32[16,384]{1,0:T(8,128)S(1)} %get-tuple-element.58.downs_ref, ...), custom_call_target="tpu_custom_call" | custom-call | tf_op jit(solution)/shard_map/pallas_call | solution.py:319
  29.5 5.0 %collective-permute-start.4 = (f32[16,640]{1,0:T(8,128)S(1)}, f32[16,640]{1,0:T(8,128)S(1)}, u32[]{:S(2)}, u32[]{:S(2)}) collective-permute-start(f32[16,640]{1,0:T(8,128)S(1)} %get-tuple-element.64), channel_id=1, source_target_pairs={{0,504},{8,16},{16,8},{24,32},{32,24},{40,48},{48,40},{56,64},{64,... | collective-permute-start | bytes 122888 | tf_op jit(solution)/shard_map/ppermute | solution.py:335
  34.5 1.9 %collective-permute-start.5 = (f32[16,640]{1,0:T(8,128)S(1)}, f32[16,640]{1,0:T(8,128)S(1)}, u32[]{:S(2)}, u32[]{:S(2)}) collective-permute-start(f32[16,640]{1,0:T(8,128)S(1)} %get-tuple-element.65), channel_id=1, source_target_pairs={{0,8},{8,0},{16,24},{24,16},{32,40},{40,32},{48,56},{56,48},{64,72... | collective-permute-start | bytes 122888 | tf_op jit(solution)/shard_map/ppermute | solution.py:335
  36.4 1.1 shard_map.111.base_ref
  37.5 2.9 %collective-permute-done.5.two_ref = f32[16,640]{1,0:T(8,128)S(1)} collective-permute-done((f32[16,640]{1,0:T(8,128)S(1)}, f32[16,640]{1,0:T(8,128)S(1)}, u32[]{:S(2)}, u32[]{:S(2)}) %collective-permute-start.5) | collective-permute-done | bytes 40992 | tf_op jit(solution)/shard_map/ppermute | solution.py:335
  40.4 1.5 %shard_map.112 = (f32[16,1024]{1,0:T(8,128)S(1)}, f32[16,640]{1,0:T(8,128)S(1)}, f32[16,384]{1,0:T(8,128)S(1)}, f32[16,640]{1,0:T(8,128)S(1)}, f32[16,640]{1,0:T(8,128)S(1)}) custom-call(f32[16,1024]{1,0:T(8,128)S(1)} %shard_map.111.base_ref, f32[16,640]{1,0:T(8,128)S(1)} %get-tuple-element.62.ups_ref, f32[16,384]{1,0:T(8,128)S(1)} %get-tuple-element.63.downs_ref, ...), custom_call_target="tpu_custom_call" | custom-call | tf_op jit(solution)/shard_map/pallas_call | solution.py:319
  41.9 8.1 %collective-permute-start.6 = (f32[16,640]{1,0:T(8,128)S(1)}, f32[16,640]{1,0:T(8,128)S(1)}, u32[]{:S(2)}, u32[]{:S(2)}) collective-permute-start(f32[16,640]{1,0:T(8,128)S(1)} %get-tuple-element.69), channel_id=1, source_target_pairs={{0,504},{8,16},{16,8},{24,32},{32,24},{40,48},{48,40},{56,64},{64,... | collective-permute-start | bytes 122888 | tf_op jit(solution)/shard_map/ppermute | solution.py:335
  50.0 1.9 %collective-permute-start.7 = (f32[16,640]{1,0:T(8,128)S(1)}, f32[16,640]{1,0:T(8,128)S(1)}, u32[]{:S(2)}, u32[]{:S(2)}) collective-permute-start(f32[16,640]{1,0:T(8,128)S(1)} %get-tuple-element.70), channel_id=1, source_target_pairs={{0,8},{8,0},{16,24},{24,16},{32,40},{40,32},{48,56},{56,48},{64,72... | collective-permute-start | bytes 122888 | tf_op jit(solution)/shard_map/ppermute | solution.py:335
  51.9 1.1 shard_map.113.base_ref
  53.0 2.9 %collective-permute-done.7.two_ref = f32[16,640]{1,0:T(8,128)S(1)} collective-permute-done((f32[16,640]{1,0:T(8,128)S(1)}, f32[16,640]{1,0:T(8,128)S(1)}, u32[]{:S(2)}, u32[]{:S(2)}) %collective-permute-start.7) | collective-permute-done | bytes 40992 | tf_op jit(solution)/shard_map/ppermute | solution.py:335
  55.9 1.5 %shard_map.114 = (f32[16,1024]{1,0:T(8,128)S(1)}, f32[16,640]{1,0:T(8,128)S(1)}, f32[16,384]{1,0:T(8,128)S(1)}, f32[16,640]{1,0:T(8,128)S(1)}, f32[16,640]{1,0:T(8,128)S(1)}) custom-call(f32[16,1024]{1,0:T(8,128)S(1)} %shard_map.113.base_ref, f32[16,640]{1,0:T(8,128)S(1)} %get-tuple-element.67.ups_ref, f32[16,384]{1,0:T(8,128)S(1)} %get-tuple-element.68.downs_ref, ...), custom_call_target="tpu_custom_call" | custom-call | tf_op jit(solution)/shard_map/pallas_call | solution.py:319
  57.4 5.0 %collective-permute-start.8 = (f32[16,640]{1,0:T(8,128)S(1)}, f32[16,640]{1,0:T(8,128)S(1)}, u32[]{:S(2)}, u32[]{:S(2)}) collective-permute-start(f32[16,640]{1,0:T(8,128)S(1)} %get-tuple-element.74), channel_id=1, source_target_pairs={{0,504},{8,16},{16,8},{24,32},{32,24},{40,48},{48,40},{56,64},{64,... | collective-permute-start | bytes 122888 | tf_op jit(solution)/shard_map/ppermute | solution.py:335
  62.4 2.1 %collective-permute-start.9 = (f32[16,640]{1,0:T(8,128)S(1)}, f32[16,640]{1,0:T(8,128)S(1)}, u32[]{:S(2)}, u32[]{:S(2)}) collective-permute-start(f32[16,640]{1,0:T(8,128)S(1)} %get-tuple-element.75), channel_id=1, source_target_pairs={{0,8},{8,0},{16,24},{24,16},{32,40},{40,32},{48,56},{56,48},{64,72... | collective-permute-start | bytes 122888 | tf_op jit(solution)/shard_map/ppermute | solution.py:335
  64.5 1.1 shard_map.115.base_ref
  65.6 2.7 %collective-permute-done.9.two_ref = f32[16,640]{1,0:T(8,128)S(1)} collective-permute-done((f32[16,640]{1,0:T(8,128)S(1)}, f32[16,640]{1,0:T(8,128)S(1)}, u32[]{:S(2)}, u32[]{:S(2)}) %collective-permute-start.9) | collective-permute-done | bytes 40992 | tf_op jit(solution)/shard_map/ppermute | solution.py:335
  68.3 1.5 %shard_map.116 = (f32[16,1024]{1,0:T(8,128)S(1)}, f32[16,640]{1,0:T(8,128)S(1)}, f32[16,384]{1,0:T(8,128)S(1)}, f32[16,640]{1,0:T(8,128)S(1)}, f32[16,640]{1,0:T(8,128)S(1)}) custom-call(f32[16,1024]{1,0:T(8,128)S(1)} %shard_map.115.base_ref, f32[16,640]{1,0:T(8,128)S(1)} %get-tuple-element.72.ups_ref, f32[16,384]{1,0:T(8,128)S(1)} %get-tuple-element.73.downs_ref, ...), custom_call_target="tpu_custom_call" | custom-call | tf_op jit(solution)/shard_map/pallas_call | solution.py:319
  69.8 4.2 %collective-permute-start.10 = (f32[16,640]{1,0:T(8,128)S(1)}, f32[16,640]{1,0:T(8,128)S(1)}, u32[]{:S(2)}, u32[]{:S(2)}) collective-permute-start(f32[16,640]{1,0:T(8,128)S(1)} %get-tuple-element.79), channel_id=1, source_target_pairs={{0,504},{8,16},{16,8},{24,32},{32,24},{40,48},{48,40},{56,64},{64,... | collective-permute-start | bytes 122888 | tf_op jit(solution)/shard_map/ppermute | solution.py:335
  74.0 1.9 %collective-permute-start.11 = (f32[16,640]{1,0:T(8,128)S(1)}, f32[16,640]{1,0:T(8,128)S(1)}, u32[]{:S(2)}, u32[]{:S(2)}) collective-permute-start(f32[16,640]{1,0:T(8,128)S(1)} %get-tuple-element.80), channel_id=1, source_target_pairs={{0,8},{8,0},{16,24},{24,16},{32,40},{40,32},{48,56},{56,48},{64,72... | collective-permute-start | bytes 122888 | tf_op jit(solution)/shard_map/ppermute | solution.py:335
  75.9 1.1 shard_map.117.base_ref
  77.0 0.8 collective-permute-done.10.one_ref
  77.8 2.1 %collective-permute-done.11.two_ref = f32[16,640]{1,0:T(8,128)S(1)} collective-permute-done((f32[16,640]{1,0:T(8,128)S(1)}, f32[16,640]{1,0:T(8,128)S(1)}, u32[]{:S(2)}, u32[]{:S(2)}) %collective-permute-start.11) | collective-permute-done | bytes 40992 | tf_op jit(solution)/shard_map/ppermute | solution.py:335
  79.9 2.1 %shard_map.118 = (f32[16,1024]{1,0:T(8,128)S(1)}, f32[16,640]{1,0:T(8,128)S(1)}, f32[16,384]{1,0:T(8,128)S(1)}, f32[16,640]{1,0:T(8,128)}, f32[16,640]{1,0:T(8,128)S(1)}, /*index=5*/f32[8,16,1024]{2,1,0:T(8,128)S(1)}) custom-call(f32[16,1024]{1,0:T(8,128)S(1)} %shard_map.117.base_ref, f32[16,640]{1,0:T(8,128)S(1)} %get-tuple-element.77.ups_ref, ...), custom_call_target="tpu_custom_call" | custom-call | tf_op jit(solution)/shard_map/pallas_call | solution.py:319
  82.1 0.8 copy-done.3
  82.9 4.3 %all-to-all-start = ((f32[8,16,1024]{2,1,0:T(8,128)}), f32[8,16,1024]{2,1,0:T(8,128)S(1)}, u32[]{:S(2)}, u32[]{:S(2)}) async-start(f32[8,16,1024]{2,1,0:T(8,128)} %copy-done.3), calls=%async_computation | async-start | bytes 1048576 | tf_op jit(solution)/shard_map/all_to_all | solution.py:381
  87.2 4.9 %collective-permute-start.12 = (f32[16,640]{1,0:T(8,128)}, f32[16,640]{1,0:T(8,128)S(1)}, u32[]{:S(2)}, u32[]{:S(2)}) collective-permute-start(f32[16,640]{1,0:T(8,128)} %get-tuple-element.86), channel_id=1, source_target_pairs={{0,504},{8,16},{16,8},{24,32},{32,24},{40,48},{48,40},{56,64},{64,... | collective-permute-start | bytes 122888 | tf_op jit(solution)/shard_map/ppermute | solution.py:335
  92.1 1.9 %collective-permute-start.13 = (f32[16,640]{1,0:T(8,128)S(1)}, f32[16,640]{1,0:T(8,128)S(1)}, u32[]{:S(2)}, u32[]{:S(2)}) collective-permute-start(f32[16,640]{1,0:T(8,128)S(1)} %get-tuple-element.87), channel_id=1, source_target_pairs={{0,8},{8,0},{16,24},{24,16},{32,40},{40,32},{48,56},{56,48},{64,72... | collective-permute-start | bytes 122888 | tf_op jit(solution)/shard_map/ppermute | solution.py:335
  94.0 1.1 shard_map.119
  95.1 0.3 collective-permute-done.12.one_ref
  95.4 2.6 %collective-permute-done.13.two_ref = f32[16,640]{1,0:T(8,128)S(1)} collective-permute-done((f32[16,640]{1,0:T(8,128)S(1)}, f32[16,640]{1,0:T(8,128)S(1)}, u32[]{:S(2)}, u32[]{:S(2)}) %collective-permute-start.13) | collective-permute-done | bytes 40992 | tf_op jit(solution)/shard_map/ppermute | solution.py:335
  98.0 1.7 %shard_map.120 = f32[4,32,128]{2,1,0:T(8,128)S(1)} custom-call(f32[16,1024]{1,0:T(8,128)S(1)} %get-tuple-element.83.base_ref, f32[16,640]{1,0:T(8,128)S(1)} %get-tuple-element.84.ups_ref, f32[16,384]{1,0:T(8,128)S(1)} %get-tuple-element.85.downs_ref, f32[16,640]{1,0:T(8,128)S(1)} %collective-permute-done.12.one_ref, ...), custom_call_target="tpu_custom_call" | custom-call | tf_op jit(solution)/shard_map/pallas_call | solution.py:319
  99.7 8.0 %all_to_all.15.parts_ref = f32[4,32,128]{2,1,0:T(8,128)S(1)} all-to-all(f32[4,32,128]{2,1,0:T(8,128)S(1)} %shard_map.120), channel_id=1, replica_groups={{0,8,16,24},{32,40,48,56},{64,72,80,88},{96,104,112,120},{128,136,144,1..., dimensions={0} | all-to-all | bytes 131072 | tf_op jit(solution)/shard_map/all_to_all | solution.py:392
  107.8 31.1 %all_to_all.16.parts_ref = f32[16,32,128]{2,1,0:T(8,128)S(1)} all-to-all(f32[16,32,128]{2,1,0:T(8,128)S(1)} %shard_map.121), channel_id=1, replica_groups={{0,32,64,96,128,160,192,224,256,288,320,352,384,416,448,480},{8,40,72,1..., dimensions={0} | all-to-all | bytes 524288 | tf_op jit(solution)/shard_map/all_to_all | solution.py:394
  138.9 0.6 shard_map.122
  (21 shorter events, 0.3 us)
Async XLA Ops:
  0.6 1.1 copy-start.5
  0.6 1.1 copy-start.1
  0.7 1.1 copy-start
  1.7 0.7 copy-start.4
  1.7 0.7 copy-start.6
  1.7 0.7 copy-start.7
  3.5 12.9 %collective-permute-start = (f32[48,640]{1,0:T(8,128)S(1)}, f32[48,640]{1,0:T(8,128)S(1)}, u32[]{:S(2)}, u32[]{:S(2)}) collective-permute-start(f32[48,640]{1,0:T(8,128)S(1)} %get-tuple-element.48.ups_ref), channel_id=1, source_target_pairs={{0,8},{8,16},{16,24},{24,32},{32,40},{40,48},{48,56},{56,64},{64,7... | collective-permute-start | bytes 368648 | tf_op jit(solution)/shard_map/ppermute | solution.py:330
  7.0 9.4 %collective-permute-start.1 = (f32[24,384]{1,0:T(8,128)S(1)}, f32[24,384]{1,0:T(8,128)S(1)}, u32[]{:S(2)}, u32[]{:S(2)}) collective-permute-start(f32[24,384]{1,0:T(8,128)S(1)} %get-tuple-element.49.downs_ref), channel_id=1, source_target_pairs={{0,504},{8,0},{16,8},{24,16},{32,24},{40,32},{48,40},{56,48},{64,5... | collective-permute-start | bytes 110600 | tf_op jit(solution)/shard_map/ppermute | solution.py:330
  14.0 1.2 copy-start.2
  19.1 8.0 %collective-permute-start.2 = (f32[16,640]{1,0:T(8,128)S(1)}, f32[16,640]{1,0:T(8,128)S(1)}, u32[]{:S(2)}, u32[]{:S(2)}) collective-permute-start(f32[16,640]{1,0:T(8,128)S(1)} %get-tuple-element.59), channel_id=1, source_target_pairs={{0,504},{8,16},{16,8},{24,32},{32,24},{40,48},{48,40},{56,64},{64,... | collective-permute-start | bytes 122888 | tf_op jit(solution)/shard_map/ppermute | solution.py:335
  22.1 5.9 %collective-permute-start.3 = (f32[16,640]{1,0:T(8,128)S(1)}, f32[16,640]{1,0:T(8,128)S(1)}, u32[]{:S(2)}, u32[]{:S(2)}) collective-permute-start(f32[16,640]{1,0:T(8,128)S(1)} %get-tuple-element.60), channel_id=1, source_target_pairs={{0,8},{8,0},{16,24},{24,16},{32,40},{40,32},{48,56},{56,48},{64,72... | collective-permute-start | bytes 122888 | tf_op jit(solution)/shard_map/ppermute | solution.py:335
  29.5 8.0 %collective-permute-start.4 = (f32[16,640]{1,0:T(8,128)S(1)}, f32[16,640]{1,0:T(8,128)S(1)}, u32[]{:S(2)}, u32[]{:S(2)}) collective-permute-start(f32[16,640]{1,0:T(8,128)S(1)} %get-tuple-element.64), channel_id=1, source_target_pairs={{0,504},{8,16},{16,8},{24,32},{32,24},{40,48},{48,40},{56,64},{64,... | collective-permute-start | bytes 122888 | tf_op jit(solution)/shard_map/ppermute | solution.py:335
  34.5 5.9 %collective-permute-start.5 = (f32[16,640]{1,0:T(8,128)S(1)}, f32[16,640]{1,0:T(8,128)S(1)}, u32[]{:S(2)}, u32[]{:S(2)}) collective-permute-start(f32[16,640]{1,0:T(8,128)S(1)} %get-tuple-element.65), channel_id=1, source_target_pairs={{0,8},{8,0},{16,24},{24,16},{32,40},{40,32},{48,56},{56,48},{64,72... | collective-permute-start | bytes 122888 | tf_op jit(solution)/shard_map/ppermute | solution.py:335
  41.9 11.1 %collective-permute-start.6 = (f32[16,640]{1,0:T(8,128)S(1)}, f32[16,640]{1,0:T(8,128)S(1)}, u32[]{:S(2)}, u32[]{:S(2)}) collective-permute-start(f32[16,640]{1,0:T(8,128)S(1)} %get-tuple-element.69), channel_id=1, source_target_pairs={{0,504},{8,16},{16,8},{24,32},{32,24},{40,48},{48,40},{56,64},{64,... | collective-permute-start | bytes 122888 | tf_op jit(solution)/shard_map/ppermute | solution.py:335
  50.0 5.9 %collective-permute-start.7 = (f32[16,640]{1,0:T(8,128)S(1)}, f32[16,640]{1,0:T(8,128)S(1)}, u32[]{:S(2)}, u32[]{:S(2)}) collective-permute-start(f32[16,640]{1,0:T(8,128)S(1)} %get-tuple-element.70), channel_id=1, source_target_pairs={{0,8},{8,0},{16,24},{24,16},{32,40},{40,32},{48,56},{56,48},{64,72... | collective-permute-start | bytes 122888 | tf_op jit(solution)/shard_map/ppermute | solution.py:335
  57.4 8.1 %collective-permute-start.8 = (f32[16,640]{1,0:T(8,128)S(1)}, f32[16,640]{1,0:T(8,128)S(1)}, u32[]{:S(2)}, u32[]{:S(2)}) collective-permute-start(f32[16,640]{1,0:T(8,128)S(1)} %get-tuple-element.74), channel_id=1, source_target_pairs={{0,504},{8,16},{16,8},{24,32},{32,24},{40,48},{48,40},{56,64},{64,... | collective-permute-start | bytes 122888 | tf_op jit(solution)/shard_map/ppermute | solution.py:335
  62.4 5.9 %collective-permute-start.9 = (f32[16,640]{1,0:T(8,128)S(1)}, f32[16,640]{1,0:T(8,128)S(1)}, u32[]{:S(2)}, u32[]{:S(2)}) collective-permute-start(f32[16,640]{1,0:T(8,128)S(1)} %get-tuple-element.75), channel_id=1, source_target_pairs={{0,8},{8,0},{16,24},{24,16},{32,40},{40,32},{48,56},{56,48},{64,72... | collective-permute-start | bytes 122888 | tf_op jit(solution)/shard_map/ppermute | solution.py:335
  69.8 8.0 %collective-permute-start.10 = (f32[16,640]{1,0:T(8,128)S(1)}, f32[16,640]{1,0:T(8,128)S(1)}, u32[]{:S(2)}, u32[]{:S(2)}) collective-permute-start(f32[16,640]{1,0:T(8,128)S(1)} %get-tuple-element.79), channel_id=1, source_target_pairs={{0,504},{8,16},{16,8},{24,32},{32,24},{40,48},{48,40},{56,64},{64,... | collective-permute-start | bytes 122888 | tf_op jit(solution)/shard_map/ppermute | solution.py:335
  74.0 5.9 %collective-permute-start.11 = (f32[16,640]{1,0:T(8,128)S(1)}, f32[16,640]{1,0:T(8,128)S(1)}, u32[]{:S(2)}, u32[]{:S(2)}) collective-permute-start(f32[16,640]{1,0:T(8,128)S(1)} %get-tuple-element.80), channel_id=1, source_target_pairs={{0,8},{8,0},{16,24},{24,16},{32,40},{40,32},{48,56},{56,48},{64,72... | collective-permute-start | bytes 122888 | tf_op jit(solution)/shard_map/ppermute | solution.py:335
  82.1 0.8 copy-start.3
  82.9 15.2 %all-to-all-start = ((f32[8,16,1024]{2,1,0:T(8,128)}), f32[8,16,1024]{2,1,0:T(8,128)S(1)}, u32[]{:S(2)}, u32[]{:S(2)}) async-start(f32[8,16,1024]{2,1,0:T(8,128)} %copy-done.3), calls=%async_computation | async-start | bytes 1048576 | tf_op jit(solution)/shard_map/all_to_all | solution.py:381
  87.2 8.2 %collective-permute-start.12 = (f32[16,640]{1,0:T(8,128)}, f32[16,640]{1,0:T(8,128)S(1)}, u32[]{:S(2)}, u32[]{:S(2)}) collective-permute-start(f32[16,640]{1,0:T(8,128)} %get-tuple-element.86), channel_id=1, source_target_pairs={{0,504},{8,16},{16,8},{24,32},{32,24},{40,48},{48,40},{56,64},{64,... | collective-permute-start | bytes 122888 | tf_op jit(solution)/shard_map/ppermute | solution.py:335
  92.1 5.9 %collective-permute-start.13 = (f32[16,640]{1,0:T(8,128)S(1)}, f32[16,640]{1,0:T(8,128)S(1)}, u32[]{:S(2)}, u32[]{:S(2)}) collective-permute-start(f32[16,640]{1,0:T(8,128)S(1)} %get-tuple-element.87), channel_id=1, source_target_pairs={{0,8},{8,0},{16,24},{24,16},{32,40},{40,32},{48,56},{56,48},{64,72... | collective-permute-start | bytes 122888 | tf_op jit(solution)/shard_map/ppermute | solution.py:335

commit v6 on v5

--- a/solution.py
+++ b/solution.py
@@ -383,14 +383,14 @@
         base, *result = inner("last" if last else "middle", current, current if last else previous)
     (copies,) = call(
         gram_kernel,
-        [((4, 32, LANES), F32)],
+        [((8, 32, LANES), F32)],
         [VM] * 13,
         base, ups, downs, up, down, *shared, current, everyone,
     )
-    near = [[4 * i + j for j in range(4)] for i in range(fe_count // 4)]
-    far = [[4 * i + j for i in range(fe_count // 4)] for j in range(4)]
+    near = [[8 * i + j for j in range(8)] for i in range(fe_count // 8)]
+    far = [[8 * i + j for i in range(fe_count // 8)] for j in range(8)]
     parts = lax.all_to_all(copies, "fe", 0, 0, axis_index_groups=near)
-    (copies,) = call(add_kernel, [((fe_count // 4, 32, LANES), F32)], [VM], parts)
+    (copies,) = call(add_kernel, [((fe_count // 8, 32, LANES), F32)], [VM], parts)
     parts = lax.all_to_all(copies, "fe", 0, 0, axis_index_groups=far)
     projected, correlation = call(
         functools.partial(last_kernel, 1.0 / (NODES * fe_count)),

time: 140 us -> 138 us (0.986)
  the two profiles are of different devices: /device:TPU:32 before, /device:TPU:2 now
where the time goes in v6:
time: 138 us
  starting transfers between devices  59.8 us (43%)
  blocking collectives  31.6 us (23%)
  Pallas kernels  24.5 us (18%)
  waiting for transfers between devices  17.2 us (12%)
  local copies, waits for them, and re-layouts  3.67 us (3%)
    ppermute x12, starting transfers between devices, swapped(): lax.ppermute(block, 'fe', [(i, (i + 1 if i % 2 == first else i - 1) % siz...  39.2 us
    pallas_call x20, Pallas kernels, call(): pl.pallas_call(kernel, out_shape=[jax.ShapeDtypeStruct(s, t) for s, t in...  24.5 us
    all_to_all x1, blocking collectives, on_device(): parts = lax.all_to_all(copies, 'fe', 0, 0, axis_index_groups=far)  22.6 us
    ppermute x12, waiting for transfers between devices, swapped(): lax.ppermute(block, 'fe', [(i, (i + 1 if i % 2 == first else i - 1) % siz...  17.2 us
    ppermute x2, starting transfers between devices, shifted(): lax.ppermute(block, 'fe', [(i, (i + distance) % size) for i in range(size)])  15.8 us
    all_to_all x1, blocking collectives, on_device(): parts = lax.all_to_all(copies, 'fe', 0, 0, axis_index_groups=near)  8.99 us
    all_to_all x1, starting transfers between devices, on_device(): everyone = lax.all_to_all(copied[0], 'band', 0, 0).reshape(-1, NODES)  4.83 us
    unnamed x17, local copies, waits for them, and re-layouts  3.67 us
  transfers between devices with their start and end apart: 15, of which 12 were waited for; matrix products, arithmetic and copies ran while one was open for 0% of the time, Pallas kernels for 7%

profile of v6, /device:TPU:2, one launch (start us, length us, event | category | flops | bytes accessed | tf_op | source)
XLA Modules:
  0.0 137.7 jit_solution(18066335909546294914)
XLA Ops:
  0.7 1.0 copy.11.proj_ref
  2.4 1.1 shard_map.106
  3.5 3.5 %collective-permute-start = (f32[48,640]{1,0:T(8,128)S(1)}, f32[48,640]{1,0:T(8,128)S(1)}, u32[]{:S(2)}, u32[]{:S(2)}) collective-permute-start(f32[48,640]{1,0:T(8,128)S(1)} %get-tuple-element.48.ups_ref), channel_id=1, source_target_pairs={{0,8},{8,16},{16,24},{24,32},{32,40},{40,48},{48,56},{56,64},{64,7... | collective-permute-start | bytes 368648 | tf_op jit(solution)/shard_map/ppermute | solution.py:330
  7.0 12.3 %collective-permute-start.1 = (f32[24,384]{1,0:T(8,128)S(1)}, f32[24,384]{1,0:T(8,128)S(1)}, u32[]{:S(2)}, u32[]{:S(2)}) collective-permute-start(f32[24,384]{1,0:T(8,128)S(1)} %get-tuple-element.49.downs_ref), channel_id=1, source_target_pairs={{0,504},{8,0},{16,8},{24,16},{32,24},{40,32},{48,40},{56,48},{64,5... | collective-permute-start | bytes 110600 | tf_op jit(solution)/shard_map/ppermute | solution.py:330
  19.3 2.5 %shard_map.103 = (s32[8,1024]{1,0:T(8,128)S(1)}, f32[128,1024]{1,0:T(8,128)S(1)}, bf16[2,1024,128]{2,1,0:T(8,128)(2,1)S(1)}) custom-call(s32[4,512]{1,0:T(4,128)S(1)} %copy-done, s32[1,256]{1,0:T(1,128)S(1)} %bitcast.18, f32[4,18,512]{2,1,0:T(8,128)S(1)} %copy.11.proj_ref), custom_call_target="tpu_custom_call" | custom-call | tf_op jit(solution)/shard_map/pallas_call | solution.py:319
  21.8 1.2 copy-done.2
  23.2 1.1 shard_map.105.base_ref
  24.3 1.1 shard_map.107
  25.4 1.5 %shard_map.108 = (f32[16,1024]{1,0:T(8,128)S(1)}, f32[16,640]{1,0:T(8,128)S(1)}, f32[16,384]{1,0:T(8,128)S(1)}, f32[16,640]{1,0:T(8,128)S(1)}, f32[16,640]{1,0:T(8,128)S(1)}) custom-call(f32[16,1024]{1,0:T(8,128)S(1)} %shard_map.105.base_ref, f32[48,640]{1,0:T(8,128)S(1)} %get-tuple-element.48.ups_ref, f32[24,384]{1,0:T(8,128)S(1)} %get-tuple-element.49.downs_ref, ...), custom_call_target="tpu_custom_call" | custom-call | tf_op jit(solution)/shard_map/pallas_call | solution.py:319
  26.9 4.2 %collective-permute-start.2 = (f32[16,640]{1,0:T(8,128)S(1)}, f32[16,640]{1,0:T(8,128)S(1)}, u32[]{:S(2)}, u32[]{:S(2)}) collective-permute-start(f32[16,640]{1,0:T(8,128)S(1)} %get-tuple-element.59), channel_id=1, source_target_pairs={{0,504},{8,16},{16,8},{24,32},{32,24},{40,48},{48,40},{56,64},{64,... | collective-permute-start | bytes 122888 | tf_op jit(solution)/shard_map/ppermute | solution.py:335
  31.2 1.9 %collective-permute-start.3 = (f32[16,640]{1,0:T(8,128)S(1)}, f32[16,640]{1,0:T(8,128)S(1)}, u32[]{:S(2)}, u32[]{:S(2)}) collective-permute-start(f32[16,640]{1,0:T(8,128)S(1)} %get-tuple-element.60), channel_id=1, source_target_pairs={{0,8},{8,0},{16,24},{24,16},{32,40},{40,32},{48,56},{56,48},{64,72... | collective-permute-start | bytes 122888 | tf_op jit(solution)/shard_map/ppermute | solution.py:335
  33.1 1.1 shard_map.109.base_ref
  34.2 2.0 %collective-permute-done.2.one_ref = f32[16,640]{1,0:T(8,128)S(1)} collective-permute-done((f32[16,640]{1,0:T(8,128)S(1)}, f32[16,640]{1,0:T(8,128)S(1)}, u32[]{:S(2)}, u32[]{:S(2)}) %collective-permute-start.2) | collective-permute-done | bytes 40992 | tf_op jit(solution)/shard_map/ppermute | solution.py:335
  36.2 0.9 collective-permute-done.3.two_ref
  37.0 1.5 %shard_map.110 = (f32[16,1024]{1,0:T(8,128)S(1)}, f32[16,640]{1,0:T(8,128)S(1)}, f32[16,384]{1,0:T(8,128)S(1)}, f32[16,640]{1,0:T(8,128)S(1)}, f32[16,640]{1,0:T(8,128)S(1)}) custom-call(f32[16,1024]{1,0:T(8,128)S(1)} %shard_map.109.base_ref, f32[16,640]{1,0:T(8,128)S(1)} %get-tuple-element.57.ups_ref, f32[16,384]{1,0:T(8,128)S(1)} %get-tuple-element.58.downs_ref, ...), custom_call_target="tpu_custom_call" | custom-call | tf_op jit(solution)/shard_map/pallas_call | solution.py:319
  38.6 5.0 %collective-permute-start.4 = (f32[16,640]{1,0:T(8,128)S(1)}, f32[16,640]{1,0:T(8,128)S(1)}, u32[]{:S(2)}, u32[]{:S(2)}) collective-permute-start(f32[16,640]{1,0:T(8,128)S(1)} %get-tuple-element.64), channel_id=1, source_target_pairs={{0,504},{8,16},{16,8},{24,32},{32,24},{40,48},{48,40},{56,64},{64,... | collective-permute-start | bytes 122888 | tf_op jit(solution)/shard_map/ppermute | solution.py:335
  43.5 1.9 %collective-permute-start.5 = (f32[16,640]{1,0:T(8,128)S(1)}, f32[16,640]{1,0:T(8,128)S(1)}, u32[]{:S(2)}, u32[]{:S(2)}) collective-permute-start(f32[16,640]{1,0:T(8,128)S(1)} %get-tuple-element.65), channel_id=1, source_target_pairs={{0,8},{8,0},{16,24},{24,16},{32,40},{40,32},{48,56},{56,48},{64,72... | collective-permute-start | bytes 122888 | tf_op jit(solution)/shard_map/ppermute | solution.py:335
  45.5 1.1 shard_map.111.base_ref
  46.5 1.3 collective-permute-done.4.one_ref
  47.8 1.6 %collective-permute-done.5.two_ref = f32[16,640]{1,0:T(8,128)S(1)} collective-permute-done((f32[16,640]{1,0:T(8,128)S(1)}, f32[16,640]{1,0:T(8,128)S(1)}, u32[]{:S(2)}, u32[]{:S(2)}) %collective-permute-start.5) | collective-permute-done | bytes 40992 | tf_op jit(solution)/shard_map/ppermute | solution.py:335
  49.4 1.5 %shard_map.112 = (f32[16,1024]{1,0:T(8,128)S(1)}, f32[16,640]{1,0:T(8,128)S(1)}, f32[16,384]{1,0:T(8,128)S(1)}, f32[16,640]{1,0:T(8,128)S(1)}, f32[16,640]{1,0:T(8,128)S(1)}) custom-call(f32[16,1024]{1,0:T(8,128)S(1)} %shard_map.111.base_ref, f32[16,640]{1,0:T(8,128)S(1)} %get-tuple-element.62.ups_ref, f32[16,384]{1,0:T(8,128)S(1)} %get-tuple-element.63.downs_ref, ...), custom_call_target="tpu_custom_call" | custom-call | tf_op jit(solution)/shard_map/pallas_call | solution.py:319
  51.0 4.2 %collective-permute-start.6 = (f32[16,640]{1,0:T(8,128)S(1)}, f32[16,640]{1,0:T(8,128)S(1)}, u32[]{:S(2)}, u32[]{:S(2)}) collective-permute-start(f32[16,640]{1,0:T(8,128)S(1)} %get-tuple-element.69), channel_id=1, source_target_pairs={{0,504},{8,16},{16,8},{24,32},{32,24},{40,48},{48,40},{56,64},{64,... | collective-permute-start | bytes 122888 | tf_op jit(solution)/shard_map/ppermute | solution.py:335
  55.2 1.9 %collective-permute-start.7 = (f32[16,640]{1,0:T(8,128)S(1)}, f32[16,640]{1,0:T(8,128)S(1)}, u32[]{:S(2)}, u32[]{:S(2)}) collective-permute-start(f32[16,640]{1,0:T(8,128)S(1)} %get-tuple-element.70), channel_id=1, source_target_pairs={{0,8},{8,0},{16,24},{24,16},{32,40},{40,32},{48,56},{56,48},{64,72... | collective-permute-start | bytes 122888 | tf_op jit(solution)/shard_map/ppermute | solution.py:335
  57.1 1.1 shard_map.113.base_ref
  58.2 2.0 %collective-permute-done.6.one_ref = f32[16,640]{1,0:T(8,128)S(1)} collective-permute-done((f32[16,640]{1,0:T(8,128)S(1)}, f32[16,640]{1,0:T(8,128)S(1)}, u32[]{:S(2)}, u32[]{:S(2)}) %collective-permute-start.6) | collective-permute-done | bytes 40992 | tf_op jit(solution)/shard_map/ppermute | solution.py:335
  60.2 0.9 collective-permute-done.7.two_ref
  61.1 1.5 %shard_map.114 = (f32[16,1024]{1,0:T(8,128)S(1)}, f32[16,640]{1,0:T(8,128)S(1)}, f32[16,384]{1,0:T(8,128)S(1)}, f32[16,640]{1,0:T(8,128)S(1)}, f32[16,640]{1,0:T(8,128)S(1)}) custom-call(f32[16,1024]{1,0:T(8,128)S(1)} %shard_map.113.base_ref, f32[16,640]{1,0:T(8,128)S(1)} %get-tuple-element.67.ups_ref, f32[16,384]{1,0:T(8,128)S(1)} %get-tuple-element.68.downs_ref, ...), custom_call_target="tpu_custom_call" | custom-call | tf_op jit(solution)/shard_map/pallas_call | solution.py:319
  62.6 5.0 %collective-permute-start.8 = (f32[16,640]{1,0:T(8,128)S(1)}, f32[16,640]{1,0:T(8,128)S(1)}, u32[]{:S(2)}, u32[]{:S(2)}) collective-permute-start(f32[16,640]{1,0:T(8,128)S(1)} %get-tuple-element.74), channel_id=1, source_target_pairs={{0,504},{8,16},{16,8},{24,32},{32,24},{40,48},{48,40},{56,64},{64,... | collective-permute-start | bytes 122888 | tf_op jit(solution)/shard_map/ppermute | solution.py:335
  67.6 2.1 %collective-permute-start.9 = (f32[16,640]{1,0:T(8,128)S(1)}, f32[16,640]{1,0:T(8,128)S(1)}, u32[]{:S(2)}, u32[]{:S(2)}) collective-permute-start(f32[16,640]{1,0:T(8,128)S(1)} %get-tuple-element.75), channel_id=1, source_target_pairs={{0,8},{8,0},{16,24},{24,16},{32,40},{40,32},{48,56},{56,48},{64,72... | collective-permute-start | bytes 122888 | tf_op jit(solution)/shard_map/ppermute | solution.py:335
  69.7 1.1 shard_map.115.base_ref
  70.7 1.1 collective-permute-done.8.one_ref
  71.8 1.6 %collective-permute-done.9.two_ref = f32[16,640]{1,0:T(8,128)S(1)} collective-permute-done((f32[16,640]{1,0:T(8,128)S(1)}, f32[16,640]{1,0:T(8,128)S(1)}, u32[]{:S(2)}, u32[]{:S(2)}) %collective-permute-start.9) | collective-permute-done | bytes 40992 | tf_op jit(solution)/shard_map/ppermute | solution.py:335
  73.5 1.5 %shard_map.116 = (f32[16,1024]{1,0:T(8,128)S(1)}, f32[16,640]{1,0:T(8,128)S(1)}, f32[16,384]{1,0:T(8,128)S(1)}, f32[16,640]{1,0:T(8,128)S(1)}, f32[16,640]{1,0:T(8,128)S(1)}) custom-call(f32[16,1024]{1,0:T(8,128)S(1)} %shard_map.115.base_ref, f32[16,640]{1,0:T(8,128)S(1)} %get-tuple-element.72.ups_ref, f32[16,384]{1,0:T(8,128)S(1)} %get-tuple-element.73.downs_ref, ...), custom_call_target="tpu_custom_call" | custom-call | tf_op jit(solution)/shard_map/pallas_call | solution.py:319
  75.0 4.2 %collective-permute-start.10 = (f32[16,640]{1,0:T(8,128)S(1)}, f32[16,640]{1,0:T(8,128)S(1)}, u32[]{:S(2)}, u32[]{:S(2)}) collective-permute-start(f32[16,640]{1,0:T(8,128)S(1)} %get-tuple-element.79), channel_id=1, source_target_pairs={{0,504},{8,16},{16,8},{24,32},{32,24},{40,48},{48,40},{56,64},{64,... | collective-permute-start | bytes 122888 | tf_op jit(solution)/shard_map/ppermute | solution.py:335
  79.2 1.9 %collective-permute-start.11 = (f32[16,640]{1,0:T(8,128)S(1)}, f32[16,640]{1,0:T(8,128)S(1)}, u32[]{:S(2)}, u32[]{:S(2)}) collective-permute-start(f32[16,640]{1,0:T(8,128)S(1)} %get-tuple-element.80), channel_id=1, source_target_pairs={{0,8},{8,0},{16,24},{24,16},{32,40},{40,32},{48,56},{56,48},{64,72... | collective-permute-start | bytes 122888 | tf_op jit(solution)/shard_map/ppermute | solution.py:335
  81.1 1.1 shard_map.117.base_ref
  82.2 2.0 %collective-permute-done.10.one_ref = f32[16,640]{1,0:T(8,128)S(1)} collective-permute-done((f32[16,640]{1,0:T(8,128)S(1)}, f32[16,640]{1,0:T(8,128)S(1)}, u32[]{:S(2)}, u32[]{:S(2)}) %collective-permute-start.10) | collective-permute-done | bytes 40992 | tf_op jit(solution)/shard_map/ppermute | solution.py:335
  84.2 0.9 collective-permute-done.11.two_ref
  85.1 2.1 %shard_map.118 = (f32[16,1024]{1,0:T(8,128)S(1)}, f32[16,640]{1,0:T(8,128)S(1)}, f32[16,384]{1,0:T(8,128)S(1)}, f32[16,640]{1,0:T(8,128)}, f32[16,640]{1,0:T(8,128)S(1)}, /*index=5*/f32[8,16,1024]{2,1,0:T(8,128)S(1)}) custom-call(f32[16,1024]{1,0:T(8,128)S(1)} %shard_map.117.base_ref, f32[16,640]{1,0:T(8,128)S(1)} %get-tuple-element.77.ups_ref, ...), custom_call_target="tpu_custom_call" | custom-call | tf_op jit(solution)/shard_map/pallas_call | solution.py:319
  88.0 4.8 %all-to-all-start = ((f32[8,16,1024]{2,1,0:T(8,128)}), f32[8,16,1024]{2,1,0:T(8,128)S(1)}, u32[]{:S(2)}, u32[]{:S(2)}) async-start(f32[8,16,1024]{2,1,0:T(8,128)} %copy-done.3), calls=%async_computation | async-start | bytes 1048576 | tf_op jit(solution)/shard_map/all_to_all | solution.py:381
  92.9 4.9 %collective-permute-start.12 = (f32[16,640]{1,0:T(8,128)}, f32[16,640]{1,0:T(8,128)S(1)}, u32[]{:S(2)}, u32[]{:S(2)}) collective-permute-start(f32[16,640]{1,0:T(8,128)} %get-tuple-element.86), channel_id=1, source_target_pairs={{0,504},{8,16},{16,8},{24,32},{32,24},{40,48},{48,40},{56,64},{64,... | collective-permute-start | bytes 122888 | tf_op jit(solution)/shard_map/ppermute | solution.py:335
  97.8 1.9 %collective-permute-start.13 = (f32[16,640]{1,0:T(8,128)S(1)}, f32[16,640]{1,0:T(8,128)S(1)}, u32[]{:S(2)}, u32[]{:S(2)}) collective-permute-start(f32[16,640]{1,0:T(8,128)S(1)} %get-tuple-element.87), channel_id=1, source_target_pairs={{0,8},{8,0},{16,24},{24,16},{32,40},{40,32},{48,56},{56,48},{64,72... | collective-permute-start | bytes 122888 | tf_op jit(solution)/shard_map/ppermute | solution.py:335
  99.7 1.1 shard_map.119
  100.8 1.5 %collective-permute-done.12.one_ref = f32[16,640]{1,0:T(8,128)S(1)} collective-permute-done((f32[16,640]{1,0:T(8,128)}, f32[16,640]{1,0:T(8,128)S(1)}, u32[]{:S(2)}, u32[]{:S(2)}) %collective-permute-start.12) | collective-permute-done | bytes 40992 | tf_op jit(solution)/shard_map/ppermute | solution.py:335
  102.3 1.4 %collective-permute-done.13.two_ref = f32[16,640]{1,0:T(8,128)S(1)} collective-permute-done((f32[16,640]{1,0:T(8,128)S(1)}, f32[16,640]{1,0:T(8,128)S(1)}, u32[]{:S(2)}, u32[]{:S(2)}) %collective-permute-start.13) | collective-permute-done | bytes 40992 | tf_op jit(solution)/shard_map/ppermute | solution.py:335
  103.7 1.7 %shard_map.120 = f32[8,32,128]{2,1,0:T(8,128)S(1)} custom-call(f32[16,1024]{1,0:T(8,128)S(1)} %get-tuple-element.83.base_ref, f32[16,640]{1,0:T(8,128)S(1)} %get-tuple-element.84.ups_ref, f32[16,384]{1,0:T(8,128)S(1)} %get-tuple-element.85.downs_ref, f32[16,640]{1,0:T(8,128)S(1)} %collective-permute-done.12.one_ref, ...), custom_call_target="tpu_custom_call" | custom-call | tf_op jit(solution)/shard_map/pallas_call | solution.py:319
  105.4 9.0 %all_to_all.15.parts_ref = f32[8,32,128]{2,1,0:T(8,128)S(1)} all-to-all(f32[8,32,128]{2,1,0:T(8,128)S(1)} %shard_map.120), channel_id=1, replica_groups={{0,8,16,24,32,40,48,56},{64,72,80,88,96,104,112,120},{128,136,144,152,1..., dimensions={0} | all-to-all | bytes 262144 | tf_op jit(solution)/shard_map/all_to_all | solution.py:392
  114.4 22.6 %all_to_all.16.parts_ref = f32[8,32,128]{2,1,0:T(8,128)S(1)} all-to-all(f32[8,32,128]{2,1,0:T(8,128)S(1)} %shard_map.121), channel_id=1, replica_groups={{0,64,128,192,256,320,384,448},{8,72,136,200,264,328,392,456},{16,80,14..., dimensions={0} | all-to-all | bytes 262144 | tf_op jit(solution)/shard_map/all_to_all | solution.py:394
  (21 shorter events, 2.2 us)
Async XLA Ops:
  0.6 1.1 copy-start.5
  0.6 1.1 copy-start.1
  0.7 1.1 copy-start
  1.7 0.7 copy-start.4
  1.7 0.7 copy-start.6
  1.7 0.7 copy-start.7
  3.5 20.7 %collective-permute-start = (f32[48,640]{1,0:T(8,128)S(1)}, f32[48,640]{1,0:T(8,128)S(1)}, u32[]{:S(2)}, u32[]{:S(2)}) collective-permute-start(f32[48,640]{1,0:T(8,128)S(1)} %get-tuple-element.48.ups_ref), channel_id=1, source_target_pairs={{0,8},{8,16},{16,24},{24,32},{32,40},{40,48},{48,56},{56,64},{64,7... | collective-permute-start | bytes 368648 | tf_op jit(solution)/shard_map/ppermute | solution.py:330
  7.0 17.2 %collective-permute-start.1 = (f32[24,384]{1,0:T(8,128)S(1)}, f32[24,384]{1,0:T(8,128)S(1)}, u32[]{:S(2)}, u32[]{:S(2)}) collective-permute-start(f32[24,384]{1,0:T(8,128)S(1)} %get-tuple-element.49.downs_ref), channel_id=1, source_target_pairs={{0,504},{8,0},{16,8},{24,16},{32,24},{40,32},{48,40},{56,48},{64,5... | collective-permute-start | bytes 110600 | tf_op jit(solution)/shard_map/ppermute | solution.py:330
  21.8 1.2 copy-start.2
  26.9 9.2 %collective-permute-start.2 = (f32[16,640]{1,0:T(8,128)S(1)}, f32[16,640]{1,0:T(8,128)S(1)}, u32[]{:S(2)}, u32[]{:S(2)}) collective-permute-start(f32[16,640]{1,0:T(8,128)S(1)} %get-tuple-element.59), channel_id=1, source_target_pairs={{0,504},{8,16},{16,8},{24,32},{32,24},{40,48},{48,40},{56,64},{64,... | collective-permute-start | bytes 122888 | tf_op jit(solution)/shard_map/ppermute | solution.py:335
  31.2 5.9 %collective-permute-start.3 = (f32[16,640]{1,0:T(8,128)S(1)}, f32[16,640]{1,0:T(8,128)S(1)}, u32[]{:S(2)}, u32[]{:S(2)}) collective-permute-start(f32[16,640]{1,0:T(8,128)S(1)} %get-tuple-element.60), channel_id=1, source_target_pairs={{0,8},{8,0},{16,24},{24,16},{32,40},{40,32},{48,56},{56,48},{64,72... | collective-permute-start | bytes 122888 | tf_op jit(solution)/shard_map/ppermute | solution.py:335
  38.6 9.2 %collective-permute-start.4 = (f32[16,640]{1,0:T(8,128)S(1)}, f32[16,640]{1,0:T(8,128)S(1)}, u32[]{:S(2)}, u32[]{:S(2)}) collective-permute-start(f32[16,640]{1,0:T(8,128)S(1)} %get-tuple-element.64), channel_id=1, source_target_pairs={{0,504},{8,16},{16,8},{24,32},{32,24},{40,48},{48,40},{56,64},{64,... | collective-permute-start | bytes 122888 | tf_op jit(solution)/shard_map/ppermute | solution.py:335
  43.5 5.9 %collective-permute-start.5 = (f32[16,640]{1,0:T(8,128)S(1)}, f32[16,640]{1,0:T(8,128)S(1)}, u32[]{:S(2)}, u32[]{:S(2)}) collective-permute-start(f32[16,640]{1,0:T(8,128)S(1)} %get-tuple-element.65), channel_id=1, source_target_pairs={{0,8},{8,0},{16,24},{24,16},{32,40},{40,32},{48,56},{56,48},{64,72... | collective-permute-start | bytes 122888 | tf_op jit(solution)/shard_map/ppermute | solution.py:335
  51.0 9.2 %collective-permute-start.6 = (f32[16,640]{1,0:T(8,128)S(1)}, f32[16,640]{1,0:T(8,128)S(1)}, u32[]{:S(2)}, u32[]{:S(2)}) collective-permute-start(f32[16,640]{1,0:T(8,128)S(1)} %get-tuple-element.69), channel_id=1, source_target_pairs={{0,504},{8,16},{16,8},{24,32},{32,24},{40,48},{48,40},{56,64},{64,... | collective-permute-start | bytes 122888 | tf_op jit(solution)/shard_map/ppermute | solution.py:335
  55.2 5.9 %collective-permute-start.7 = (f32[16,640]{1,0:T(8,128)S(1)}, f32[16,640]{1,0:T(8,128)S(1)}, u32[]{:S(2)}, u32[]{:S(2)}) collective-permute-start(f32[16,640]{1,0:T(8,128)S(1)} %get-tuple-element.70), channel_id=1, source_target_pairs={{0,8},{8,0},{16,24},{24,16},{32,40},{40,32},{48,56},{56,48},{64,72... | collective-permute-start | bytes 122888 | tf_op jit(solution)/shard_map/ppermute | solution.py:335
  62.6 9.2 %collective-permute-start.8 = (f32[16,640]{1,0:T(8,128)S(1)}, f32[16,640]{1,0:T(8,128)S(1)}, u32[]{:S(2)}, u32[]{:S(2)}) collective-permute-start(f32[16,640]{1,0:T(8,128)S(1)} %get-tuple-element.74), channel_id=1, source_target_pairs={{0,504},{8,16},{16,8},{24,32},{32,24},{40,48},{48,40},{56,64},{64,... | collective-permute-start | bytes 122888 | tf_op jit(solution)/shard_map/ppermute | solution.py:335
  67.6 5.9 %collective-permute-start.9 = (f32[16,640]{1,0:T(8,128)S(1)}, f32[16,640]{1,0:T(8,128)S(1)}, u32[]{:S(2)}, u32[]{:S(2)}) collective-permute-start(f32[16,640]{1,0:T(8,128)S(1)} %get-tuple-element.75), channel_id=1, source_target_pairs={{0,8},{8,0},{16,24},{24,16},{32,40},{40,32},{48,56},{56,48},{64,72... | collective-permute-start | bytes 122888 | tf_op jit(solution)/shard_map/ppermute | solution.py:335
  75.0 9.2 %collective-permute-start.10 = (f32[16,640]{1,0:T(8,128)S(1)}, f32[16,640]{1,0:T(8,128)S(1)}, u32[]{:S(2)}, u32[]{:S(2)}) collective-permute-start(f32[16,640]{1,0:T(8,128)S(1)} %get-tuple-element.79), channel_id=1, source_target_pairs={{0,504},{8,16},{16,8},{24,32},{32,24},{40,48},{48,40},{56,64},{64,... | collective-permute-start | bytes 122888 | tf_op jit(solution)/shard_map/ppermute | solution.py:335
  79.2 5.9 %collective-permute-start.11 = (f32[16,640]{1,0:T(8,128)S(1)}, f32[16,640]{1,0:T(8,128)S(1)}, u32[]{:S(2)}, u32[]{:S(2)}) collective-permute-start(f32[16,640]{1,0:T(8,128)S(1)} %get-tuple-element.80), channel_id=1, source_target_pairs={{0,8},{8,0},{16,24},{24,16},{32,40},{40,32},{48,56},{56,48},{64,72... | collective-permute-start | bytes 122888 | tf_op jit(solution)/shard_map/ppermute | solution.py:335
  87.2 0.8 copy-start.3
  88.0 15.7 %all-to-all-start = ((f32[8,16,1024]{2,1,0:T(8,128)}), f32[8,16,1024]{2,1,0:T(8,128)S(1)}, u32[]{:S(2)}, u32[]{:S(2)}) async-start(f32[8,16,1024]{2,1,0:T(8,128)} %copy-done.3), calls=%async_computation | async-start | bytes 1048576 | tf_op jit(solution)/shard_map/all_to_all | solution.py:381
  92.9 9.4 %collective-permute-start.12 = (f32[16,640]{1,0:T(8,128)}, f32[16,640]{1,0:T(8,128)S(1)}, u32[]{:S(2)}, u32[]{:S(2)}) collective-permute-start(f32[16,640]{1,0:T(8,128)} %get-tuple-element.86), channel_id=1, source_target_pairs={{0,504},{8,16},{16,8},{24,32},{32,24},{40,48},{48,40},{56,64},{64,... | collective-permute-start | bytes 122888 | tf_op jit(solution)/shard_map/ppermute | solution.py:335
  97.8 5.9 %collective-permute-start.13 = (f32[16,640]{1,0:T(8,128)S(1)}, f32[16,640]{1,0:T(8,128)S(1)}, u32[]{:S(2)}, u32[]{:S(2)}) collective-permute-start(f32[16,640]{1,0:T(8,128)S(1)} %get-tuple-element.87), channel_id=1, source_target_pairs={{0,8},{8,0},{16,24},{24,16},{32,40},{40,32},{48,56},{56,48},{64,72... | collective-permute-start | bytes 122888 | tf_op jit(solution)/shard_map/ppermute | solution.py:335

commit v7 on v6

--- a/solution.py
+++ b/solution.py
@@ -44,8 +44,9 @@
 
 def product(x_high, x_low, w_high, w_low):
     rows = x_high.shape[0]
+    less = dot(x_high, w_low)
     both = dot(jnp.concatenate([x_high, x_low], axis=0), w_high)
-    return both[:rows] + both[rows:] + dot(x_high, w_low)
+    return both[:rows] + (both[rows:] + less)
 
 
 def blocks_of(x):
@@ -250,6 +251,7 @@
     edge = ups_ref[0:BANDS, 0:NPC] + pick_row(blocks_of(from_upper), conn_ref[3:4, :] - NODES)
     low = from_lower + pick_row(blocks_of(downs_ref[0:BANDS, 0:GHOST]), index_ref[3:4, 0:NPC])
     x_high, x_low = split2(jnp.concatenate([edge, low], axis=0))
+    y = product(x_high, x_low, e_ref[0], e_ref[1])
     wide = product(x_high, x_low, pe_ref[0], pe_ref[1])
     which = lane_iota(BANDS, LANES) >> 5
     edges = jnp.where(which == 0, wide[:BANDS], jnp.where(which == 1, wide[BANDS:], 0.0))
@@ -257,7 +259,6 @@
     sums = dot(jnp.concatenate(split3(partials), axis=0), k_ref[...])
     w_high, w_low = split2(sums[0:16] + sums[16:32] + sums[32:48])
     nonlocal_part = product(w_high, w_low, p_ref[0], p_ref[1])
-    y = product(x_high, x_low, e_ref[0], e_ref[1])
     own, other = blocks_of(y[:BANDS]), blocks_of(y[BANDS:])
     out = []
     for k in range(NODES // LANES):
@@ -286,11 +287,17 @@
 
 def gram_kernel(base_ref, ups_ref, downs_ref, one_ref, two_ref, conn_ref, index_ref, e_ref, p_ref, pe_ref, k_ref,
                 v_ref, all_ref, out_ref):
+    a_high, a_low = split2(all_ref[...])
+
+    def against_all(x):
+        x_high, x_low = split2(x)
+        less = dot_nt(x_high, a_low)
+        both = dot_nt(jnp.concatenate([x_high, x_low], axis=0), a_high)
+        return both[:BANDS] + (both[BANDS:] + less)
+
+    correlation = against_all(v_ref[...])
     h = base_ref[...] + outer(True, ups_ref, downs_ref, one_ref, two_ref, conn_ref, index_ref, e_ref, p_ref, pe_ref, k_ref)
-    s_high, s_low = split2(jnp.concatenate([h, v_ref[...]], axis=0))
-    a_high, a_low = split2(all_ref[...])
-    both = dot_nt(jnp.concatenate([s_high, s_low], axis=0), a_high)
-    panel = both[:32] + both[32:] + dot_nt(s_high, a_low)
+    panel = jnp.concatenate([against_all(h), correlation], axis=0)
     for i in range(out_ref.shape[0]):
         out_ref[i] = panel
 

time: 138 us -> 135 us (0.978)
  Pallas kernels: 24.5 us -> 21.4 us
    pallas_call x20, Pallas kernels: 24.5 us -> 21.4 us  [call(): pl.pallas_call(kernel, out_shape=[jax.ShapeDtypeStruct(s, t) for s, t in...]
  transfers between devices with their start and end apart: 15 -> 15, of which waited for: 12 -> 12; matrix products, arithmetic and copies ran while one was open for 0% -> 0% of each run, Pallas kernels for 7% -> 8%
where the time goes in v7:
time: 135 us; the launch traced here: 134 us
  starting transfers between devices  59.8 us (44%)
  blocking collectives  31.6 us (23%)
  Pallas kernels  21.4 us (16%)
  waiting for transfers between devices  17.1 us (13%)
  local copies, waits for them, and re-layouts  3.67 us (3%)
    ppermute x12, starting transfers between devices, swapped(): lax.ppermute(block, 'fe', [(i, (i + 1 if i % 2 == first else i - 1) % siz...  39.2 us
    all_to_all x1, blocking collectives, on_device(): parts = lax.all_to_all(copies, 'fe', 0, 0, axis_index_groups=far)  22.6 us
    pallas_call x20, Pallas kernels, call(): pl.pallas_call(kernel, out_shape=[jax.ShapeDtypeStruct(s, t) for s, t in...  21.4 us
    ppermute x12, waiting for transfers between devices, swapped(): lax.ppermute(block, 'fe', [(i, (i + 1 if i % 2 == first else i - 1) % siz...  17.1 us
    ppermute x2, starting transfers between devices, shifted(): lax.ppermute(block, 'fe', [(i, (i + distance) % size) for i in range(size)])  15.8 us
    all_to_all x1, blocking collectives, on_device(): parts = lax.all_to_all(copies, 'fe', 0, 0, axis_index_groups=near)  9 us
    all_to_all x1, starting transfers between devices, on_device(): everyone = lax.all_to_all(copied[0], 'band', 0, 0).reshape(-1, NODES)  4.84 us
    unnamed x17, local copies, waits for them, and re-layouts  3.67 us
  transfers between devices with their start and end apart: 15, of which 12 were waited for; matrix products, arithmetic and copies ran while one was open for 0% of the time, Pallas kernels for 8%

profile of v7, /device:TPU:2, one launch (start us, length us, event | category | flops | bytes accessed | tf_op | source)
XLA Modules:
  0.0 134.4 jit_solution(10057974236155913852)
XLA Ops:
  0.7 1.0 copy.11.proj_ref
  2.4 1.1 shard_map.106
  3.5 3.5 %collective-permute-start = (f32[48,640]{1,0:T(8,128)S(1)}, f32[48,640]{1,0:T(8,128)S(1)}, u32[]{:S(2)}, u32[]{:S(2)}) collective-permute-start(f32[48,640]{1,0:T(8,128)S(1)} %get-tuple-element.48.ups_ref), channel_id=1, source_target_pairs={{0,8},{8,16},{16,24},{24,32},{32,40},{40,48},{48,56},{56,64},{64,7... | collective-permute-start | bytes 368648 | tf_op jit(solution)/shard_map/ppermute | solution.py:337
  7.0 12.3 %collective-permute-start.1 = (f32[24,384]{1,0:T(8,128)S(1)}, f32[24,384]{1,0:T(8,128)S(1)}, u32[]{:S(2)}, u32[]{:S(2)}) collective-permute-start(f32[24,384]{1,0:T(8,128)S(1)} %get-tuple-element.49.downs_ref), channel_id=1, source_target_pairs={{0,504},{8,0},{16,8},{24,16},{32,24},{40,32},{48,40},{56,48},{64,5... | collective-permute-start | bytes 110600 | tf_op jit(solution)/shard_map/ppermute | solution.py:337
  19.3 2.5 %shard_map.103 = (s32[8,1024]{1,0:T(8,128)S(1)}, f32[128,1024]{1,0:T(8,128)S(1)}, bf16[2,1024,128]{2,1,0:T(8,128)(2,1)S(1)}) custom-call(s32[4,512]{1,0:T(4,128)S(1)} %copy-done, s32[1,256]{1,0:T(1,128)S(1)} %bitcast.18, f32[4,18,512]{2,1,0:T(8,128)S(1)} %copy.11.proj_ref), custom_call_target="tpu_custom_call" | custom-call | tf_op jit(solution)/shard_map/pallas_call | solution.py:326
  21.8 1.2 copy-done.2
  23.2 1.1 shard_map.105.base_ref
  24.3 1.1 shard_map.107
  25.4 1.0 shard_map.108
  26.5 4.2 %collective-permute-start.2 = (f32[16,640]{1,0:T(8,128)S(1)}, f32[16,640]{1,0:T(8,128)S(1)}, u32[]{:S(2)}, u32[]{:S(2)}) collective-permute-start(f32[16,640]{1,0:T(8,128)S(1)} %get-tuple-element.59), channel_id=1, source_target_pairs={{0,504},{8,16},{16,8},{24,32},{32,24},{40,48},{48,40},{56,64},{64,... | collective-permute-start | bytes 122888 | tf_op jit(solution)/shard_map/ppermute | solution.py:342
  30.7 1.9 %collective-permute-start.3 = (f32[16,640]{1,0:T(8,128)S(1)}, f32[16,640]{1,0:T(8,128)S(1)}, u32[]{:S(2)}, u32[]{:S(2)}) collective-permute-start(f32[16,640]{1,0:T(8,128)S(1)} %get-tuple-element.60), channel_id=1, source_target_pairs={{0,8},{8,0},{16,24},{24,16},{32,40},{40,32},{48,56},{56,48},{64,72... | collective-permute-start | bytes 122888 | tf_op jit(solution)/shard_map/ppermute | solution.py:342
  32.6 1.1 shard_map.109.base_ref
  33.7 2.0 %collective-permute-done.2.one_ref = f32[16,640]{1,0:T(8,128)S(1)} collective-permute-done((f32[16,640]{1,0:T(8,128)S(1)}, f32[16,640]{1,0:T(8,128)S(1)}, u32[]{:S(2)}, u32[]{:S(2)}) %collective-permute-start.2) | collective-permute-done | bytes 40992 | tf_op jit(solution)/shard_map/ppermute | solution.py:342
  35.7 0.9 collective-permute-done.3.two_ref
  36.6 1.0 shard_map.110
  37.6 5.0 %collective-permute-start.4 = (f32[16,640]{1,0:T(8,128)S(1)}, f32[16,640]{1,0:T(8,128)S(1)}, u32[]{:S(2)}, u32[]{:S(2)}) collective-permute-start(f32[16,640]{1,0:T(8,128)S(1)} %get-tuple-element.64), channel_id=1, source_target_pairs={{0,504},{8,16},{16,8},{24,32},{32,24},{40,48},{48,40},{56,64},{64,... | collective-permute-start | bytes 122888 | tf_op jit(solution)/shard_map/ppermute | solution.py:342
  42.6 1.9 %collective-permute-start.5 = (f32[16,640]{1,0:T(8,128)S(1)}, f32[16,640]{1,0:T(8,128)S(1)}, u32[]{:S(2)}, u32[]{:S(2)}) collective-permute-start(f32[16,640]{1,0:T(8,128)S(1)} %get-tuple-element.65), channel_id=1, source_target_pairs={{0,8},{8,0},{16,24},{24,16},{32,40},{40,32},{48,56},{56,48},{64,72... | collective-permute-start | bytes 122888 | tf_op jit(solution)/shard_map/ppermute | solution.py:342
  44.5 1.1 shard_map.111.base_ref
  45.6 1.2 collective-permute-done.4.one_ref
  46.8 1.7 %collective-permute-done.5.two_ref = f32[16,640]{1,0:T(8,128)S(1)} collective-permute-done((f32[16,640]{1,0:T(8,128)S(1)}, f32[16,640]{1,0:T(8,128)S(1)}, u32[]{:S(2)}, u32[]{:S(2)}) %collective-permute-start.5) | collective-permute-done | bytes 40992 | tf_op jit(solution)/shard_map/ppermute | solution.py:342
  48.5 1.0 shard_map.112
  49.5 4.2 %collective-permute-start.6 = (f32[16,640]{1,0:T(8,128)S(1)}, f32[16,640]{1,0:T(8,128)S(1)}, u32[]{:S(2)}, u32[]{:S(2)}) collective-permute-start(f32[16,640]{1,0:T(8,128)S(1)} %get-tuple-element.69), channel_id=1, source_target_pairs={{0,504},{8,16},{16,8},{24,32},{32,24},{40,48},{48,40},{56,64},{64,... | collective-permute-start | bytes 122888 | tf_op jit(solution)/shard_map/ppermute | solution.py:342
  53.7 1.9 %collective-permute-start.7 = (f32[16,640]{1,0:T(8,128)S(1)}, f32[16,640]{1,0:T(8,128)S(1)}, u32[]{:S(2)}, u32[]{:S(2)}) collective-permute-start(f32[16,640]{1,0:T(8,128)S(1)} %get-tuple-element.70), channel_id=1, source_target_pairs={{0,8},{8,0},{16,24},{24,16},{32,40},{40,32},{48,56},{56,48},{64,72... | collective-permute-start | bytes 122888 | tf_op jit(solution)/shard_map/ppermute | solution.py:342
  55.6 1.1 shard_map.113.base_ref
  56.7 2.0 %collective-permute-done.6.one_ref = f32[16,640]{1,0:T(8,128)S(1)} collective-permute-done((f32[16,640]{1,0:T(8,128)S(1)}, f32[16,640]{1,0:T(8,128)S(1)}, u32[]{:S(2)}, u32[]{:S(2)}) %collective-permute-start.6) | collective-permute-done | bytes 40992 | tf_op jit(solution)/shard_map/ppermute | solution.py:342
  58.7 0.9 collective-permute-done.7.two_ref
  59.6 1.0 shard_map.114
  60.7 5.0 %collective-permute-start.8 = (f32[16,640]{1,0:T(8,128)S(1)}, f32[16,640]{1,0:T(8,128)S(1)}, u32[]{:S(2)}, u32[]{:S(2)}) collective-permute-start(f32[16,640]{1,0:T(8,128)S(1)} %get-tuple-element.74), channel_id=1, source_target_pairs={{0,504},{8,16},{16,8},{24,32},{32,24},{40,48},{48,40},{56,64},{64,... | collective-permute-start | bytes 122888 | tf_op jit(solution)/shard_map/ppermute | solution.py:342
  65.6 1.9 %collective-permute-start.9 = (f32[16,640]{1,0:T(8,128)S(1)}, f32[16,640]{1,0:T(8,128)S(1)}, u32[]{:S(2)}, u32[]{:S(2)}) collective-permute-start(f32[16,640]{1,0:T(8,128)S(1)} %get-tuple-element.75), channel_id=1, source_target_pairs={{0,8},{8,0},{16,24},{24,16},{32,40},{40,32},{48,56},{56,48},{64,72... | collective-permute-start | bytes 122888 | tf_op jit(solution)/shard_map/ppermute | solution.py:342
  67.6 1.1 shard_map.115.base_ref
  68.7 1.2 collective-permute-done.8.one_ref
  69.9 1.7 %collective-permute-done.9.two_ref = f32[16,640]{1,0:T(8,128)S(1)} collective-permute-done((f32[16,640]{1,0:T(8,128)S(1)}, f32[16,640]{1,0:T(8,128)S(1)}, u32[]{:S(2)}, u32[]{:S(2)}) %collective-permute-start.9) | collective-permute-done | bytes 40992 | tf_op jit(solution)/shard_map/ppermute | solution.py:342
  71.5 1.0 shard_map.116
  72.6 4.2 %collective-permute-start.10 = (f32[16,640]{1,0:T(8,128)S(1)}, f32[16,640]{1,0:T(8,128)S(1)}, u32[]{:S(2)}, u32[]{:S(2)}) collective-permute-start(f32[16,640]{1,0:T(8,128)S(1)} %get-tuple-element.79), channel_id=1, source_target_pairs={{0,504},{8,16},{16,8},{24,32},{32,24},{40,48},{48,40},{56,64},{64,... | collective-permute-start | bytes 122888 | tf_op jit(solution)/shard_map/ppermute | solution.py:342
  76.8 2.1 %collective-permute-start.11 = (f32[16,640]{1,0:T(8,128)S(1)}, f32[16,640]{1,0:T(8,128)S(1)}, u32[]{:S(2)}, u32[]{:S(2)}) collective-permute-start(f32[16,640]{1,0:T(8,128)S(1)} %get-tuple-element.80), channel_id=1, source_target_pairs={{0,8},{8,0},{16,24},{24,16},{32,40},{40,32},{48,56},{56,48},{64,72... | collective-permute-start | bytes 122888 | tf_op jit(solution)/shard_map/ppermute | solution.py:342
  78.9 1.1 shard_map.117.base_ref
  80.0 1.8 %collective-permute-done.10.one_ref = f32[16,640]{1,0:T(8,128)S(1)} collective-permute-done((f32[16,640]{1,0:T(8,128)S(1)}, f32[16,640]{1,0:T(8,128)S(1)}, u32[]{:S(2)}, u32[]{:S(2)}) %collective-permute-start.10) | collective-permute-done | bytes 40992 | tf_op jit(solution)/shard_map/ppermute | solution.py:342
  81.8 0.9 collective-permute-done.11.two_ref
  82.7 1.7 %shard_map.118 = (f32[16,1024]{1,0:T(8,128)S(1)}, f32[16,640]{1,0:T(8,128)S(1)}, f32[16,384]{1,0:T(8,128)S(1)}, f32[16,640]{1,0:T(8,128)}, f32[16,640]{1,0:T(8,128)S(1)}, /*index=5*/f32[8,16,1024]{2,1,0:T(8,128)S(1)}) custom-call(f32[16,1024]{1,0:T(8,128)S(1)} %shard_map.117.base_ref, f32[16,640]{1,0:T(8,128)S(1)} %get-tuple-element.77.ups_ref, ...), custom_call_target="tpu_custom_call" | custom-call | tf_op jit(solution)/shard_map/pallas_call | solution.py:326
  85.1 4.8 %all-to-all-start = ((f32[8,16,1024]{2,1,0:T(8,128)}), f32[8,16,1024]{2,1,0:T(8,128)S(1)}, u32[]{:S(2)}, u32[]{:S(2)}) async-start(f32[8,16,1024]{2,1,0:T(8,128)} %copy-done.3), calls=%async_computation | async-start | bytes 1048576 | tf_op jit(solution)/shard_map/all_to_all | solution.py:388
  90.0 5.0 %collective-permute-start.12 = (f32[16,640]{1,0:T(8,128)}, f32[16,640]{1,0:T(8,128)S(1)}, u32[]{:S(2)}, u32[]{:S(2)}) collective-permute-start(f32[16,640]{1,0:T(8,128)} %get-tuple-element.86), channel_id=1, source_target_pairs={{0,504},{8,16},{16,8},{24,32},{32,24},{40,48},{48,40},{56,64},{64,... | collective-permute-start | bytes 122888 | tf_op jit(solution)/shard_map/ppermute | solution.py:342
  95.0 1.9 %collective-permute-start.13 = (f32[16,640]{1,0:T(8,128)S(1)}, f32[16,640]{1,0:T(8,128)S(1)}, u32[]{:S(2)}, u32[]{:S(2)}) collective-permute-start(f32[16,640]{1,0:T(8,128)S(1)} %get-tuple-element.87), channel_id=1, source_target_pairs={{0,8},{8,0},{16,24},{24,16},{32,40},{40,32},{48,56},{56,48},{64,72... | collective-permute-start | bytes 122888 | tf_op jit(solution)/shard_map/ppermute | solution.py:342
  96.9 1.1 shard_map.119
  98.0 1.4 %collective-permute-done.12.one_ref = f32[16,640]{1,0:T(8,128)S(1)} collective-permute-done((f32[16,640]{1,0:T(8,128)}, f32[16,640]{1,0:T(8,128)S(1)}, u32[]{:S(2)}, u32[]{:S(2)}) %collective-permute-start.12) | collective-permute-done | bytes 40992 | tf_op jit(solution)/shard_map/ppermute | solution.py:342
  99.4 1.5 %collective-permute-done.13.two_ref = f32[16,640]{1,0:T(8,128)S(1)} collective-permute-done((f32[16,640]{1,0:T(8,128)S(1)}, f32[16,640]{1,0:T(8,128)S(1)}, u32[]{:S(2)}, u32[]{:S(2)}) %collective-permute-start.13) | collective-permute-done | bytes 40992 | tf_op jit(solution)/shard_map/ppermute | solution.py:342
  100.9 1.3 shard_map.120
  102.2 9.0 %all_to_all.15.parts_ref = f32[8,32,128]{2,1,0:T(8,128)S(1)} all-to-all(f32[8,32,128]{2,1,0:T(8,128)S(1)} %shard_map.120), channel_id=1, replica_groups={{0,8,16,24,32,40,48,56},{64,72,80,88,96,104,112,120},{128,136,144,152,1..., dimensions={0} | all-to-all | bytes 262144 | tf_op jit(solution)/shard_map/all_to_all | solution.py:399
  111.2 22.6 %all_to_all.16.parts_ref = f32[8,32,128]{2,1,0:T(8,128)S(1)} all-to-all(f32[8,32,128]{2,1,0:T(8,128)S(1)} %shard_map.121), channel_id=1, replica_groups={{0,64,128,192,256,320,384,448},{8,72,136,200,264,328,392,456},{16,80,14..., dimensions={0} | all-to-all | bytes 262144 | tf_op jit(solution)/shard_map/all_to_all | solution.py:401
  (21 shorter events, 2.2 us)
Async XLA Ops:
  0.6 1.1 copy-start.5
  0.6 1.1 copy-start.1
  0.7 1.1 copy-start
  1.7 0.7 copy-start.4
  1.7 0.7 copy-start.6
  1.7 0.7 copy-start.7
  3.5 20.8 %collective-permute-start = (f32[48,640]{1,0:T(8,128)S(1)}, f32[48,640]{1,0:T(8,128)S(1)}, u32[]{:S(2)}, u32[]{:S(2)}) collective-permute-start(f32[48,640]{1,0:T(8,128)S(1)} %get-tuple-element.48.ups_ref), channel_id=1, source_target_pairs={{0,8},{8,16},{16,24},{24,32},{32,40},{40,48},{48,56},{56,64},{64,7... | collective-permute-start | bytes 368648 | tf_op jit(solution)/shard_map/ppermute | solution.py:337
  7.0 17.3 %collective-permute-start.1 = (f32[24,384]{1,0:T(8,128)S(1)}, f32[24,384]{1,0:T(8,128)S(1)}, u32[]{:S(2)}, u32[]{:S(2)}) collective-permute-start(f32[24,384]{1,0:T(8,128)S(1)} %get-tuple-element.49.downs_ref), channel_id=1, source_target_pairs={{0,504},{8,0},{16,8},{24,16},{32,24},{40,32},{48,40},{56,48},{64,5... | collective-permute-start | bytes 110600 | tf_op jit(solution)/shard_map/ppermute | solution.py:337
  21.8 1.2 copy-start.2
  26.5 9.2 %collective-permute-start.2 = (f32[16,640]{1,0:T(8,128)S(1)}, f32[16,640]{1,0:T(8,128)S(1)}, u32[]{:S(2)}, u32[]{:S(2)}) collective-permute-start(f32[16,640]{1,0:T(8,128)S(1)} %get-tuple-element.59), channel_id=1, source_target_pairs={{0,504},{8,16},{16,8},{24,32},{32,24},{40,48},{48,40},{56,64},{64,... | collective-permute-start | bytes 122888 | tf_op jit(solution)/shard_map/ppermute | solution.py:342
  30.7 5.9 %collective-permute-start.3 = (f32[16,640]{1,0:T(8,128)S(1)}, f32[16,640]{1,0:T(8,128)S(1)}, u32[]{:S(2)}, u32[]{:S(2)}) collective-permute-start(f32[16,640]{1,0:T(8,128)S(1)} %get-tuple-element.60), channel_id=1, source_target_pairs={{0,8},{8,0},{16,24},{24,16},{32,40},{40,32},{48,56},{56,48},{64,72... | collective-permute-start | bytes 122888 | tf_op jit(solution)/shard_map/ppermute | solution.py:342
  37.6 9.2 %collective-permute-start.4 = (f32[16,640]{1,0:T(8,128)S(1)}, f32[16,640]{1,0:T(8,128)S(1)}, u32[]{:S(2)}, u32[]{:S(2)}) collective-permute-start(f32[16,640]{1,0:T(8,128)S(1)} %get-tuple-element.64), channel_id=1, source_target_pairs={{0,504},{8,16},{16,8},{24,32},{32,24},{40,48},{48,40},{56,64},{64,... | collective-permute-start | bytes 122888 | tf_op jit(solution)/shard_map/ppermute | solution.py:342
  42.6 5.9 %collective-permute-start.5 = (f32[16,640]{1,0:T(8,128)S(1)}, f32[16,640]{1,0:T(8,128)S(1)}, u32[]{:S(2)}, u32[]{:S(2)}) collective-permute-start(f32[16,640]{1,0:T(8,128)S(1)} %get-tuple-element.65), channel_id=1, source_target_pairs={{0,8},{8,0},{16,24},{24,16},{32,40},{40,32},{48,56},{56,48},{64,72... | collective-permute-start | bytes 122888 | tf_op jit(solution)/shard_map/ppermute | solution.py:342
  49.5 9.2 %collective-permute-start.6 = (f32[16,640]{1,0:T(8,128)S(1)}, f32[16,640]{1,0:T(8,128)S(1)}, u32[]{:S(2)}, u32[]{:S(2)}) collective-permute-start(f32[16,640]{1,0:T(8,128)S(1)} %get-tuple-element.69), channel_id=1, source_target_pairs={{0,504},{8,16},{16,8},{24,32},{32,24},{40,48},{48,40},{56,64},{64,... | collective-permute-start | bytes 122888 | tf_op jit(solution)/shard_map/ppermute | solution.py:342
  53.7 5.9 %collective-permute-start.7 = (f32[16,640]{1,0:T(8,128)S(1)}, f32[16,640]{1,0:T(8,128)S(1)}, u32[]{:S(2)}, u32[]{:S(2)}) collective-permute-start(f32[16,640]{1,0:T(8,128)S(1)} %get-tuple-element.70), channel_id=1, source_target_pairs={{0,8},{8,0},{16,24},{24,16},{32,40},{40,32},{48,56},{56,48},{64,72... | collective-permute-start | bytes 122888 | tf_op jit(solution)/shard_map/ppermute | solution.py:342
  60.7 9.2 %collective-permute-start.8 = (f32[16,640]{1,0:T(8,128)S(1)}, f32[16,640]{1,0:T(8,128)S(1)}, u32[]{:S(2)}, u32[]{:S(2)}) collective-permute-start(f32[16,640]{1,0:T(8,128)S(1)} %get-tuple-element.74), channel_id=1, source_target_pairs={{0,504},{8,16},{16,8},{24,32},{32,24},{40,48},{48,40},{56,64},{64,... | collective-permute-start | bytes 122888 | tf_op jit(solution)/shard_map/ppermute | solution.py:342
  65.6 5.9 %collective-permute-start.9 = (f32[16,640]{1,0:T(8,128)S(1)}, f32[16,640]{1,0:T(8,128)S(1)}, u32[]{:S(2)}, u32[]{:S(2)}) collective-permute-start(f32[16,640]{1,0:T(8,128)S(1)} %get-tuple-element.75), channel_id=1, source_target_pairs={{0,8},{8,0},{16,24},{24,16},{32,40},{40,32},{48,56},{56,48},{64,72... | collective-permute-start | bytes 122888 | tf_op jit(solution)/shard_map/ppermute | solution.py:342
  72.6 9.2 %collective-permute-start.10 = (f32[16,640]{1,0:T(8,128)S(1)}, f32[16,640]{1,0:T(8,128)S(1)}, u32[]{:S(2)}, u32[]{:S(2)}) collective-permute-start(f32[16,640]{1,0:T(8,128)S(1)} %get-tuple-element.79), channel_id=1, source_target_pairs={{0,504},{8,16},{16,8},{24,32},{32,24},{40,48},{48,40},{56,64},{64,... | collective-permute-start | bytes 122888 | tf_op jit(solution)/shard_map/ppermute | solution.py:342
  76.8 5.9 %collective-permute-start.11 = (f32[16,640]{1,0:T(8,128)S(1)}, f32[16,640]{1,0:T(8,128)S(1)}, u32[]{:S(2)}, u32[]{:S(2)}) collective-permute-start(f32[16,640]{1,0:T(8,128)S(1)} %get-tuple-element.80), channel_id=1, source_target_pairs={{0,8},{8,0},{16,24},{24,16},{32,40},{40,32},{48,56},{56,48},{64,72... | collective-permute-start | bytes 122888 | tf_op jit(solution)/shard_map/ppermute | solution.py:342
  84.4 0.8 copy-start.3
  85.1 15.7 %all-to-all-start = ((f32[8,16,1024]{2,1,0:T(8,128)}), f32[8,16,1024]{2,1,0:T(8,128)S(1)}, u32[]{:S(2)}, u32[]{:S(2)}) async-start(f32[8,16,1024]{2,1,0:T(8,128)} %copy-done.3), calls=%async_computation | async-start | bytes 1048576 | tf_op jit(solution)/shard_map/all_to_all | solution.py:388
  90.0 9.4 %collective-permute-start.12 = (f32[16,640]{1,0:T(8,128)}, f32[16,640]{1,0:T(8,128)S(1)}, u32[]{:S(2)}, u32[]{:S(2)}) collective-permute-start(f32[16,640]{1,0:T(8,128)} %get-tuple-element.86), channel_id=1, source_target_pairs={{0,504},{8,16},{16,8},{24,32},{32,24},{40,48},{48,40},{56,64},{64,... | collective-permute-start | bytes 122888 | tf_op jit(solution)/shard_map/ppermute | solution.py:342
  95.0 5.9 %collective-permute-start.13 = (f32[16,640]{1,0:T(8,128)S(1)}, f32[16,640]{1,0:T(8,128)S(1)}, u32[]{:S(2)}, u32[]{:S(2)}) collective-permute-start(f32[16,640]{1,0:T(8,128)S(1)} %get-tuple-element.87), channel_id=1, source_target_pairs={{0,8},{8,0},{16,24},{24,16},{32,40},{40,32},{48,56},{56,48},{64,72... | collective-permute-start | bytes 122888 | tf_op jit(solution)/shard_map/ppermute | solution.py:342

commit v8 on v7

--- a/solution.py
+++ b/solution.py
@@ -120,9 +120,9 @@
     down_ref[...] = jnp.zeros_like(down_ref)
     pack_message(v, partials, conn_ref, send_ref, up_ref, down_ref)
     up_ref[16 : 16 + NPROJ, 0:NPC] = proj_ref[3]
-    up_ref[40:41, 0:NPC] = edge.astype(F32)
-    up_ref[41:42, 0:GHOST] = jnp.concatenate(inverse, axis=1)
-    up_ref[42:43, 0:LANES] = atoms
+    up_ref[34:35, 0:NPC] = edge.astype(F32)
+    up_ref[35:36, 0:GHOST] = jnp.concatenate(inverse, axis=1)
+    up_ref[36:37, 0:LANES] = atoms
     down_ref[16:17, 0:LANES] = atoms
 
 
@@ -161,7 +161,7 @@
 
 
 def joined_kernel(up_ref, down_ref, maps_ref, atom_ref, proj_ref, coupling_ref, pn_ref, p_ref, pe_ref, k_ref, index_ref):
-    low_atoms, high_atoms = up_ref[42:43, 0:LANES], down_ref[16:17, 0:LANES]
+    low_atoms, high_atoms = up_ref[36:37, 0:LANES], down_ref[16:17, 0:LANES]
     which = lane_iota(1, LANES) >> 5
     own = jnp.full((1, LANES), -100.0, F32)
     for c in range(4):
@@ -171,27 +171,22 @@
     from_upper = jnp.where(which < 3, high_atoms + float(ATOM_DEV), -300.0)
     from_lower = jnp.where(which < 3, low_atoms - float(ATOM_DEV), -400.0)
     source = jnp.concatenate([jnp.where(which < 3, own, -500.0), edges, from_upper, from_lower], axis=1)
-    inside = (lane_iota(SLOT, 4 * LANES) & (SLOT - 1)) == row_iota(SLOT, 4 * LANES)
-    rows = []
-    for c in range(5):
-        if c < 4:
-            same = source == atom_ref[c].astype(F32)
-        else:
-            same = source == jnp.concatenate([edge_low] * 4, axis=1)
-        rows.append(jnp.where(inside & jnp.broadcast_to(same, inside.shape), 1.0, 0.0))
-    rows.append(jnp.zeros((3 * SLOT, 4 * LANES), F32))
-    k_ref[...] = jnp.concatenate(rows, axis=0).T.astype(BF16)
+    target = [own, jnp.where(which == 0, edge_low, -700.0)]
+    names = column(source)
+    inside = (lane_iota(4 * LANES, LANES) & (SLOT - 1)) == (row_iota(4 * LANES, LANES) & (SLOT - 1))
+    for i in range(2):
+        k_ref[:, i * LANES : (i + 1) * LANES] = jnp.where(inside & (names == target[i]), 1.0, 0.0).astype(BF16)
     low = padded_projectors(up_ref[16 : 16 + NPROJ, 0:NPC])
     stacked = jnp.concatenate([padded_projectors(proj_ref[3]), low, jnp.zeros((2 * SLOT, NPC), F32)], axis=0)
     pe_ref[0], pe_ref[1] = split2(stacked.T)
     index_ref[...] = jnp.zeros_like(index_ref)
     index_ref[0:2, :] = maps_ref[0:2, :]
     sent = maps_ref[2:3, :]
-    rows8 = [jnp.broadcast_to(b, (8, LANES)) for b in blocks_of(up_ref[41:42, 0:GHOST])]
+    rows8 = [jnp.broadcast_to(b, (8, LANES)) for b in blocks_of(up_ref[35:36, 0:GHOST])]
     third = pick_row(rows8, sent)
     third = jnp.where(jnp.broadcast_to(sent, third.shape) >= 0, third, -1.0)[0:1].astype(jnp.int32)
     index_ref[2:3, :] = third
-    index_ref[3:4, 0:NPC] = up_ref[40:41, 0:NPC].astype(jnp.int32) - NODES
+    index_ref[3:4, 0:NPC] = up_ref[34:35, 0:NPC].astype(jnp.int32) - NODES
     size = lax.axis_size("fe")
     fe = lax.axis_index("fe")
     below = lax.rem(fe + size - 1, size)
@@ -269,13 +264,22 @@
 
 
 def outer_kernel(paired, factor, base_ref, ups_ref, downs_ref, one_ref, two_ref, conn_ref, index_ref, e_ref, p_ref, pe_ref, k_ref,
-                 send_ref, pt_ref, new_ref, upo_ref, downo_ref, oneo_ref, twoo_ref, *copies_ref):
+                 *rest):
+    if len(rest) == 2:
+        new_ref, outs = rest[0], rest[1:]
+    else:
+        new_ref, outs = rest[2], rest[:2] + rest[3:]
     h = outer(paired, ups_ref, downs_ref, one_ref, two_ref, conn_ref, index_ref, e_ref, p_ref, pe_ref, k_ref)
     new = base_ref[...] + h * factor
     new_ref[...] = new
-    for ref in copies_ref:
-        for i in range(ref.shape[0]):
-            ref[i] = new
+    if len(outs) == 1:
+        for i in range(outs[0].shape[0]):
+            outs[0][i] = new
+    else:
+        pack(new, conn_ref, *outs)
+
+
+def pack(new, conn_ref, send_ref, pt_ref, upo_ref, downo_ref, oneo_ref, twoo_ref):
     v_high, v_low = split2(new)
     pack_message(new, product(v_high, v_low, pt_ref[0], pt_ref[1]), conn_ref, send_ref, upo_ref, downo_ref)
     up = upo_ref[...]
@@ -283,6 +287,10 @@
     odd = is_odd()
     oneo_ref[...] = jnp.where(odd, up, down)
     twoo_ref[...] = jnp.where(odd, down, up)
+
+
+def pack_kernel(new_ref, conn_ref, send_ref, pt_ref, *outs):
+    pack(new_ref[...], conn_ref, send_ref, pt_ref, *outs)
 
 
 def gram_kernel(base_ref, ups_ref, downs_ref, one_ref, two_ref, conn_ref, index_ref, e_ref, p_ref, pe_ref, k_ref,
@@ -348,7 +356,7 @@
     pot, couple = potential.reshape(1, NODES), coupling.T
     ups, downs = call(
         first_kernel,
-        [((48, 640), F32), ((24, 384), F32)],
+        [((40, 640), F32), ((24, 384), F32)],
         [VM, VM, VM, SM, VM, VM, VM],
         v, conn, send, atom_of_cell, projectors, pot, couple,
     )
@@ -374,18 +382,20 @@
         up, down, maps, atom_of_cell, projectors, couple, pn,
     )
     shared = (conn, index, e, p, pe, k)
+    messages = [((BANDS, 640), F32), ((BANDS, 384), F32), ((BANDS, 640), F32), ((BANDS, 640), F32)]
     for step in range(DEGREE):
         last = step == DEGREE - 1
-        copied = [((lax.axis_size("band"), BANDS, NODES), F32)] if last else []
-        new, ups, downs, one, two, *copied = call(
-            functools.partial(outer_kernel, step > 0, (1.0 if step == 0 else 2.0) / HALF_WIDTH),
-            [((BANDS, NODES), F32), ((BANDS, 640), F32), ((BANDS, 384), F32), ((BANDS, 640), F32), ((BANDS, 640), F32)] + copied,
-            [VM] * 13,
-            base, ups, downs, up, down, *shared, send, pt,
-        )
+        kernel = functools.partial(outer_kernel, step > 0, (1.0 if step == 0 else 2.0) / HALF_WIDTH)
+        vectors = ((BANDS, NODES), F32)
+        given = (base, ups, downs, up, down, *shared)
+        if last:
+            copied = ((lax.axis_size("band"), BANDS, NODES), F32)
+            new, copied = call(kernel, [vectors, copied], [VM] * 11, *given)
+            everyone = lax.all_to_all(copied, "band", 0, 0).reshape(-1, NODES)
+            ups, downs, one, two = call(pack_kernel, messages, [VM] * 4, new, conn, send, pt)
+        else:
+            new, ups, downs, one, two = call(kernel, [vectors] + messages, [VM] * 13, *given, send, pt)
         previous, current = current, new
-        if last:
-            everyone = lax.all_to_all(copied[0], "band", 0, 0).reshape(-1, NODES)
         up, down = swapped(one, 1), swapped(two, 0)
         base, *result = inner("last" if last else "middle", current, current if last else previous)
     (copies,) = call(

time: 135 us -> 136 us (level)
    pallas_call x20 -> x21, Pallas kernels: 21.4 us -> 21.8 us  [call(): pl.pallas_call(kernel, out_shape=[jax.ShapeDtypeStruct(s, t) for s, t in...]
where the time goes in v8:
time: 136 us; the launch traced here: 135 us
  starting transfers between devices  59.8 us (44%)
  blocking collectives  31.6 us (23%)
  Pallas kernels  21.8 us (16%)
  waiting for transfers between devices  17.1 us (13%)
  local copies, waits for them, and re-layouts  3.68 us (3%)
    ppermute x12, starting transfers between devices, swapped(): lax.ppermute(block, 'fe', [(i, (i + 1 if i % 2 == first else i - 1) % siz...  39.2 us
    all_to_all x1, blocking collectives, on_device(): parts = lax.all_to_all(copies, 'fe', 0, 0, axis_index_groups=far)  22.6 us
    pallas_call x21, Pallas kernels, call(): pl.pallas_call(kernel, out_shape=[jax.ShapeDtypeStruct(s, t) for s, t in...  21.8 us
    ppermute x12, waiting for transfers between devices, swapped(): lax.ppermute(block, 'fe', [(i, (i + 1 if i % 2 == first else i - 1) % siz...  17.1 us
    ppermute x2, starting transfers between devices, shifted(): lax.ppermute(block, 'fe', [(i, (i + distance) % size) for i in range(size)])  15.8 us
    all_to_all x1, blocking collectives, on_device(): parts = lax.all_to_all(copies, 'fe', 0, 0, axis_index_groups=near)  9 us
    all_to_all x1, starting transfers between devices, on_device(): everyone = lax.all_to_all(copied, 'band', 0, 0).reshape(-1, NODES)  4.83 us
    unnamed x17, local copies, waits for them, and re-layouts  3.68 us
  transfers between devices with their start and end apart: 15, of which 12 were waited for; matrix products, arithmetic and copies ran while one was open for 0% of the time, Pallas kernels for 8%

profile of v8, /device:TPU:2, one launch (start us, length us, event | category | flops | bytes accessed | tf_op | source)
XLA Modules:
  0.0 134.9 jit_solution(13463058618138691922)
XLA Ops:
  0.7 1.0 copy.11.proj_ref
  2.4 1.1 shard_map.106
  3.5 3.5 %collective-permute-start = (f32[40,640]{1,0:T(8,128)S(1)}, f32[40,640]{1,0:T(8,128)S(1)}, u32[]{:S(2)}, u32[]{:S(2)}) collective-permute-start(f32[40,640]{1,0:T(8,128)S(1)} %get-tuple-element.48.ups_ref), channel_id=1, source_target_pairs={{0,8},{8,16},{16,24},{24,32},{32,40},{40,48},{48,56},{56,64},{64,7... | collective-permute-start | bytes 307208 | tf_op jit(solution)/shard_map/ppermute | solution.py:345
  7.0 12.3 %collective-permute-start.1 = (f32[24,384]{1,0:T(8,128)S(1)}, f32[24,384]{1,0:T(8,128)S(1)}, u32[]{:S(2)}, u32[]{:S(2)}) collective-permute-start(f32[24,384]{1,0:T(8,128)S(1)} %get-tuple-element.49.downs_ref), channel_id=1, source_target_pairs={{0,504},{8,0},{16,8},{24,16},{32,24},{40,32},{48,40},{56,48},{64,5... | collective-permute-start | bytes 110600 | tf_op jit(solution)/shard_map/ppermute | solution.py:345
  19.3 2.5 %shard_map.103 = (s32[8,1024]{1,0:T(8,128)S(1)}, f32[128,1024]{1,0:T(8,128)S(1)}, bf16[2,1024,128]{2,1,0:T(8,128)(2,1)S(1)}) custom-call(s32[4,512]{1,0:T(4,128)S(1)} %copy-done, s32[1,256]{1,0:T(1,128)S(1)} %bitcast.17, f32[4,18,512]{2,1,0:T(8,128)S(1)} %copy.11.proj_ref), custom_call_target="tpu_custom_call" | custom-call | tf_op jit(solution)/shard_map/pallas_call | solution.py:334
  21.8 1.2 copy-done.2
  23.2 1.1 shard_map.105.base_ref
  24.3 1.1 shard_map.107
  25.4 1.0 shard_map.108
  26.4 4.2 %collective-permute-start.2 = (f32[16,640]{1,0:T(8,128)S(1)}, f32[16,640]{1,0:T(8,128)S(1)}, u32[]{:S(2)}, u32[]{:S(2)}) collective-permute-start(f32[16,640]{1,0:T(8,128)S(1)} %get-tuple-element.59), channel_id=1, source_target_pairs={{0,504},{8,16},{16,8},{24,32},{32,24},{40,48},{48,40},{56,64},{64,... | collective-permute-start | bytes 122888 | tf_op jit(solution)/shard_map/ppermute | solution.py:350
  30.6 1.9 %collective-permute-start.3 = (f32[16,640]{1,0:T(8,128)S(1)}, f32[16,640]{1,0:T(8,128)S(1)}, u32[]{:S(2)}, u32[]{:S(2)}) collective-permute-start(f32[16,640]{1,0:T(8,128)S(1)} %get-tuple-element.60), channel_id=1, source_target_pairs={{0,8},{8,0},{16,24},{24,16},{32,40},{40,32},{48,56},{56,48},{64,72... | collective-permute-start | bytes 122888 | tf_op jit(solution)/shard_map/ppermute | solution.py:350
  32.6 1.1 shard_map.109.base_ref
  33.6 2.0 %collective-permute-done.2.one_ref = f32[16,640]{1,0:T(8,128)S(1)} collective-permute-done((f32[16,640]{1,0:T(8,128)S(1)}, f32[16,640]{1,0:T(8,128)S(1)}, u32[]{:S(2)}, u32[]{:S(2)}) %collective-permute-start.2) | collective-permute-done | bytes 40992 | tf_op jit(solution)/shard_map/ppermute | solution.py:350
  35.6 0.9 collective-permute-done.3.two_ref
  36.5 1.0 shard_map.110
  37.6 5.0 %collective-permute-start.4 = (f32[16,640]{1,0:T(8,128)S(1)}, f32[16,640]{1,0:T(8,128)S(1)}, u32[]{:S(2)}, u32[]{:S(2)}) collective-permute-start(f32[16,640]{1,0:T(8,128)S(1)} %get-tuple-element.64), channel_id=1, source_target_pairs={{0,504},{8,16},{16,8},{24,32},{32,24},{40,48},{48,40},{56,64},{64,... | collective-permute-start | bytes 122888 | tf_op jit(solution)/shard_map/ppermute | solution.py:350
  42.5 1.9 %collective-permute-start.5 = (f32[16,640]{1,0:T(8,128)S(1)}, f32[16,640]{1,0:T(8,128)S(1)}, u32[]{:S(2)}, u32[]{:S(2)}) collective-permute-start(f32[16,640]{1,0:T(8,128)S(1)} %get-tuple-element.65), channel_id=1, source_target_pairs={{0,8},{8,0},{16,24},{24,16},{32,40},{40,32},{48,56},{56,48},{64,72... | collective-permute-start | bytes 122888 | tf_op jit(solution)/shard_map/ppermute | solution.py:350
  44.5 1.1 shard_map.111.base_ref
  45.6 1.2 collective-permute-done.4.one_ref
  46.8 1.7 %collective-permute-done.5.two_ref = f32[16,640]{1,0:T(8,128)S(1)} collective-permute-done((f32[16,640]{1,0:T(8,128)S(1)}, f32[16,640]{1,0:T(8,128)S(1)}, u32[]{:S(2)}, u32[]{:S(2)}) %collective-permute-start.5) | collective-permute-done | bytes 40992 | tf_op jit(solution)/shard_map/ppermute | solution.py:350
  48.4 1.1 shard_map.112
  49.5 4.2 %collective-permute-start.6 = (f32[16,640]{1,0:T(8,128)S(1)}, f32[16,640]{1,0:T(8,128)S(1)}, u32[]{:S(2)}, u32[]{:S(2)}) collective-permute-start(f32[16,640]{1,0:T(8,128)S(1)} %get-tuple-element.69), channel_id=1, source_target_pairs={{0,504},{8,16},{16,8},{24,32},{32,24},{40,48},{48,40},{56,64},{64,... | collective-permute-start | bytes 122888 | tf_op jit(solution)/shard_map/ppermute | solution.py:350
  53.7 1.9 %collective-permute-start.7 = (f32[16,640]{1,0:T(8,128)S(1)}, f32[16,640]{1,0:T(8,128)S(1)}, u32[]{:S(2)}, u32[]{:S(2)}) collective-permute-start(f32[16,640]{1,0:T(8,128)S(1)} %get-tuple-element.70), channel_id=1, source_target_pairs={{0,8},{8,0},{16,24},{24,16},{32,40},{40,32},{48,56},{56,48},{64,72... | collective-permute-start | bytes 122888 | tf_op jit(solution)/shard_map/ppermute | solution.py:350
  55.6 1.1 shard_map.113.base_ref
  56.7 2.0 %collective-permute-done.6.one_ref = f32[16,640]{1,0:T(8,128)S(1)} collective-permute-done((f32[16,640]{1,0:T(8,128)S(1)}, f32[16,640]{1,0:T(8,128)S(1)}, u32[]{:S(2)}, u32[]{:S(2)}) %collective-permute-start.6) | collective-permute-done | bytes 40992 | tf_op jit(solution)/shard_map/ppermute | solution.py:350
  58.7 0.9 collective-permute-done.7.two_ref
  59.6 1.0 shard_map.114
  60.6 5.0 %collective-permute-start.8 = (f32[16,640]{1,0:T(8,128)S(1)}, f32[16,640]{1,0:T(8,128)S(1)}, u32[]{:S(2)}, u32[]{:S(2)}) collective-permute-start(f32[16,640]{1,0:T(8,128)S(1)} %get-tuple-element.74), channel_id=1, source_target_pairs={{0,504},{8,16},{16,8},{24,32},{32,24},{40,48},{48,40},{56,64},{64,... | collective-permute-start | bytes 122888 | tf_op jit(solution)/shard_map/ppermute | solution.py:350
  65.6 1.9 %collective-permute-start.9 = (f32[16,640]{1,0:T(8,128)S(1)}, f32[16,640]{1,0:T(8,128)S(1)}, u32[]{:S(2)}, u32[]{:S(2)}) collective-permute-start(f32[16,640]{1,0:T(8,128)S(1)} %get-tuple-element.75), channel_id=1, source_target_pairs={{0,8},{8,0},{16,24},{24,16},{32,40},{40,32},{48,56},{56,48},{64,72... | collective-permute-start | bytes 122888 | tf_op jit(solution)/shard_map/ppermute | solution.py:350
  67.5 1.1 shard_map.115.base_ref
  68.6 1.2 collective-permute-done.8.one_ref
  69.8 1.7 %collective-permute-done.9.two_ref = f32[16,640]{1,0:T(8,128)S(1)} collective-permute-done((f32[16,640]{1,0:T(8,128)S(1)}, f32[16,640]{1,0:T(8,128)S(1)}, u32[]{:S(2)}, u32[]{:S(2)}) %collective-permute-start.9) | collective-permute-done | bytes 40992 | tf_op jit(solution)/shard_map/ppermute | solution.py:350
  71.5 1.0 shard_map.116
  72.6 4.2 %collective-permute-start.10 = (f32[16,640]{1,0:T(8,128)S(1)}, f32[16,640]{1,0:T(8,128)S(1)}, u32[]{:S(2)}, u32[]{:S(2)}) collective-permute-start(f32[16,640]{1,0:T(8,128)S(1)} %get-tuple-element.79), channel_id=1, source_target_pairs={{0,504},{8,16},{16,8},{24,32},{32,24},{40,48},{48,40},{56,64},{64,... | collective-permute-start | bytes 122888 | tf_op jit(solution)/shard_map/ppermute | solution.py:350
  76.7 2.1 %collective-permute-start.11 = (f32[16,640]{1,0:T(8,128)S(1)}, f32[16,640]{1,0:T(8,128)S(1)}, u32[]{:S(2)}, u32[]{:S(2)}) collective-permute-start(f32[16,640]{1,0:T(8,128)S(1)} %get-tuple-element.80), channel_id=1, source_target_pairs={{0,8},{8,0},{16,24},{24,16},{32,40},{40,32},{48,56},{56,48},{64,72... | collective-permute-start | bytes 122888 | tf_op jit(solution)/shard_map/ppermute | solution.py:350
  78.9 1.1 shard_map.117.base_ref
  79.9 1.8 %collective-permute-done.10.one_ref = f32[16,640]{1,0:T(8,128)S(1)} collective-permute-done((f32[16,640]{1,0:T(8,128)S(1)}, f32[16,640]{1,0:T(8,128)S(1)}, u32[]{:S(2)}, u32[]{:S(2)}) %collective-permute-start.10) | collective-permute-done | bytes 40992 | tf_op jit(solution)/shard_map/ppermute | solution.py:350
  81.8 0.9 collective-permute-done.11.two_ref
  82.6 0.9 shard_map.118
  84.4 4.8 %all-to-all-start = ((f32[8,16,1024]{2,1,0:T(8,128)}), f32[8,16,1024]{2,1,0:T(8,128)}, u32[]{:S(2)}, u32[]{:S(2)}) async-start(f32[8,16,1024]{2,1,0:T(8,128)} %copy-done.3), calls=%async_computation | async-start | bytes 1048576 | tf_op jit(solution)/shard_map/all_to_all | solution.py:394
  89.4 5.0 %collective-permute-start.12 = (f32[16,640]{1,0:T(8,128)S(1)}, f32[16,640]{1,0:T(8,128)S(1)}, u32[]{:S(2)}, u32[]{:S(2)}) collective-permute-start(f32[16,640]{1,0:T(8,128)S(1)} %get-tuple-element.86), channel_id=1, source_target_pairs={{0,504},{8,16},{16,8},{24,32},{32,24},{40,48},{48,40},{56,64},{64,... | collective-permute-start | bytes 122888 | tf_op jit(solution)/shard_map/ppermute | solution.py:350
  94.4 1.9 %collective-permute-start.13 = (f32[16,640]{1,0:T(8,128)S(1)}, f32[16,640]{1,0:T(8,128)S(1)}, u32[]{:S(2)}, u32[]{:S(2)}) collective-permute-start(f32[16,640]{1,0:T(8,128)S(1)} %get-tuple-element.87), channel_id=1, source_target_pairs={{0,8},{8,0},{16,24},{24,16},{32,40},{40,32},{48,56},{56,48},{64,72... | collective-permute-start | bytes 122888 | tf_op jit(solution)/shard_map/ppermute | solution.py:350
  96.3 1.1 shard_map.119
  97.4 1.2 collective-permute-done.12.one_ref
  98.6 1.7 %collective-permute-done.13.two_ref = f32[16,640]{1,0:T(8,128)S(1)} collective-permute-done((f32[16,640]{1,0:T(8,128)S(1)}, f32[16,640]{1,0:T(8,128)S(1)}, u32[]{:S(2)}, u32[]{:S(2)}) %collective-permute-start.13) | collective-permute-done | bytes 40992 | tf_op jit(solution)/shard_map/ppermute | solution.py:350
  100.3 2.3 %shard_map.121 = f32[8,32,128]{2,1,0:T(8,128)S(1)} custom-call(f32[16,1024]{1,0:T(8,128)S(1)} %get-tuple-element.83.base_ref, f32[16,640]{1,0:T(8,128)S(1)} %get-tuple-element.84.ups_ref, f32[16,384]{1,0:T(8,128)S(1)} %get-tuple-element.85.downs_ref, f32[16,640]{1,0:T(8,128)S(1)} %collective-permute-done.12.one_ref, ...), custom_call_target="tpu_custom_call" | custom-call | tf_op jit(solution)/shard_map/pallas_call | solution.py:334
  102.6 9.0 %all_to_all.15.parts_ref = f32[8,32,128]{2,1,0:T(8,128)S(1)} all-to-all(f32[8,32,128]{2,1,0:T(8,128)S(1)} %shard_map.121), channel_id=1, replica_groups={{0,8,16,24,32,40,48,56},{64,72,80,88,96,104,112,120},{128,136,144,152,1..., dimensions={0} | all-to-all | bytes 262144 | tf_op jit(solution)/shard_map/all_to_all | solution.py:409
  111.6 22.6 %all_to_all.16.parts_ref = f32[8,32,128]{2,1,0:T(8,128)S(1)} all-to-all(f32[8,32,128]{2,1,0:T(8,128)S(1)} %shard_map.122), channel_id=1, replica_groups={{0,64,128,192,256,320,384,448},{8,72,136,200,264,328,392,456},{16,80,14..., dimensions={0} | all-to-all | bytes 262144 | tf_op jit(solution)/shard_map/all_to_all | solution.py:411
  (22 shorter events, 2.5 us)
Async XLA Ops:
  0.6 1.1 copy-start.5
  0.6 1.1 copy-start.1
  0.7 1.1 copy-start
  1.7 0.7 copy-start.4
  1.7 0.7 copy-start.6
  1.7 0.7 copy-start.7
  3.5 20.8 %collective-permute-start = (f32[40,640]{1,0:T(8,128)S(1)}, f32[40,640]{1,0:T(8,128)S(1)}, u32[]{:S(2)}, u32[]{:S(2)}) collective-permute-start(f32[40,640]{1,0:T(8,128)S(1)} %get-tuple-element.48.ups_ref), channel_id=1, source_target_pairs={{0,8},{8,16},{16,24},{24,32},{32,40},{40,48},{48,56},{56,64},{64,7... | collective-permute-start | bytes 307208 | tf_op jit(solution)/shard_map/ppermute | solution.py:345
  7.0 17.3 %collective-permute-start.1 = (f32[24,384]{1,0:T(8,128)S(1)}, f32[24,384]{1,0:T(8,128)S(1)}, u32[]{:S(2)}, u32[]{:S(2)}) collective-permute-start(f32[24,384]{1,0:T(8,128)S(1)} %get-tuple-element.49.downs_ref), channel_id=1, source_target_pairs={{0,504},{8,0},{16,8},{24,16},{32,24},{40,32},{48,40},{56,48},{64,5... | collective-permute-start | bytes 110600 | tf_op jit(solution)/shard_map/ppermute | solution.py:345
  21.8 1.2 copy-start.2
  26.4 9.2 %collective-permute-start.2 = (f32[16,640]{1,0:T(8,128)S(1)}, f32[16,640]{1,0:T(8,128)S(1)}, u32[]{:S(2)}, u32[]{:S(2)}) collective-permute-start(f32[16,640]{1,0:T(8,128)S(1)} %get-tuple-element.59), channel_id=1, source_target_pairs={{0,504},{8,16},{16,8},{24,32},{32,24},{40,48},{48,40},{56,64},{64,... | collective-permute-start | bytes 122888 | tf_op jit(solution)/shard_map/ppermute | solution.py:350
  30.6 5.9 %collective-permute-start.3 = (f32[16,640]{1,0:T(8,128)S(1)}, f32[16,640]{1,0:T(8,128)S(1)}, u32[]{:S(2)}, u32[]{:S(2)}) collective-permute-start(f32[16,640]{1,0:T(8,128)S(1)} %get-tuple-element.60), channel_id=1, source_target_pairs={{0,8},{8,0},{16,24},{24,16},{32,40},{40,32},{48,56},{56,48},{64,72... | collective-permute-start | bytes 122888 | tf_op jit(solution)/shard_map/ppermute | solution.py:350
  37.6 9.2 %collective-permute-start.4 = (f32[16,640]{1,0:T(8,128)S(1)}, f32[16,640]{1,0:T(8,128)S(1)}, u32[]{:S(2)}, u32[]{:S(2)}) collective-permute-start(f32[16,640]{1,0:T(8,128)S(1)} %get-tuple-element.64), channel_id=1, source_target_pairs={{0,504},{8,16},{16,8},{24,32},{32,24},{40,48},{48,40},{56,64},{64,... | collective-permute-start | bytes 122888 | tf_op jit(solution)/shard_map/ppermute | solution.py:350
  42.5 5.9 %collective-permute-start.5 = (f32[16,640]{1,0:T(8,128)S(1)}, f32[16,640]{1,0:T(8,128)S(1)}, u32[]{:S(2)}, u32[]{:S(2)}) collective-permute-start(f32[16,640]{1,0:T(8,128)S(1)} %get-tuple-element.65), channel_id=1, source_target_pairs={{0,8},{8,0},{16,24},{24,16},{32,40},{40,32},{48,56},{56,48},{64,72... | collective-permute-start | bytes 122888 | tf_op jit(solution)/shard_map/ppermute | solution.py:350
  49.5 9.2 %collective-permute-start.6 = (f32[16,640]{1,0:T(8,128)S(1)}, f32[16,640]{1,0:T(8,128)S(1)}, u32[]{:S(2)}, u32[]{:S(2)}) collective-permute-start(f32[16,640]{1,0:T(8,128)S(1)} %get-tuple-element.69), channel_id=1, source_target_pairs={{0,504},{8,16},{16,8},{24,32},{32,24},{40,48},{48,40},{56,64},{64,... | collective-permute-start | bytes 122888 | tf_op jit(solution)/shard_map/ppermute | solution.py:350
  53.7 5.9 %collective-permute-start.7 = (f32[16,640]{1,0:T(8,128)S(1)}, f32[16,640]{1,0:T(8,128)S(1)}, u32[]{:S(2)}, u32[]{:S(2)}) collective-permute-start(f32[16,640]{1,0:T(8,128)S(1)} %get-tuple-element.70), channel_id=1, source_target_pairs={{0,8},{8,0},{16,24},{24,16},{32,40},{40,32},{48,56},{56,48},{64,72... | collective-permute-start | bytes 122888 | tf_op jit(solution)/shard_map/ppermute | solution.py:350
  60.6 9.2 %collective-permute-start.8 = (f32[16,640]{1,0:T(8,128)S(1)}, f32[16,640]{1,0:T(8,128)S(1)}, u32[]{:S(2)}, u32[]{:S(2)}) collective-permute-start(f32[16,640]{1,0:T(8,128)S(1)} %get-tuple-element.74), channel_id=1, source_target_pairs={{0,504},{8,16},{16,8},{24,32},{32,24},{40,48},{48,40},{56,64},{64,... | collective-permute-start | bytes 122888 | tf_op jit(solution)/shard_map/ppermute | solution.py:350
  65.6 5.9 %collective-permute-start.9 = (f32[16,640]{1,0:T(8,128)S(1)}, f32[16,640]{1,0:T(8,128)S(1)}, u32[]{:S(2)}, u32[]{:S(2)}) collective-permute-start(f32[16,640]{1,0:T(8,128)S(1)} %get-tuple-element.75), channel_id=1, source_target_pairs={{0,8},{8,0},{16,24},{24,16},{32,40},{40,32},{48,56},{56,48},{64,72... | collective-permute-start | bytes 122888 | tf_op jit(solution)/shard_map/ppermute | solution.py:350
  72.6 9.2 %collective-permute-start.10 = (f32[16,640]{1,0:T(8,128)S(1)}, f32[16,640]{1,0:T(8,128)S(1)}, u32[]{:S(2)}, u32[]{:S(2)}) collective-permute-start(f32[16,640]{1,0:T(8,128)S(1)} %get-tuple-element.79), channel_id=1, source_target_pairs={{0,504},{8,16},{16,8},{24,32},{32,24},{40,48},{48,40},{56,64},{64,... | collective-permute-start | bytes 122888 | tf_op jit(solution)/shard_map/ppermute | solution.py:350
  76.7 5.9 %collective-permute-start.11 = (f32[16,640]{1,0:T(8,128)S(1)}, f32[16,640]{1,0:T(8,128)S(1)}, u32[]{:S(2)}, u32[]{:S(2)}) collective-permute-start(f32[16,640]{1,0:T(8,128)S(1)} %get-tuple-element.80), channel_id=1, source_target_pairs={{0,8},{8,0},{16,24},{24,16},{32,40},{40,32},{48,56},{56,48},{64,72... | collective-permute-start | bytes 122888 | tf_op jit(solution)/shard_map/ppermute | solution.py:350
  83.5 0.8 copy-start.3
  84.4 15.9 %all-to-all-start = ((f32[8,16,1024]{2,1,0:T(8,128)}), f32[8,16,1024]{2,1,0:T(8,128)}, u32[]{:S(2)}, u32[]{:S(2)}) async-start(f32[8,16,1024]{2,1,0:T(8,128)} %copy-done.3), calls=%async_computation | async-start | bytes 1048576 | tf_op jit(solution)/shard_map/all_to_all | solution.py:394
  89.4 9.2 %collective-permute-start.12 = (f32[16,640]{1,0:T(8,128)S(1)}, f32[16,640]{1,0:T(8,128)S(1)}, u32[]{:S(2)}, u32[]{:S(2)}) collective-permute-start(f32[16,640]{1,0:T(8,128)S(1)} %get-tuple-element.86), channel_id=1, source_target_pairs={{0,504},{8,16},{16,8},{24,32},{32,24},{40,48},{48,40},{56,64},{64,... | collective-permute-start | bytes 122888 | tf_op jit(solution)/shard_map/ppermute | solution.py:350
  94.4 5.9 %collective-permute-start.13 = (f32[16,640]{1,0:T(8,128)S(1)}, f32[16,640]{1,0:T(8,128)S(1)}, u32[]{:S(2)}, u32[]{:S(2)}) collective-permute-start(f32[16,640]{1,0:T(8,128)S(1)} %get-tuple-element.87), channel_id=1, source_target_pairs={{0,8},{8,0},{16,24},{24,16},{32,40},{40,32},{48,56},{56,48},{64,72... | collective-permute-start | bytes 122888 | tf_op jit(solution)/shard_map/ppermute | solution.py:350

commit v9 on v8

--- a/solution.py
+++ b/solution.py
@@ -294,18 +294,16 @@
 
 
 def gram_kernel(base_ref, ups_ref, downs_ref, one_ref, two_ref, conn_ref, index_ref, e_ref, p_ref, pe_ref, k_ref,
-                v_ref, all_ref, out_ref):
+                v_ref, all_in, out_ref, all_ref, sem):
+    copy = pltpu.make_async_copy(all_in, all_ref, sem)
+    copy.start()
+    h = base_ref[...] + outer(True, ups_ref, downs_ref, one_ref, two_ref, conn_ref, index_ref, e_ref, p_ref, pe_ref, k_ref)
+    x_high, x_low = split2(jnp.concatenate([h, v_ref[...]], axis=0))
+    copy.wait()
     a_high, a_low = split2(all_ref[...])
-
-    def against_all(x):
-        x_high, x_low = split2(x)
-        less = dot_nt(x_high, a_low)
-        both = dot_nt(jnp.concatenate([x_high, x_low], axis=0), a_high)
-        return both[:BANDS] + (both[BANDS:] + less)
-
-    correlation = against_all(v_ref[...])
-    h = base_ref[...] + outer(True, ups_ref, downs_ref, one_ref, two_ref, conn_ref, index_ref, e_ref, p_ref, pe_ref, k_ref)
-    panel = jnp.concatenate([against_all(h), correlation], axis=0)
+    less = dot_nt(x_high, a_low)
+    both = dot_nt(jnp.concatenate([x_high, x_low], axis=0), a_high)
+    panel = both[: 2 * BANDS] + (both[2 * BANDS :] + less)
     for i in range(out_ref.shape[0]):
         out_ref[i] = panel
 
@@ -330,9 +328,10 @@
 SM = pl.BlockSpec(memory_space=pltpu.SMEM)
 
 
-def call(kernel, outs, ins, *args):
+def call(kernel, outs, ins, *args, scratch=()):
     return pl.pallas_call(
         kernel,
+        scratch_shapes=scratch,
         out_shape=[jax.ShapeDtypeStruct(s, t) for s, t in outs],
         in_specs=ins,
         out_specs=[VM] * len(outs),
@@ -401,8 +400,9 @@
     (copies,) = call(
         gram_kernel,
         [((8, 32, LANES), F32)],
-        [VM] * 13,
+        [VM] * 12 + [pl.BlockSpec(memory_space=pl.ANY)],
         base, ups, downs, up, down, *shared, current, everyone,
+        scratch=[pltpu.VMEM((LANES, NODES), F32), pltpu.SemaphoreType.DMA],
     )
     near = [[8 * i + j for j in range(8)] for i in range(fe_count // 8)]
     far = [[8 * i + j for i in range(fe_count // 8)] for j in range(8)]

time: 136 us -> 135 us (level)
  no operation moved by 1% of the time
where the time goes in v9:
time: 135 us; the launch traced here: 134 us
  starting transfers between devices  59.8 us (44%)
  blocking collectives  31.6 us (23%)
  Pallas kernels  20.9 us (15%)
  waiting for transfers between devices  17.1 us (13%)
  local copies, waits for them, and re-layouts  3.68 us (3%)
    ppermute x12, starting transfers between devices, swapped(): lax.ppermute(block, 'fe', [(i, (i + 1 if i % 2 == first else i - 1) % siz...  39.2 us
    all_to_all x1, blocking collectives, on_device(): parts = lax.all_to_all(copies, 'fe', 0, 0, axis_index_groups=far)  22.6 us
    pallas_call x21, Pallas kernels, call(): pl.pallas_call(kernel, scratch_shapes=scratch, out_shape=[jax.ShapeDtypeS...  20.9 us
    ppermute x12, waiting for transfers between devices, swapped(): lax.ppermute(block, 'fe', [(i, (i + 1 if i % 2 == first else i - 1) % siz...  17.1 us
    ppermute x2, starting transfers between devices, shifted(): lax.ppermute(block, 'fe', [(i, (i + distance) % size) for i in range(size)])  15.8 us
    all_to_all x1, blocking collectives, on_device(): parts = lax.all_to_all(copies, 'fe', 0, 0, axis_index_groups=near)  8.97 us
    all_to_all x1, starting transfers between devices, on_device(): everyone = lax.all_to_all(copied, 'band', 0, 0).reshape(-1, NODES)  4.83 us
    unnamed x17, local copies, waits for them, and re-layouts  3.68 us
  transfers between devices with their start and end apart: 15, of which 12 were waited for; matrix products, arithmetic and copies ran while one was open for 0% of the time, Pallas kernels for 8%

profile of v9, /device:TPU:2, one launch (start us, length us, event | category | flops | bytes accessed | tf_op | source)
XLA Modules:
  0.0 134.0 jit_solution(10231098309820448253)
XLA Ops:
  0.7 1.0 copy.11.proj_ref
  2.4 1.1 shard_map.106
  3.5 3.5 %collective-permute-start = (f32[40,640]{1,0:T(8,128)S(1)}, f32[40,640]{1,0:T(8,128)S(1)}, u32[]{:S(2)}, u32[]{:S(2)}) collective-permute-start(f32[40,640]{1,0:T(8,128)S(1)} %get-tuple-element.48.ups_ref), channel_id=1, source_target_pairs={{0,8},{8,16},{16,24},{24,32},{32,40},{40,48},{48,56},{56,64},{64,7... | collective-permute-start | bytes 307208 | tf_op jit(solution)/shard_map/ppermute | solution.py:344
  7.0 12.3 %collective-permute-start.1 = (f32[24,384]{1,0:T(8,128)S(1)}, f32[24,384]{1,0:T(8,128)S(1)}, u32[]{:S(2)}, u32[]{:S(2)}) collective-permute-start(f32[24,384]{1,0:T(8,128)S(1)} %get-tuple-element.49.downs_ref), channel_id=1, source_target_pairs={{0,504},{8,0},{16,8},{24,16},{32,24},{40,32},{48,40},{56,48},{64,5... | collective-permute-start | bytes 110600 | tf_op jit(solution)/shard_map/ppermute | solution.py:344
  19.3 2.5 %shard_map.103 = (s32[8,1024]{1,0:T(8,128)S(1)}, f32[128,1024]{1,0:T(8,128)S(1)}, bf16[2,1024,128]{2,1,0:T(8,128)(2,1)S(1)}) custom-call(s32[4,512]{1,0:T(4,128)S(1)} %copy-done, s32[1,256]{1,0:T(1,128)S(1)} %bitcast.17, f32[4,18,512]{2,1,0:T(8,128)S(1)} %copy.11.proj_ref), custom_call_target="tpu_custom_call" | custom-call | tf_op jit(solution)/shard_map/pallas_call | solution.py:332
  21.8 1.2 copy-done.2
  23.2 1.1 shard_map.105.base_ref
  24.3 1.1 shard_map.107
  25.4 1.0 shard_map.108
  26.4 4.2 %collective-permute-start.2 = (f32[16,640]{1,0:T(8,128)S(1)}, f32[16,640]{1,0:T(8,128)S(1)}, u32[]{:S(2)}, u32[]{:S(2)}) collective-permute-start(f32[16,640]{1,0:T(8,128)S(1)} %get-tuple-element.59), channel_id=1, source_target_pairs={{0,504},{8,16},{16,8},{24,32},{32,24},{40,48},{48,40},{56,64},{64,... | collective-permute-start | bytes 122888 | tf_op jit(solution)/shard_map/ppermute | solution.py:349
  30.6 1.9 %collective-permute-start.3 = (f32[16,640]{1,0:T(8,128)S(1)}, f32[16,640]{1,0:T(8,128)S(1)}, u32[]{:S(2)}, u32[]{:S(2)}) collective-permute-start(f32[16,640]{1,0:T(8,128)S(1)} %get-tuple-element.60), channel_id=1, source_target_pairs={{0,8},{8,0},{16,24},{24,16},{32,40},{40,32},{48,56},{56,48},{64,72... | collective-permute-start | bytes 122888 | tf_op jit(solution)/shard_map/ppermute | solution.py:349
  32.6 1.1 shard_map.109.base_ref
  33.6 2.0 %collective-permute-done.2.one_ref = f32[16,640]{1,0:T(8,128)S(1)} collective-permute-done((f32[16,640]{1,0:T(8,128)S(1)}, f32[16,640]{1,0:T(8,128)S(1)}, u32[]{:S(2)}, u32[]{:S(2)}) %collective-permute-start.2) | collective-permute-done | bytes 40992 | tf_op jit(solution)/shard_map/ppermute | solution.py:349
  35.6 0.9 collective-permute-done.3.two_ref
  36.5 1.0 shard_map.110
  37.6 5.0 %collective-permute-start.4 = (f32[16,640]{1,0:T(8,128)S(1)}, f32[16,640]{1,0:T(8,128)S(1)}, u32[]{:S(2)}, u32[]{:S(2)}) collective-permute-start(f32[16,640]{1,0:T(8,128)S(1)} %get-tuple-element.64), channel_id=1, source_target_pairs={{0,504},{8,16},{16,8},{24,32},{32,24},{40,48},{48,40},{56,64},{64,... | collective-permute-start | bytes 122888 | tf_op jit(solution)/shard_map/ppermute | solution.py:349
  42.5 1.9 %collective-permute-start.5 = (f32[16,640]{1,0:T(8,128)S(1)}, f32[16,640]{1,0:T(8,128)S(1)}, u32[]{:S(2)}, u32[]{:S(2)}) collective-permute-start(f32[16,640]{1,0:T(8,128)S(1)} %get-tuple-element.65), channel_id=1, source_target_pairs={{0,8},{8,0},{16,24},{24,16},{32,40},{40,32},{48,56},{56,48},{64,72... | collective-permute-start | bytes 122888 | tf_op jit(solution)/shard_map/ppermute | solution.py:349
  44.5 1.1 shard_map.111.base_ref
  45.6 1.2 collective-permute-done.4.one_ref
  46.8 1.7 %collective-permute-done.5.two_ref = f32[16,640]{1,0:T(8,128)S(1)} collective-permute-done((f32[16,640]{1,0:T(8,128)S(1)}, f32[16,640]{1,0:T(8,128)S(1)}, u32[]{:S(2)}, u32[]{:S(2)}) %collective-permute-start.5) | collective-permute-done | bytes 40992 | tf_op jit(solution)/shard_map/ppermute | solution.py:349
  48.4 1.1 shard_map.112
  49.5 4.2 %collective-permute-start.6 = (f32[16,640]{1,0:T(8,128)S(1)}, f32[16,640]{1,0:T(8,128)S(1)}, u32[]{:S(2)}, u32[]{:S(2)}) collective-permute-start(f32[16,640]{1,0:T(8,128)S(1)} %get-tuple-element.69), channel_id=1, source_target_pairs={{0,504},{8,16},{16,8},{24,32},{32,24},{40,48},{48,40},{56,64},{64,... | collective-permute-start | bytes 122888 | tf_op jit(solution)/shard_map/ppermute | solution.py:349
  53.7 1.9 %collective-permute-start.7 = (f32[16,640]{1,0:T(8,128)S(1)}, f32[16,640]{1,0:T(8,128)S(1)}, u32[]{:S(2)}, u32[]{:S(2)}) collective-permute-start(f32[16,640]{1,0:T(8,128)S(1)} %get-tuple-element.70), channel_id=1, source_target_pairs={{0,8},{8,0},{16,24},{24,16},{32,40},{40,32},{48,56},{56,48},{64,72... | collective-permute-start | bytes 122888 | tf_op jit(solution)/shard_map/ppermute | solution.py:349
  55.6 1.1 shard_map.113.base_ref
  56.7 2.0 %collective-permute-done.6.one_ref = f32[16,640]{1,0:T(8,128)S(1)} collective-permute-done((f32[16,640]{1,0:T(8,128)S(1)}, f32[16,640]{1,0:T(8,128)S(1)}, u32[]{:S(2)}, u32[]{:S(2)}) %collective-permute-start.6) | collective-permute-done | bytes 40992 | tf_op jit(solution)/shard_map/ppermute | solution.py:349
  58.7 0.9 collective-permute-done.7.two_ref
  59.6 1.0 shard_map.114
  60.6 5.0 %collective-permute-start.8 = (f32[16,640]{1,0:T(8,128)S(1)}, f32[16,640]{1,0:T(8,128)S(1)}, u32[]{:S(2)}, u32[]{:S(2)}) collective-permute-start(f32[16,640]{1,0:T(8,128)S(1)} %get-tuple-element.74), channel_id=1, source_target_pairs={{0,504},{8,16},{16,8},{24,32},{32,24},{40,48},{48,40},{56,64},{64,... | collective-permute-start | bytes 122888 | tf_op jit(solution)/shard_map/ppermute | solution.py:349
  65.6 1.9 %collective-permute-start.9 = (f32[16,640]{1,0:T(8,128)S(1)}, f32[16,640]{1,0:T(8,128)S(1)}, u32[]{:S(2)}, u32[]{:S(2)}) collective-permute-start(f32[16,640]{1,0:T(8,128)S(1)} %get-tuple-element.75), channel_id=1, source_target_pairs={{0,8},{8,0},{16,24},{24,16},{32,40},{40,32},{48,56},{56,48},{64,72... | collective-permute-start | bytes 122888 | tf_op jit(solution)/shard_map/ppermute | solution.py:349
  67.5 1.1 shard_map.115.base_ref
  68.6 1.2 collective-permute-done.8.one_ref
  69.8 1.7 %collective-permute-done.9.two_ref = f32[16,640]{1,0:T(8,128)S(1)} collective-permute-done((f32[16,640]{1,0:T(8,128)S(1)}, f32[16,640]{1,0:T(8,128)S(1)}, u32[]{:S(2)}, u32[]{:S(2)}) %collective-permute-start.9) | collective-permute-done | bytes 40992 | tf_op jit(solution)/shard_map/ppermute | solution.py:349
  71.5 1.0 shard_map.116
  72.6 4.2 %collective-permute-start.10 = (f32[16,640]{1,0:T(8,128)S(1)}, f32[16,640]{1,0:T(8,128)S(1)}, u32[]{:S(2)}, u32[]{:S(2)}) collective-permute-start(f32[16,640]{1,0:T(8,128)S(1)} %get-tuple-element.79), channel_id=1, source_target_pairs={{0,504},{8,16},{16,8},{24,32},{32,24},{40,48},{48,40},{56,64},{64,... | collective-permute-start | bytes 122888 | tf_op jit(solution)/shard_map/ppermute | solution.py:349
  76.7 2.1 %collective-permute-start.11 = (f32[16,640]{1,0:T(8,128)S(1)}, f32[16,640]{1,0:T(8,128)S(1)}, u32[]{:S(2)}, u32[]{:S(2)}) collective-permute-start(f32[16,640]{1,0:T(8,128)S(1)} %get-tuple-element.80), channel_id=1, source_target_pairs={{0,8},{8,0},{16,24},{24,16},{32,40},{40,32},{48,56},{56,48},{64,72... | collective-permute-start | bytes 122888 | tf_op jit(solution)/shard_map/ppermute | solution.py:349
  78.9 1.1 shard_map.117.base_ref
  79.9 1.8 %collective-permute-done.10.one_ref = f32[16,640]{1,0:T(8,128)S(1)} collective-permute-done((f32[16,640]{1,0:T(8,128)S(1)}, f32[16,640]{1,0:T(8,128)S(1)}, u32[]{:S(2)}, u32[]{:S(2)}) %collective-permute-start.10) | collective-permute-done | bytes 40992 | tf_op jit(solution)/shard_map/ppermute | solution.py:349
  81.8 0.9 collective-permute-done.11.two_ref
  82.6 0.9 shard_map.118
  84.4 4.8 %all-to-all-start = ((f32[8,16,1024]{2,1,0:T(8,128)}), f32[8,16,1024]{2,1,0:T(8,128)}, u32[]{:S(2)}, u32[]{:S(2)}) async-start(f32[8,16,1024]{2,1,0:T(8,128)} %copy-done.3), calls=%async_computation | async-start | bytes 1048576 | tf_op jit(solution)/shard_map/all_to_all | solution.py:393
  89.4 5.0 %collective-permute-start.12 = (f32[16,640]{1,0:T(8,128)S(1)}, f32[16,640]{1,0:T(8,128)S(1)}, u32[]{:S(2)}, u32[]{:S(2)}) collective-permute-start(f32[16,640]{1,0:T(8,128)S(1)} %get-tuple-element.86), channel_id=1, source_target_pairs={{0,504},{8,16},{16,8},{24,32},{32,24},{40,48},{48,40},{56,64},{64,... | collective-permute-start | bytes 122888 | tf_op jit(solution)/shard_map/ppermute | solution.py:349
  94.4 1.9 %collective-permute-start.13 = (f32[16,640]{1,0:T(8,128)S(1)}, f32[16,640]{1,0:T(8,128)S(1)}, u32[]{:S(2)}, u32[]{:S(2)}) collective-permute-start(f32[16,640]{1,0:T(8,128)S(1)} %get-tuple-element.87), channel_id=1, source_target_pairs={{0,8},{8,0},{16,24},{24,16},{32,40},{40,32},{48,56},{56,48},{64,72... | collective-permute-start | bytes 122888 | tf_op jit(solution)/shard_map/ppermute | solution.py:349
  96.3 1.1 shard_map.119
  97.4 1.2 collective-permute-done.12.one_ref
  98.6 1.7 %collective-permute-done.13.two_ref = f32[16,640]{1,0:T(8,128)S(1)} collective-permute-done((f32[16,640]{1,0:T(8,128)S(1)}, f32[16,640]{1,0:T(8,128)S(1)}, u32[]{:S(2)}, u32[]{:S(2)}) %collective-permute-start.13) | collective-permute-done | bytes 40992 | tf_op jit(solution)/shard_map/ppermute | solution.py:349
  100.3 1.5 %shard_map.121 = f32[8,32,128]{2,1,0:T(8,128)S(1)} custom-call(f32[16,1024]{1,0:T(8,128)S(1)} %get-tuple-element.83.base_ref, f32[16,640]{1,0:T(8,128)S(1)} %get-tuple-element.84.ups_ref, f32[16,384]{1,0:T(8,128)S(1)} %get-tuple-element.85.downs_ref, f32[16,640]{1,0:T(8,128)S(1)} %collective-permute-done.12.one_ref, ...), custom_call_target="tpu_custom_call" | custom-call | tf_op jit(solution)/shard_map/pallas_call | solution.py:332
  101.8 9.0 %all_to_all.15.parts_ref = f32[8,32,128]{2,1,0:T(8,128)S(1)} all-to-all(f32[8,32,128]{2,1,0:T(8,128)S(1)} %shard_map.121), channel_id=1, replica_groups={{0,8,16,24,32,40,48,56},{64,72,80,88,96,104,112,120},{128,136,144,152,1..., dimensions={0} | all-to-all | bytes 262144 | tf_op jit(solution)/shard_map/all_to_all | solution.py:409
  110.8 22.6 %all_to_all.16.parts_ref = f32[8,32,128]{2,1,0:T(8,128)S(1)} all-to-all(f32[8,32,128]{2,1,0:T(8,128)S(1)} %shard_map.122), channel_id=1, replica_groups={{0,64,128,192,256,320,384,448},{8,72,136,200,264,328,392,456},{16,80,14..., dimensions={0} | all-to-all | bytes 262144 | tf_op jit(solution)/shard_map/all_to_all | solution.py:411
  (22 shorter events, 2.5 us)
Async XLA Ops:
  0.6 1.1 copy-start.5
  0.6 1.1 copy-start.1
  0.7 1.1 copy-start
  1.7 0.7 copy-start.4
  1.7 0.7 copy-start.6
  1.7 0.7 copy-start.7
  3.5 20.8 %collective-permute-start = (f32[40,640]{1,0:T(8,128)S(1)}, f32[40,640]{1,0:T(8,128)S(1)}, u32[]{:S(2)}, u32[]{:S(2)}) collective-permute-start(f32[40,640]{1,0:T(8,128)S(1)} %get-tuple-element.48.ups_ref), channel_id=1, source_target_pairs={{0,8},{8,16},{16,24},{24,32},{32,40},{40,48},{48,56},{56,64},{64,7... | collective-permute-start | bytes 307208 | tf_op jit(solution)/shard_map/ppermute | solution.py:344
  7.0 17.3 %collective-permute-start.1 = (f32[24,384]{1,0:T(8,128)S(1)}, f32[24,384]{1,0:T(8,128)S(1)}, u32[]{:S(2)}, u32[]{:S(2)}) collective-permute-start(f32[24,384]{1,0:T(8,128)S(1)} %get-tuple-element.49.downs_ref), channel_id=1, source_target_pairs={{0,504},{8,0},{16,8},{24,16},{32,24},{40,32},{48,40},{56,48},{64,5... | collective-permute-start | bytes 110600 | tf_op jit(solution)/shard_map/ppermute | solution.py:344
  21.8 1.2 copy-start.2
  26.4 9.2 %collective-permute-start.2 = (f32[16,640]{1,0:T(8,128)S(1)}, f32[16,640]{1,0:T(8,128)S(1)}, u32[]{:S(2)}, u32[]{:S(2)}) collective-permute-start(f32[16,640]{1,0:T(8,128)S(1)} %get-tuple-element.59), channel_id=1, source_target_pairs={{0,504},{8,16},{16,8},{24,32},{32,24},{40,48},{48,40},{56,64},{64,... | collective-permute-start | bytes 122888 | tf_op jit(solution)/shard_map/ppermute | solution.py:349
  30.6 5.9 %collective-permute-start.3 = (f32[16,640]{1,0:T(8,128)S(1)}, f32[16,640]{1,0:T(8,128)S(1)}, u32[]{:S(2)}, u32[]{:S(2)}) collective-permute-start(f32[16,640]{1,0:T(8,128)S(1)} %get-tuple-element.60), channel_id=1, source_target_pairs={{0,8},{8,0},{16,24},{24,16},{32,40},{40,32},{48,56},{56,48},{64,72... | collective-permute-start | bytes 122888 | tf_op jit(solution)/shard_map/ppermute | solution.py:349
  37.6 9.2 %collective-permute-start.4 = (f32[16,640]{1,0:T(8,128)S(1)}, f32[16,640]{1,0:T(8,128)S(1)}, u32[]{:S(2)}, u32[]{:S(2)}) collective-permute-start(f32[16,640]{1,0:T(8,128)S(1)} %get-tuple-element.64), channel_id=1, source_target_pairs={{0,504},{8,16},{16,8},{24,32},{32,24},{40,48},{48,40},{56,64},{64,... | collective-permute-start | bytes 122888 | tf_op jit(solution)/shard_map/ppermute | solution.py:349
  42.5 5.9 %collective-permute-start.5 = (f32[16,640]{1,0:T(8,128)S(1)}, f32[16,640]{1,0:T(8,128)S(1)}, u32[]{:S(2)}, u32[]{:S(2)}) collective-permute-start(f32[16,640]{1,0:T(8,128)S(1)} %get-tuple-element.65), channel_id=1, source_target_pairs={{0,8},{8,0},{16,24},{24,16},{32,40},{40,32},{48,56},{56,48},{64,72... | collective-permute-start | bytes 122888 | tf_op jit(solution)/shard_map/ppermute | solution.py:349
  49.5 9.2 %collective-permute-start.6 = (f32[16,640]{1,0:T(8,128)S(1)}, f32[16,640]{1,0:T(8,128)S(1)}, u32[]{:S(2)}, u32[]{:S(2)}) collective-permute-start(f32[16,640]{1,0:T(8,128)S(1)} %get-tuple-element.69), channel_id=1, source_target_pairs={{0,504},{8,16},{16,8},{24,32},{32,24},{40,48},{48,40},{56,64},{64,... | collective-permute-start | bytes 122888 | tf_op jit(solution)/shard_map/ppermute | solution.py:349
  53.7 5.9 %collective-permute-start.7 = (f32[16,640]{1,0:T(8,128)S(1)}, f32[16,640]{1,0:T(8,128)S(1)}, u32[]{:S(2)}, u32[]{:S(2)}) collective-permute-start(f32[16,640]{1,0:T(8,128)S(1)} %get-tuple-element.70), channel_id=1, source_target_pairs={{0,8},{8,0},{16,24},{24,16},{32,40},{40,32},{48,56},{56,48},{64,72... | collective-permute-start | bytes 122888 | tf_op jit(solution)/shard_map/ppermute | solution.py:349
  60.6 9.2 %collective-permute-start.8 = (f32[16,640]{1,0:T(8,128)S(1)}, f32[16,640]{1,0:T(8,128)S(1)}, u32[]{:S(2)}, u32[]{:S(2)}) collective-permute-start(f32[16,640]{1,0:T(8,128)S(1)} %get-tuple-element.74), channel_id=1, source_target_pairs={{0,504},{8,16},{16,8},{24,32},{32,24},{40,48},{48,40},{56,64},{64,... | collective-permute-start | bytes 122888 | tf_op jit(solution)/shard_map/ppermute | solution.py:349
  65.6 5.9 %collective-permute-start.9 = (f32[16,640]{1,0:T(8,128)S(1)}, f32[16,640]{1,0:T(8,128)S(1)}, u32[]{:S(2)}, u32[]{:S(2)}) collective-permute-start(f32[16,640]{1,0:T(8,128)S(1)} %get-tuple-element.75), channel_id=1, source_target_pairs={{0,8},{8,0},{16,24},{24,16},{32,40},{40,32},{48,56},{56,48},{64,72... | collective-permute-start | bytes 122888 | tf_op jit(solution)/shard_map/ppermute | solution.py:349
  72.6 9.2 %collective-permute-start.10 = (f32[16,640]{1,0:T(8,128)S(1)}, f32[16,640]{1,0:T(8,128)S(1)}, u32[]{:S(2)}, u32[]{:S(2)}) collective-permute-start(f32[16,640]{1,0:T(8,128)S(1)} %get-tuple-element.79), channel_id=1, source_target_pairs={{0,504},{8,16},{16,8},{24,32},{32,24},{40,48},{48,40},{56,64},{64,... | collective-permute-start | bytes 122888 | tf_op jit(solution)/shard_map/ppermute | solution.py:349
  76.7 5.9 %collective-permute-start.11 = (f32[16,640]{1,0:T(8,128)S(1)}, f32[16,640]{1,0:T(8,128)S(1)}, u32[]{:S(2)}, u32[]{:S(2)}) collective-permute-start(f32[16,640]{1,0:T(8,128)S(1)} %get-tuple-element.80), channel_id=1, source_target_pairs={{0,8},{8,0},{16,24},{24,16},{32,40},{40,32},{48,56},{56,48},{64,72... | collective-permute-start | bytes 122888 | tf_op jit(solution)/shard_map/ppermute | solution.py:349
  83.5 0.8 copy-start.3
  84.4 15.9 %all-to-all-start = ((f32[8,16,1024]{2,1,0:T(8,128)}), f32[8,16,1024]{2,1,0:T(8,128)}, u32[]{:S(2)}, u32[]{:S(2)}) async-start(f32[8,16,1024]{2,1,0:T(8,128)} %copy-done.3), calls=%async_computation | async-start | bytes 1048576 | tf_op jit(solution)/shard_map/all_to_all | solution.py:393
  89.4 9.2 %collective-permute-start.12 = (f32[16,640]{1,0:T(8,128)S(1)}, f32[16,640]{1,0:T(8,128)S(1)}, u32[]{:S(2)}, u32[]{:S(2)}) collective-permute-start(f32[16,640]{1,0:T(8,128)S(1)} %get-tuple-element.86), channel_id=1, source_target_pairs={{0,504},{8,16},{16,8},{24,32},{32,24},{40,48},{48,40},{56,64},{64,... | collective-permute-start | bytes 122888 | tf_op jit(solution)/shard_map/ppermute | solution.py:349
  94.4 5.9 %collective-permute-start.13 = (f32[16,640]{1,0:T(8,128)S(1)}, f32[16,640]{1,0:T(8,128)S(1)}, u32[]{:S(2)}, u32[]{:S(2)}) collective-permute-start(f32[16,640]{1,0:T(8,128)S(1)} %get-tuple-element.87), channel_id=1, source_target_pairs={{0,8},{8,0},{16,24},{24,16},{32,40},{40,32},{48,56},{56,48},{64,72... | collective-permute-start | bytes 122888 | tf_op jit(solution)/shard_map/ppermute | solution.py:349
